TPU v7x, 256 devices: a whole 4x4x8 slice. The times are simulated.
256 devices in a mesh: tm: 16 (over y, z_lo, core), row: 4 (over x), coil: 4 (over z_hi).
Axes of the slice: x: 4, y: 4, z: 8 (z_hi: 4, z_lo: 2; z = z_hi * 2 + z_lo), core: 2. Of those that a mesh axis runs over, the one named last changes fastest.
Arguments:
- image_now: float32 [2, 16, 256, 256], P(None, 'tm', 'row'), may hold values from -6 to 6
- split_now: float32 [2, 16, 256, 256], P(None, 'tm', 'row'), may hold values from -6 to 6
- vector_one: float32 [3, 2, 16, 256, 256], P(None, None, 'tm', 'row'), may hold values from -4 to 4
- vector_two: float32 [3, 2, 16, 256, 256], P(None, None, 'tm', 'row'), may hold values from -4 to 4
- kspace_dual: float32 [2, 16, 12, 256, 256], P(None, 'tm', 'coil', 'row'), may hold values from -6 to 6
- grad_one: float32 [3, 2, 16, 256, 256], P(None, None, 'tm', 'row'), may hold values from -6 to 6
- grad_two: float32 [3, 2, 16, 256, 256], P(None, None, 'tm', 'row'), may hold values from -6 to 6
- sym_one: float32 [6, 2, 16, 256, 256], P(None, None, 'tm', 'row'), may hold values from -4 to 4
- sym_two: float32 [6, 2, 16, 256, 256], P(None, None, 'tm', 'row'), may hold values from -4 to 4
- measured: float32 [2, 16, 12, 256, 256], P(None, 'tm', 'coil', 'row'), may hold values from -6 to 6
- sensitivity: float32 [2, 12, 256, 256], P(None, 'coil', 'row'), may hold values from -4 to 4
- sampled: int32 [16, 256], P('tm'), may hold values 0 or 1
Outputs:
- image_new: float32 [2, 16, 256, 256], P(None, 'tm', 'row')
- split_new: float32 [2, 16, 256, 256], P(None, 'tm', 'row')
- vector_one_new: float32 [3, 2, 16, 256, 256], P(None, None, 'tm', 'row')
- vector_two_new: float32 [3, 2, 16, 256, 256], P(None, None, 'tm', 'row')
- kspace_new: float32 [2, 16, 12, 256, 256], P(None, 'tm', 'coil', 'row')
- grad_one_new: float32 [3, 2, 16, 256, 256], P(None, None, 'tm', 'row')
- grad_two_new: float32 [3, 2, 16, 256, 256], P(None, None, 'tm', 'row')
- sym_one_new: float32 [6, 2, 16, 256, 256], P(None, None, 'tm', 'row')
- sym_two_new: float32 [6, 2, 16, 256, 256], P(None, None, 'tm', 'row')
All inputs are finite; a program needn't handle non-finite values. No bound on the sum of `sampled` on one device may be relied on, other than what follows from the above.
Results may differ from a plain program's by a relative error of at most 0.00005.
Values sent between devices are 32-bit elements; how exact they have to be, the bound alone decides.
No kernel may reach another device: no remote copies, remote signals or barrier semaphores. Data moves between devices by JAX's collectives and lax.ppermute only.
A program may use at most 64 MiB of HBM per device.

v0:
```python
import math

import jax
import jax.numpy as jnp
from jax import lax
from jax.sharding import PartitionSpec as P

TAU = 0.25
SIGMA = 0.25
LAMBDA_DATA = 2.0
ALPHA_ONE = 2.0
ALPHA_ZERO = 1.2
BETA_ONE = 2.0
BETA_TWO = 0.5
HIGHEST = lax.Precision.HIGHEST


def shifted_2(block, axis, distance):
    devices = range(lax.axis_size(axis))
    route = [(i - distance, i) for i in devices if i - distance in devices]
    return lax.ppermute(block, axis, route)


def dft_table(length, direction_sign):
    positions = jnp.arange(length, dtype=jnp.int32)
    product = positions[:, None] * positions[None, :] % length
    angles = product.astype(jnp.float32) * (2.0 * math.pi / length)
    factor = 1.0 / math.sqrt(length)
    return (jnp.cos(angles) * factor, direction_sign * jnp.sin(angles) * factor)


def complex_contract(pattern, values, tables):
    real_part = jnp.einsum(pattern, values[0], tables[0], precision=HIGHEST) - jnp.einsum(
        pattern, values[1], tables[1], precision=HIGHEST
    )
    imag_part = jnp.einsum(pattern, values[0], tables[1], precision=HIGHEST) + jnp.einsum(
        pattern, values[1], tables[0], precision=HIGHEST
    )
    return jnp.stack([real_part, imag_part])


def forward_diff(values, dimension):
    length = values.shape[dimension]
    shifted = jnp.concatenate(
        [
            lax.slice_in_dim(values, 1, length, axis=dimension),
            lax.slice_in_dim(values, length - 1, length, axis=dimension),
        ],
        axis=dimension,
    )
    return shifted - values


def adjoint_diff(values, dimension):
    length = values.shape[dimension]
    zero_slab = jnp.zeros_like(lax.slice_in_dim(values, 0, 1, axis=dimension))
    trimmed = jnp.concatenate(
        [lax.slice_in_dim(values, 0, length - 1, axis=dimension), zero_slab], axis=dimension
    )
    behind = jnp.concatenate(
        [zero_slab, lax.slice_in_dim(trimmed, 0, length - 1, axis=dimension)], axis=dimension
    )
    return behind - trimmed


def project(duals, radius):
    magnitude = jnp.sqrt(jnp.sum(duals * duals, axis=(0, 1)))
    return duals / jnp.maximum(1.0, magnitude / radius)[None, None]


def coil_images(image_values, sensitivity):
    sens_real = sensitivity[0][None]
    sens_imag = sensitivity[1][None]
    image_real = image_values[0][:, None]
    image_imag = image_values[1][:, None]
    return jnp.stack(
        [
            sens_real * image_real - sens_imag * image_imag,
            sens_real * image_imag + sens_imag * image_real,
        ]
    )


def coil_combine(coil_values, sensitivity):
    sens_real = sensitivity[0][None]
    sens_imag = sensitivity[1][None]
    real_part = jnp.sum(sens_real * coil_values[0] + sens_imag * coil_values[1], axis=1)
    imag_part = jnp.sum(sens_real * coil_values[1] - sens_imag * coil_values[0], axis=1)
    return jnp.stack([real_part, imag_part])


def frame_last(stack):
    frames = stack.shape[2]
    global_frame = lax.axis_index("tm") * frames + jnp.arange(frames, dtype=jnp.int32)
    return (global_frame == lax.axis_size("tm") * frames - 1)[None, None, :, None, None]


def row_last(stack):
    rows_local = stack.shape[3]
    global_row = lax.axis_index("row") * rows_local + jnp.arange(rows_local, dtype=jnp.int32)
    return (global_row == lax.axis_size("row") * rows_local - 1)[None, None, None, :, None]


def ahead_time(stack):
    incoming = shifted_2(stack, "tm", -1)
    shifted = jnp.concatenate([stack[:, :, 1:], incoming], axis=2)
    return jnp.where(frame_last(stack), 0.0, shifted - stack)


def ahead_rows(stack):
    incoming = shifted_2(stack[:, :, :, :1], "row", -1)
    shifted = jnp.concatenate([stack[:, :, :, 1:], incoming], axis=3)
    return jnp.where(row_last(stack), 0.0, shifted - stack)


def behind_time(stack):
    frames = stack.shape[2]
    trimmed = jnp.where(frame_last(stack), 0.0, stack)
    incoming = shifted_2(stack, "tm", 1)
    behind = jnp.concatenate([incoming, trimmed[:, :, : frames - 1]], axis=2)
    return behind - trimmed


def behind_rows(stack):
    rows_local = stack.shape[3]
    trimmed = jnp.where(row_last(stack), 0.0, stack)
    incoming = shifted_2(stack[:, :, :, rows_local - 1 :], "row", 1)
    behind = jnp.concatenate([incoming, trimmed[:, :, :, : rows_local - 1]], axis=3)
    return behind - trimmed


def body(
    image_now,
    split_now,
    vector_one,
    vector_two,
    kspace_dual,
    grad_one,
    grad_two,
    sym_one,
    sym_two,
    measured,
    sensitivity,
    sampled,
):
    columns = image_now.shape[3]
    height = kspace_dual.shape[4]
    mask_lines = sampled.astype(jnp.float32)[None, :, None, None, :]
    forward_cols = dft_table(columns, -1.0)
    forward_rows = dft_table(height, -1.0)
    inverse_cols = dft_table(columns, 1.0)
    inverse_rows = dft_table(height, 1.0)
    spectrum = complex_contract("fckq,yq->fcky", kspace_dual * mask_lines, inverse_rows)
    coil_values = complex_contract(
        "fckr,kx->fcrx",
        lax.all_to_all(spectrum, "row", split_axis=4, concat_axis=3, tiled=True),
        inverse_cols,
    )
    partial_sum = coil_combine(coil_values, sensitivity)
    data_back = lax.psum(partial_sum, "coil")
    time_stack = jnp.stack(
        [
            grad_one[0],
            grad_two[0],
            sym_one[0],
            sym_one[3],
            sym_one[4],
            sym_two[0],
            sym_two[3],
            sym_two[4],
        ]
    )
    rows_stack = jnp.stack(
        [
            grad_one[1],
            grad_two[1],
            sym_one[1],
            sym_one[3],
            sym_one[5],
            sym_two[1],
            sym_two[3],
            sym_two[5],
        ]
    )
    cols_stack = jnp.stack(
        [
            grad_one[2],
            grad_two[2],
            sym_one[2],
            sym_one[4],
            sym_one[5],
            sym_two[2],
            sym_two[4],
            sym_two[5],
        ]
    )
    adj_time = behind_time(time_stack)
    adj_rows = behind_rows(rows_stack)
    adj_cols = adjoint_diff(cols_stack, 4)
    tgv_one = BETA_ONE * adj_time[0] + adj_rows[0] + adj_cols[0]
    tgv_two = BETA_TWO * adj_time[1] + adj_rows[1] + adj_cols[1]
    sym_adj_one = jnp.stack(
        [
            BETA_ONE * adj_time[2] + 0.5 * adj_rows[3] + 0.5 * adj_cols[3],
            adj_rows[2] + 0.5 * BETA_ONE * adj_time[3] + 0.5 * adj_cols[4],
            adj_cols[2] + 0.5 * BETA_ONE * adj_time[4] + 0.5 * adj_rows[4],
        ]
    )
    sym_adj_two = jnp.stack(
        [
            BETA_TWO * adj_time[5] + 0.5 * adj_rows[6] + 0.5 * adj_cols[6],
            adj_rows[5] + 0.5 * BETA_TWO * adj_time[6] + 0.5 * adj_cols[7],
            adj_cols[5] + 0.5 * BETA_TWO * adj_time[7] + 0.5 * adj_rows[7],
        ]
    )
    image_new = image_now - TAU * (data_back + tgv_one)
    split_new = split_now - TAU * (tgv_two - tgv_one)
    vector_one_new = vector_one - TAU * (sym_adj_one - grad_one)
    vector_two_new = vector_two - TAU * (sym_adj_two - grad_two)
    image_bar = 2.0 * image_new - image_now
    split_bar = 2.0 * split_new - split_now
    vector_one_bar = 2.0 * vector_one_new - vector_one
    vector_two_bar = 2.0 * vector_two_new - vector_two
    row_spectrum = complex_contract(
        "fcyx,xk->fcyk", coil_images(image_bar, sensitivity), forward_cols
    )
    predicted = complex_contract(
        "fcyk,yq->fckq",
        lax.all_to_all(row_spectrum, "row", split_axis=4, concat_axis=3, tiled=True),
        forward_rows,
    )
    kspace_new = (kspace_dual + SIGMA * mask_lines * (predicted - measured)) / (
        1.0 + SIGMA / LAMBDA_DATA
    )
    field_stack = jnp.stack(
        [
            image_bar - split_bar,
            split_bar,
            vector_one_bar[0],
            vector_one_bar[1],
            vector_one_bar[2],
            vector_two_bar[0],
            vector_two_bar[1],
            vector_two_bar[2],
        ]
    )
    diff_time = ahead_time(field_stack)
    diff_rows = ahead_rows(field_stack)
    diff_cols = forward_diff(field_stack, 4)
    grad_one_step = jnp.stack([BETA_ONE * diff_time[0], diff_rows[0], diff_cols[0]])
    grad_two_step = jnp.stack([BETA_TWO * diff_time[1], diff_rows[1], diff_cols[1]])
    sym_one_step = jnp.stack(
        [
            BETA_ONE * diff_time[2],
            diff_rows[3],
            diff_cols[4],
            0.5 * (diff_rows[2] + BETA_ONE * diff_time[3]),
            0.5 * (diff_cols[2] + BETA_ONE * diff_time[4]),
            0.5 * (diff_cols[3] + diff_rows[4]),
        ]
    )
    sym_two_step = jnp.stack(
        [
            BETA_TWO * diff_time[5],
            diff_rows[6],
            diff_cols[7],
            0.5 * (diff_rows[5] + BETA_TWO * diff_time[6]),
            0.5 * (diff_cols[5] + BETA_TWO * diff_time[7]),
            0.5 * (diff_cols[6] + diff_rows[7]),
        ]
    )
    grad_one_new = project(grad_one + SIGMA * (grad_one_step - vector_one_bar), ALPHA_ONE)
    grad_two_new = project(grad_two + SIGMA * (grad_two_step - vector_two_bar), ALPHA_ONE)
    sym_one_new = project(sym_one + SIGMA * sym_one_step, ALPHA_ZERO)
    sym_two_new = project(sym_two + SIGMA * sym_two_step, ALPHA_ZERO)
    return (
        image_new,
        split_new,
        vector_one_new,
        vector_two_new,
        kspace_new,
        grad_one_new,
        grad_two_new,
        sym_one_new,
        sym_two_new,
    )


def solution(mesh):
    return jax.shard_map(
        body,
        mesh=mesh,
        in_specs=(
            P(None, "tm", "row", None),
            P(None, "tm", "row", None),
            P(None, None, "tm", "row", None),
            P(None, None, "tm", "row", None),
            P(None, "tm", "coil", "row", None),
            P(None, None, "tm", "row", None),
            P(None, None, "tm", "row", None),
            P(None, None, "tm", "row", None),
            P(None, None, "tm", "row", None),
            P(None, "tm", "coil", "row", None),
            P(None, "coil", "row", None),
            P("tm", None),
        ),
        out_specs=(
            P(None, "tm", "row", None),
            P(None, "tm", "row", None),
            P(None, None, "tm", "row", None),
            P(None, None, "tm", "row", None),
            P(None, "tm", "coil", "row", None),
            P(None, None, "tm", "row", None),
            P(None, None, "tm", "row", None),
            P(None, None, "tm", "row", None),
            P(None, None, "tm", "row", None),
        ),
        check_vma=False,
    )
```

profile of v0, /device:TPU:1, one launch (start us, length us, event | category | flops | bytes accessed | tf_op | source)
XLA Modules:
  0.0 165.4 jit_solution(15767861791778655400)
XLA Ops:
  7.2 1.8 %slice_dynamic-update-slice_fusion.23 = (f32[8,2,1,64,256]{4,3,2,1,0:T(8,128)}, f32[8,2,1,64,256]{4,3,2,1,0:T(8,128)S(1)}, f32[8,2,1,64,256]{4,3,2,1,0:T(8,128)S(1)}) fusion(f32[3,2,1,64,256]{4,3,2,1,0:T(8,128)} %param.17), kind=kLoop, calls=%fused_computation.203 | loop fusion | bytes 786432
  13.1 4.9 %collective-permute-start = (f32[8,2,1,64,256]{4,3,2,1,0:T(8,128)}, f32[8,2,1,64,256]{4,3,2,1,0:T(8,128)}, u32[]{:S(2)}, u32[]{:S(2)}) collective-permute-start(f32[8,2,1,64,256]{4,3,2,1,0:T(8,128)} %get-tuple-element.75), channel_id=1, source_target_pairs={{0,16},{16,32},{32,48},{48,64},{64,80},{80,96},{96,112},{112,128},... | collective-permute-start | bytes 3145736 | tf_op jit(solution)/shard_map/ppermute | solution.py:21
  18.0 3.1 %collective-permute-start.1 = (f32[8,2,1,1,256]{4,3,2,1,0:T(1,128)S(1)}, f32[8,2,1,1,256]{4,3,2,1,0:T(1,128)S(1)}, u32[]{:S(2)}, u32[]{:S(2)}) collective-permute-start(f32[8,2,1,1,256]{4,3,2,1,0:T(1,128)S(1)} %slice.374), channel_id=1, source_target_pairs={{0,4},{4,8},{8,12},{1,5},{5,9},{9,13},{2,6},{6,10},{10,14},{3,7},{... | collective-permute-start | bytes 49160 | tf_op jit(solution)/shard_map/ppermute | solution.py:21
  21.2 1.4 fusion.45
  22.6 1.4 fusion.32
  24.0 1.4 fusion.7
  25.4 1.4 fusion.6
  28.0 2.7 %reshape.1055 = f32[4,1,24576]{2,1,0:T(1,128)} reshape(f32[256,1,3,2,64]{4,3,2,1,0:T(2,128)} %bitcast.159) | data formatting | bytes 786432
  30.7 3.7 %all-to-all-start = ((f32[4,1,24576]{2,1,0:T(1,128)}), f32[4,1,24576]{2,1,0:T(1,128)S(1)}, u32[]{:S(2)}, u32[]{:S(2)}) async-start(f32[4,1,24576]{2,1,0:T(1,128)} %reshape.1055), calls=%async_computation | async-start | bytes 786432 | tf_op jit(solution)/shard_map/all_to_all | solution.py:156
  38.2 2.4 %maximum_subtract_fusion = f32[8,2,1,64,256]{4,3,2,1,0:T(8,128)} fusion(f32[8,2,1,63,256]{4,3,2,1,0:T(8,128)} %bitcast.154, f32[8,2,1,1,256]{4,3,2,1,0:T(1,128)S(1)} %collective-permute-done.1, f32[8,2,1,64,256]{4,3,2,1,0:T(8,128)S(1)} %get-tuple-element.79, pred[64]{0:T(512)(128)(4,1)S(1)} %add_compare_fusion), kind=kLoop, calls=%fused_computation.16 | loop fusion | flops 786432 | bytes 3145792 | tf_op jit(solution)/shard_map/sub | solution.py:129
  40.6 2.1 %all-to-all-done = f32[4,1,24576]{2,1,0:T(1,128)S(1)} async-done(((f32[4,1,24576]{2,1,0:T(1,128)}), f32[4,1,24576]{2,1,0:T(1,128)S(1)}, u32[]{:S(2)}, u32[]{:S(2)}) %all-to-all-start) | async-done | bytes 393248 | tf_op jit(solution)/shard_map/all_to_all | solution.py:156
  43.2 1.7 %reduce.6 = f32[4,24576]{1,0:T(4,128)S(1)} reduce(f32[4,1,24576]{2,1,0:T(1,128)S(1)} %all-to-all-done, f32[]{:T(128)} %broadcast.567), dimensions={1}, to_apply=%all_to_all.22.reduce_sub_computation | reduce | bytes 786436 | tf_op jit(solution)/shard_map/all_to_all | solution.py:156
  44.9 1.5 reshape.1056
  46.4 1.6 copy.69
  51.7 1.3 fusion.5
  54.4 1.3 add_reduce_fusion
  56.5 2.8 %select_subtract_fusion.1 = f32[8,2,1,64,256]{4,3,2,1,0:T(8,128)} fusion(f32[8,2,1,64,256]{4,3,2,1,0:T(8,128)} %collective-permute-done, f32[8,2,1,64,256]{4,3,2,1,0:T(8,128)} %get-tuple-element.75, pred[]{:T(512)S(6)} %eq.18), kind=kLoop, calls=%fused_computation.23 | loop fusion | flops 524288 | bytes 3145729 | tf_op jit(solution)/shard_map/sub | solution.py:121
  59.3 2.2 %fusion.84 = (f32[1,2,1,64,256]{4,3,2,1,0:T(8,128)}, f32[1,2,1,64,256]{4,3,2,1,0:T(8,128)}, f32[1,2,1,64,256]{4,3,2,1,0:T(8,128)}, f32[1,2,1,64,256]{4,3,2,1,0:T...) fusion(f32[8,2,1,64,256]{4,3,2,1,0:T(8,128)S(1)} %copy-done.10, ...), kind=kLoop, calls=%fused_computation.155 | loop fusion | flops 720896 | bytes 3145728 | tf_op jit(solution)/shard_map/add | solution.py:211
  61.5 43.0 %all-reduce.3.cloned.1.call-done = f32[2,1,64,256]{3,2,0,1:T(8,128)} async-done(((f32[2,1,64,256]{3,2,0,1:T(8,128)}), f32[2,1,64,256]{3,2,0,1:T(8,128)}) %all-reduce.3.cloned.1.call-update) | async-done | bytes 131088 | tf_op jit(solution)/shard_map/psum | solution.py:160
  104.5 2.0 %subtract_bitcast_fusion = (f32[1,2,1,64,256]{4,3,2,1,0:T(8,128)}, f32[2,1,64,256]{3,2,0,1:T(8,128)S(1)}, f32[2,1,64,256]{3,2,0,1:T(8,128)S(1)}, f32[2,1,64,256]{3,2,0,1:T(8,128)}) fusion(f32[2,1,64,256]{3,2,1,0:T(8,128)S(1)} %copy-done.19, f32[2,1,64,256]{3,2,0,1:T(8,128)} %all-reduce.3.cloned.1.call-done, f32[2,1,64,256]{3,2,1,0:T(8,128)S(1)} %copy-done.21, ...), kind=kLoop, calls=%fused_computation.183 | loop fusion | flops 557056 | bytes 1703936 | tf_op jit(solution)/shard_map/stack | solution.py:235
  107.8 1.5 fusion.26
  112.7 1.6 reshape.1057
  114.3 4.2 %all-to-all-start.1 = ((f32[4,1,24576]{2,1,0:T(1,128)}), f32[4,1,24576]{2,1,0:T(1,128)}, u32[]{:S(2)}, u32[]{:S(2)}) async-start(f32[4,1,24576]{2,1,0:T(1,128)} %reshape.1057), calls=%async_computation.1 | async-start | bytes 786432 | tf_op jit(solution)/shard_map/all_to_all | solution.py:229
  118.6 2.4 %multiply_subtract_fusion = (f32[3,2,1,64,256]{4,3,2,1,0:T(8,128)S(1)}, f32[3,2,1,64,256]{4,3,2,1,0:T(8,128)}, f32[3,2,1,64,256]{4,3,2,1,0:T(8,128)S(1)}, f32[3,2,1,64,256]{4,3,2,1,0:T(8,128)}) fusion(f32[3,2,1,64,256]{4,3,2,1,0:T(8,128)} %param.15, f32[3,2,1,64,256]{4,3,2,1,0:T(8,128)S(1)} %copy-done.2, f32[1,2,1,64,256]{4,3,2,1,0:T(8,128)S(1)} %copy-done.18, ...), kind=kLoop, calls=%fused_computation.53 | loop fusion | flops 1376256 | bytes 3932160 | tf_op jit(solution)/shard_map/sub | solution.py:223
  121.1 4.7 %collective-permute-start.2 = (f32[8,2,1,64,256]{4,3,2,1,0:T(8,128)S(1)}, f32[8,2,1,64,256]{4,3,2,1,0:T(8,128)}, u32[]{:S(2)}, u32[]{:S(2)}) collective-permute-start(f32[8,2,1,64,256]{4,3,2,1,0:T(8,128)S(1)} %pad_maximum_fusion), channel_id=1, source_target_pairs={{16,0},{32,16},{48,32},{64,48},{80,64},{96,80},{112,96},{128,112},... | collective-permute-start | bytes 3145736 | tf_op jit(solution)/shard_map/ppermute | solution.py:21
  131.9 3.3 %reduce.7 = f32[4,24576]{1,0:T(4,128)} reduce(f32[4,1,24576]{2,1,0:T(1,128)} %all-to-all-done.1, f32[]{:T(128)} %broadcast.567), dimensions={1}, to_apply=%all_to_all.25.reduce_sub_computation | reduce | bytes 786436 | tf_op jit(solution)/shard_map/all_to_all | solution.py:229
  135.2 2.5 %reshape.1058 = f32[256,1,3,2,64]{4,3,2,1,0:T(2,128)} reshape(f32[4,24576]{1,0:T(4,128)} %reduce.7) | data formatting | bytes 786432
  137.7 1.6 copy.68
  140.2 1.9 %reshape.1050 = f32[3,256,64]{1,2,0:T(8,128)} reshape(f32[1,1,3,4,64,64]{4,3,5,2,1,0:T(4,128)} %get-tuple-element.74) | data formatting | bytes 393216 | tf_op jit(solution)/shard_map/reshape.47
  142.2 1.9 %reshape.1051 = f32[3,256,64]{1,2,0:T(8,128)} reshape(f32[1,1,3,4,64,64]{4,3,5,2,1,0:T(4,128)} %get-tuple-element.73) | data formatting | bytes 393216 | tf_op jit(solution)/shard_map/reshape.51
  144.1 2.3 %fusion.36 = f32[3,64,256]{2,1,0:T(8,128)S(1)} fusion(f32[3,256,64]{1,2,0:T(8,128)} %reshape.1050), kind=kOutput, calls=%fused_computation.74 | convolution fusion | flops 151977984 | bytes 393216 | tf_op jit(solution)/shard_map/fcyk,yq->fckq/dot_general | solution.py:33
  152.0 1.8 %subtract_select_fusion = (f32[8,2,1,64,256]{4,3,2,1,0:T(8,128)S(1)}, f32[8,2,1,64,256]{4,3,2,1,0:T(8,128)S(1)}, f32[8,2,1,64,256]{4,3,2,1,0:T(8,128)S(1)}) fusion(f32[8,2,1,64,256]{4,3,2,1,0:T(8,128)} %collective-permute-done.2, pred[]{:T(512)S(6)} %eq.18, f32[3,2,1,64,256]{4,3,2,1,0:T(8,128)S(1)} %get-tuple-element.42, ...), kind=kLoop, calls=%fused_computation.21 | loop fusion | flops 2621440 | bytes 7340097 | tf_op jit(solution)/shard_map/jit(_where)/select_n | solution.py:107
  (139 shorter events, 36.9 us)
Async XLA Ops:
  7.2 1.8 %copy-start.2 = (f32[3,2,1,64,256]{4,3,2,1,0:T(8,128)S(1)}, f32[3,2,1,64,256]{4,3,2,1,0:T(8,128)}, u32[]{:S(2)}) copy-start(f32[3,2,1,64,256]{4,3,2,1,0:T(8,128)} %param.18) | copy-start | bytes 1179652
  7.2 2.5 %copy-start.1 = (f32[6,2,1,64,256]{4,3,2,1,0:T(8,128)S(1)}, f32[6,2,1,64,256]{4,3,2,1,0:T(8,128)}, u32[]{:S(2)}) copy-start(f32[6,2,1,64,256]{4,3,2,1,0:T(8,128)} %param.19) | copy-start | bytes 2359300
  12.3 8.9 %copy-start.13 = (f32[2,1,3,64,256]{4,3,2,1,0:T(8,128)S(1)}, f32[2,1,3,64,256]{4,3,2,1,0:T(8,128)}, u32[]{:S(2)}) copy-start(f32[2,1,3,64,256]{4,3,2,1,0:T(8,128)} %param.16) | copy-start | bytes 1179652
  13.1 10.9 %copy-start.6 = (f32[8,2,1,64,256]{4,3,2,1,0:T(8,128)}, f32[8,2,1,64,256]{4,3,2,1,0:T(8,128)S(1)}, u32[]{:S(2)}) copy-start(f32[8,2,1,64,256]{4,3,2,1,0:T(8,128)S(1)} %get-tuple-element.76) | copy-start | bytes 3145732
  13.1 43.4 %collective-permute-start = (f32[8,2,1,64,256]{4,3,2,1,0:T(8,128)}, f32[8,2,1,64,256]{4,3,2,1,0:T(8,128)}, u32[]{:S(2)}, u32[]{:S(2)}) collective-permute-start(f32[8,2,1,64,256]{4,3,2,1,0:T(8,128)} %get-tuple-element.75), channel_id=1, source_target_pairs={{0,16},{16,32},{32,48},{48,64},{64,80},{80,96},{96,112},{112,128},... | collective-permute-start | bytes 3145736 | tf_op jit(solution)/shard_map/ppermute | solution.py:21
  18.0 3.2 %copy-start.31 = (s32[1,256]{1,0:T(1,128)S(1)}, s32[1,256]{1,0:T(1,128)}, u32[]{:S(2)}) copy-start(s32[1,256]{1,0:T(1,128)} %param.23) | copy-start | bytes 3076
  18.0 20.2 %collective-permute-start.1 = (f32[8,2,1,1,256]{4,3,2,1,0:T(1,128)S(1)}, f32[8,2,1,1,256]{4,3,2,1,0:T(1,128)S(1)}, u32[]{:S(2)}, u32[]{:S(2)}) collective-permute-start(f32[8,2,1,1,256]{4,3,2,1,0:T(1,128)S(1)} %slice.374), channel_id=1, source_target_pairs={{0,4},{4,8},{8,12},{1,5},{5,9},{9,13},{2,6},{6,10},{10,14},{3,7},{... | collective-permute-start | bytes 49160 | tf_op jit(solution)/shard_map/ppermute | solution.py:21
  30.7 12.1 %all-to-all-start = ((f32[4,1,24576]{2,1,0:T(1,128)}), f32[4,1,24576]{2,1,0:T(1,128)S(1)}, u32[]{:S(2)}, u32[]{:S(2)}) async-start(f32[4,1,24576]{2,1,0:T(1,128)} %reshape.1055), calls=%async_computation | async-start | bytes 786432 | tf_op jit(solution)/shard_map/all_to_all | solution.py:156
  34.4 70.1 %all-reduce.3.cloned.1.call-start = ((), (), s32[]{:S(2)}) async-start(), calls=%async_computation.2 | async-start | bytes 262144 | tf_op jit(solution)/shard_map/psum | solution.py:160
  34.4 3.8 %copy-start.28 = (pred[64]{0:T(512)(128)(4,1)}, pred[64]{0:T(512)(128)(4,1)S(1)}, u32[]{:S(2)}) copy-start(pred[64]{0:T(512)(128)(4,1)S(1)} %add_compare_fusion) | copy-start | bytes 196
  56.4 2.9 %copy-start.10 = (f32[8,2,1,64,256]{4,3,2,1,0:T(8,128)S(1)}, f32[8,2,1,64,256]{4,3,2,1,0:T(8,128)}, u32[]{:S(2)}) copy-start(f32[8,2,1,64,256]{4,3,2,1,0:T(8,128)} %select_subtract_fusion) | copy-start | bytes 3145732
  56.4 2.9 %copy-start.11 = (f32[8,2,1,64,256]{4,3,2,1,0:T(8,128)S(1)}, f32[8,2,1,64,256]{4,3,2,1,0:T(8,128)}, u32[]{:S(2)}) copy-start(f32[8,2,1,64,256]{4,3,2,1,0:T(8,128)} %maximum_subtract_fusion) | copy-start | bytes 3145732
  59.3 45.2 %copy-start.19 = (f32[2,1,64,256]{3,2,1,0:T(8,128)S(1)}, f32[2,1,64,256]{3,2,1,0:T(8,128)}, u32[]{:S(2)}) copy-start(f32[2,1,64,256]{3,2,1,0:T(8,128)} %param.13) | copy-start | bytes 393220
  59.3 45.2 %copy-start.21 = (f32[2,1,64,256]{3,2,1,0:T(8,128)S(1)}, f32[2,1,64,256]{3,2,1,0:T(8,128)}, u32[]{:S(2)}) copy-start(f32[2,1,64,256]{3,2,1,0:T(8,128)} %param.12) | copy-start | bytes 393220
  104.5 2.0 %copy-start.34 = (f32[2,3,64,256]{3,2,1,0:T(8,128)S(1)}, f32[2,3,64,256]{3,2,1,0:T(8,128)}, u32[]{:S(2)}) copy-start(f32[2,3,64,256]{3,2,1,0:T(8,128)} %param.22) | copy-start | bytes 1179652
  106.5 2.9 %copy-start.20 = (f32[2,1,64,256]{3,2,0,1:T(8,128)}, f32[2,1,64,256]{3,2,0,1:T(8,128)S(1)}, u32[]{:S(2)}) copy-start(f32[2,1,64,256]{3,2,0,1:T(8,128)S(1)} %get-tuple-element.40) | copy-start | bytes 393220
  114.3 4.3 %copy-start.4 = (f32[3,2,1,64,256]{4,3,2,1,0:T(8,128)S(1)}, f32[3,2,1,64,256]{4,3,2,1,0:T(8,128)}, u32[]{:S(2)}) copy-start(f32[3,2,1,64,256]{4,3,2,1,0:T(8,128)} %param.17) | copy-start | bytes 1179652
  114.3 4.3 %copy-start.17 = (f32[1,2,1,64,256]{4,3,2,1,0:T(8,128)S(1)}, f32[1,2,1,64,256]{4,3,2,1,0:T(8,128)}, u32[]{:S(2)}) copy-start(f32[1,2,1,64,256]{4,3,2,1,0:T(8,128)} %get-tuple-element.46) | copy-start | bytes 393220
  114.3 4.3 %copy-start.18 = (f32[1,2,1,64,256]{4,3,2,1,0:T(8,128)S(1)}, f32[1,2,1,64,256]{4,3,2,1,0:T(8,128)}, u32[]{:S(2)}) copy-start(f32[1,2,1,64,256]{4,3,2,1,0:T(8,128)} %get-tuple-element.47) | copy-start | bytes 393220
  114.3 17.6 %all-to-all-start.1 = ((f32[4,1,24576]{2,1,0:T(1,128)}), f32[4,1,24576]{2,1,0:T(1,128)}, u32[]{:S(2)}, u32[]{:S(2)}) async-start(f32[4,1,24576]{2,1,0:T(1,128)} %reshape.1057), calls=%async_computation.1 | async-start | bytes 786432 | tf_op jit(solution)/shard_map/all_to_all | solution.py:229
  118.6 2.4 %copy-start.15 = (f32[1,2,1,64,256]{4,3,2,1,0:T(8,128)S(1)}, f32[1,2,1,64,256]{4,3,2,1,0:T(8,128)}, u32[]{:S(2)}) copy-start(f32[1,2,1,64,256]{4,3,2,1,0:T(8,128)} %get-tuple-element.38) | copy-start | bytes 393220
  121.1 30.3 %collective-permute-start.2 = (f32[8,2,1,64,256]{4,3,2,1,0:T(8,128)S(1)}, f32[8,2,1,64,256]{4,3,2,1,0:T(8,128)}, u32[]{:S(2)}, u32[]{:S(2)}) collective-permute-start(f32[8,2,1,64,256]{4,3,2,1,0:T(8,128)S(1)} %pad_maximum_fusion), channel_id=1, source_target_pairs={{16,0},{32,16},{48,32},{64,48},{80,64},{96,80},{112,96},{128,112},... | collective-permute-start | bytes 3145736 | tf_op jit(solution)/shard_map/ppermute | solution.py:21
  128.2 2.9 %copy-start.22 = (f32[2,1,64,256]{3,2,1,0:T(8,128)S(1)}, f32[2,1,64,256]{3,2,1,0:T(8,128)}, u32[]{:S(2)}) copy-start(f32[2,1,64,256]{3,2,1,0:T(8,128)} %param.12) | copy-start | bytes 393220
  128.2 2.9 %copy-start.23 = (f32[2,1,64,256]{3,2,0,1:T(8,128)S(1)}, f32[2,1,64,256]{3,2,0,1:T(8,128)}, u32[]{:S(2)}) copy-start(f32[2,1,64,256]{3,2,0,1:T(8,128)} %all-reduce.3.cloned.1.call-done) | copy-start | bytes 393220
  128.2 2.9 %copy-start.24 = (f32[2,1,64,256]{3,2,0,1:T(8,128)S(1)}, f32[2,1,64,256]{3,2,0,1:T(8,128)}, u32[]{:S(2)}) copy-start(f32[2,1,64,256]{3,2,0,1:T(8,128)} %get-tuple-element.41) | copy-start | bytes 393220
  129.9 21.5 %collective-permute-start.3 = (f32[8,2,1,1,256]{4,3,2,1,0:T(1,128)}, f32[8,2,1,1,256]{4,3,2,1,0:T(1,128)S(1)}, u32[]{:S(2)}, u32[]{:S(2)}) collective-permute-start(f32[8,2,1,1,256]{4,3,2,1,0:T(1,128)} %slice.406), channel_id=1, source_target_pairs={{4,0},{8,4},{12,8},{5,1},{9,5},{13,9},{6,2},{10,6},{14,10},{7,3},{... | collective-permute-start | bytes 49160 | tf_op jit(solution)/shard_map/ppermute | solution.py:21
  144.1 2.3 %copy-start.27 = (f32[3,256,64]{1,2,0:T(8,128)S(1)}, f32[3,256,64]{1,2,0:T(8,128)}, u32[]{:S(2)}) copy-start(f32[3,256,64]{1,2,0:T(8,128)} %reshape.1051) | copy-start | bytes 589828
  147.8 2.7 %copy-start.14 = (f32[2,1,3,64,256]{4,3,2,1,0:T(8,128)S(1)}, f32[2,1,3,64,256]{4,3,2,1,0:T(8,128)}, u32[]{:S(2)}) copy-start(f32[2,1,3,64,256]{4,3,2,1,0:T(8,128)} %param.16) | copy-start | bytes 1179652
  147.8 2.7 %copy-start.25 = (f32[2,1,3,64,256]{4,3,2,1,0:T(8,128)S(1)}, f32[2,1,3,64,256]{4,3,2,1,0:T(8,128)}, u32[]{:S(2)}) copy-start(f32[2,1,3,64,256]{4,3,2,1,0:T(8,128)} %param.21) | copy-start | bytes 1179652
  149.1 2.2 %copy-start.9 = (f32[8,2,1,64,255]{4,3,2,1,0:T(8,128)S(1)}, f32[8,2,1,64,255]{4,3,2,1,0:T(8,128)}, u32[]{:S(2)}) copy-start(f32[8,2,1,64,255]{4,3,2,1,0:T(8,128)} %slice.408) | copy-start | bytes 3133444
  149.2 2.2 %copy-start.16 = (f32[1,2,1,64,256]{4,3,2,1,0:T(8,128)S(1)}, f32[1,2,1,64,256]{4,3,2,1,0:T(8,128)}, u32[]{:S(2)}) copy-start(f32[1,2,1,64,256]{4,3,2,1,0:T(8,128)} %get-tuple-element.38) | copy-start | bytes 393220
  150.5 1.5 copy-start.12
  (10 other events, 12.2 us)
Sparse Core Ops, SparseCore 0:
  56.6 47.8 all-reduce.2
where the time goes:
time: 167 us; the launch traced here: 165 us
  waiting for transfers between devices  45.1 us (27%)
  local copies, waits for them, and re-layouts  32.5 us (19%)
  other arithmetic  28.5 us (17%)
  matrix products  22.6 us (14%)
  starting transfers between devices  22 us (13%)
  between operations  14.7 us (9%)
    psum x1, waiting for transfers between devices, body(): data_back = lax.psum(partial_sum, 'coil')  43 us
    unnamed x85, local copies, waits for them, and re-layouts  15.1 us
    ppermute x4, starting transfers between devices, shifted_2(): return lax.ppermute(block, axis, route)  14.1 us
    dot_general x4, matrix products, complex_contract(): jnp.einsum(pattern, values[0], tables[0], precision=HIGHEST)  6.27 us
    dot_general x4, matrix products, complex_contract(): jnp.einsum(pattern, values[0], tables[1], precision=HIGHEST)  5.58 us
    another operation x4, local copies, waits for them, and re-layouts  5.4 us
    dot_general x4, matrix products, complex_contract(): jnp.einsum(pattern, values[1], tables[1], precision=HIGHEST)  5.36 us
    dot_general x4, matrix products, complex_contract(): jnp.einsum(pattern, values[1], tables[0], precision=HIGHEST)  5.35 us
  transfers between devices with their start and end apart: 7, of which 2 were waited for; matrix products, arithmetic and copies ran while one was open for 36% of the time, Pallas kernels for 0%

commit v1 on v0

v1 whole, which is shorter than its diff:
```python
import functools
import math

import jax
import jax.numpy as jnp
import ml_dtypes
import numpy as np
from jax import lax
from jax.experimental import pallas as pl
from jax.experimental.pallas import tpu as pltpu
from jax.sharding import PartitionSpec as P

TAU = 0.25
SIGMA = 0.25
LAMBDA_DATA = 2.0
ALPHA_ONE = 2.0
ALPHA_ZERO = 1.2
BETA_ONE = 2.0
BETA_TWO = 0.5

LENGTH = 256
COIL = 3
BLOCK = 64
ROWS = 4
F32 = jnp.float32
BF16 = jnp.bfloat16
LIMIT = 24 * 1024 * 1024


def dft_table():
    positions = np.arange(LENGTH)
    angles = (positions[:, None] * positions[None, :] % LENGTH) * (2.0 * math.pi / LENGTH)
    real = np.cos(angles) / math.sqrt(LENGTH)
    imag = np.sin(angles) / math.sqrt(LENGTH)
    of_real = np.concatenate([real, imag], axis=1).reshape(ROWS, 1, BLOCK, 2 * LENGTH)
    of_imag = np.concatenate([-imag, real], axis=1).reshape(ROWS, 1, BLOCK, 2 * LENGTH)
    table = np.concatenate([of_real, of_imag], axis=1).reshape(2 * LENGTH, 2 * LENGTH)
    high = table.astype(ml_dtypes.bfloat16)
    low = (table - high.astype(np.float64)).astype(ml_dtypes.bfloat16)
    return high, low


def split(values):
    high = values.astype(BF16)
    return high, (values - high.astype(F32)).astype(BF16)


def dot_nt(a, b):
    return lax.dot_general(a, b, (((1,), (1,)), ((), ())), preferred_element_type=F32)


def dot_nn(a, b):
    return lax.dot_general(a, b, (((1,), (0,)), ((), ())), preferred_element_type=F32)


def first_transform(table_high, table_low, right, row):
    def blocks(ref):
        return jnp.concatenate(
            [ref[pl.ds(pl.multiple_of(lax.rem(row + d, ROWS) * 128, 128), BLOCK), :] for d in range(ROWS)], axis=0
        )

    high, low = split(right)
    left_high = blocks(table_high)
    return dot_nt(left_high, high) + (dot_nt(left_high, low) + dot_nt(blocks(table_low), high))


def second_transform(table_high, table_low, received, row):
    def blocks(ref):
        return jnp.concatenate(
            [ref[pl.ds(pl.multiple_of(lax.rem(row + ROWS - d, ROWS) * 128, 128), 128), :] for d in range(ROWS)], axis=0
        )

    left = jnp.concatenate(
        [
            jnp.concatenate([block[:BLOCK, 128 * c : 128 * (c + 1)] for block in received], axis=1)
            for c in range(COIL)
        ],
        axis=0,
    )
    high, low = split(left)
    right_high = blocks(table_high)
    return dot_nn(high, right_high) + (dot_nn(low, right_high) + dot_nn(high, blocks(table_low)))


def iota(shape, dimension):
    return lax.broadcasted_iota(jnp.int32, shape, dimension)


ROW_PARTS = (("g1", 1), ("g2", 1), ("s1", 1), ("s1", 3), ("s1", 5), ("s2", 1), ("s2", 3), ("s2", 5))
TIME_PARTS = (("g1", 0), ("g2", 0), ("s1", 0), ("s1", 3), ("s1", 4), ("s2", 0), ("s2", 3), ("s2", 4))


def start_kernel(kd_ref, lines_ref, th_ref, tl_ref, g1_ref, g2_ref, s1_ref, s2_ref, o0, o1, o2, o3):
    row = lax.axis_index("row")
    mask = lines_ref[...].astype(F32)
    parts = []
    for c in range(COIL):
        real = kd_ref[c] * mask
        imag = kd_ref[COIL + c] * mask
        parts.append(jnp.concatenate([real, -imag], axis=1))
        parts.append(jnp.concatenate([imag, real], axis=1))
    out = first_transform(th_ref, tl_ref, jnp.concatenate(parts, axis=0), row)
    for d, ref in enumerate((o0, o1, o2, o3)):
        ref[0:BLOCK, :] = out[BLOCK * d : BLOCK * (d + 1)]
    refs = dict(g1=g1_ref, g2=g2_ref, s1=s1_ref, s2=s2_ref)
    o1[BLOCK:, LENGTH:] = jnp.zeros((16, 128), F32)
    for index, (name, part) in enumerate(ROW_PARTS):
        for reim in range(2):
            place = BLOCK + 2 * index + reim
            o1[place : place + 1, 0:LENGTH] = refs[name][2 * part + reim, 7:8, :]


def chunk(ref, plane, i):
    return ref[plane, pl.ds(pl.multiple_of(i * 8, 8), 8), :]


def plain_kernel(img, spl, v1, v2, g1, g2, s1, s2, order, q_out, w_out):
    row = lax.axis_index("row")
    keep_time = (lax.axis_index("tm") != lax.axis_size("tm") - 1).astype(F32)
    refs = dict(g1=g1, g2=g2, s1=s1, s2=s2)

    def step(i, carry):
        rows = iota((8, LENGTH), 0)
        cols = iota((8, LENGTH), 1)
        drop_row = (rows == 7) & (i == 7) & (row == ROWS - 1)

        def adj_rows(ref, plane):
            here = chunk(ref, plane, i)
            above = chunk(ref, plane, jnp.maximum(i - 1, 0))
            above = jnp.where(i == 0, 0.0, above)
            behind = jnp.where(rows == 0, pltpu.roll(above, 1, 0), pltpu.roll(here, 1, 0))
            return behind - jnp.where(drop_row, 0.0, here)

        def adj_cols(ref, plane):
            here = chunk(ref, plane, i)
            behind = jnp.where(cols == 0, 0.0, pltpu.roll(here, 1, 1))
            return behind - jnp.where(cols == LENGTH - 1, 0.0, here)

        def put(ref, plane, value):
            ref[plane, pl.ds(pl.multiple_of(i * 8, 8), 8), :] = value

        for reim in range(2):
            for index, (name, part) in enumerate(TIME_PARTS):
                put(q_out, 2 * index + reim, chunk(refs[name], 2 * part + reim, i))
            z, y, x = reim, 2 + reim, 4 + reim
            one = -BETA_ONE * keep_time * chunk(g1, z, i) + adj_rows(g1, y) + adj_cols(g1, x)
            two = -BETA_TWO * keep_time * chunk(g2, z, i) + adj_rows(g2, y) + adj_cols(g2, x)
            image = chunk(img, reim, i) - 2.0 * TAU * one
            other = chunk(spl, reim, i) - 2.0 * TAU * (two - one)
            put(w_out, reim, image - other)
            put(w_out, 2 + reim, other)
            for base, vec, grad, sym, beta in ((4, v1, g1, s1, BETA_ONE), (10, v2, g2, s2, BETA_TWO)):
                p0, p1, p2, p3, p4, p5 = (2 * k + reim for k in range(6))
                first = -beta * keep_time * chunk(sym, p0, i) + 0.5 * (adj_rows(sym, p3) + adj_cols(sym, p4))
                second = adj_rows(sym, p1) - 0.5 * beta * keep_time * chunk(sym, p3, i) + 0.5 * adj_cols(sym, p5)
                third = adj_cols(sym, p2) - 0.5 * beta * keep_time * chunk(sym, p4, i) + 0.5 * adj_rows(sym, p5)
                for k, adjoint in enumerate((first, second, third)):
                    value = chunk(vec, 2 * k + reim, i) - 2.0 * TAU * (adjoint - chunk(grad, 2 * k + reim, i))
                    put(w_out, base + 2 * k + reim, value)
        return carry

    lax.fori_loop(0, 8, step, 0)


def combine_kernel(b0, b1, b2, b3, th_ref, tl_ref, sens, out):
    row = lax.axis_index("row")
    both = second_transform(th_ref, tl_ref, (b0, b1, b2, b3), row)
    real_sum = None
    for c in range(COIL):
        real = both[BLOCK * c : BLOCK * (c + 1), :LENGTH]
        imag = both[BLOCK * c : BLOCK * (c + 1), LENGTH:]
        real_term = sens[c] * real + sens[COIL + c] * imag
        imag_term = sens[c] * imag - sens[COIL + c] * real
        real_sum = real_term if real_sum is None else real_sum + real_term
        imag_sum = imag_term if c == 0 else imag_sum + imag_term
    out[0] = real_sum
    out[1] = imag_sum


def time_term(q, field):
    if field == 0:
        return -2.0 * TAU * (2.0 * BETA_ONE * q(0) - BETA_TWO * q(1))
    if field == 1:
        return -2.0 * TAU * (BETA_TWO * q(1) - BETA_ONE * q(0))
    beta = BETA_ONE if field < 5 else BETA_TWO
    return (-2.0 * TAU * beta * (1.0 if field in (2, 5) else 0.5)) * q(field)


def row_term(r, field):
    if field == 0:
        return -2.0 * TAU * (2.0 * r(0) - r(1))
    if field == 1:
        return -2.0 * TAU * (r(1) - r(0))
    index, factor = {2: (3, 0.5), 3: (2, 1.0), 4: (4, 0.5), 5: (6, 0.5), 6: (5, 1.0), 7: (7, 0.5)}[field]
    return (-2.0 * TAU * factor) * r(index)


def predict_kernel(sum_a, sum_b, w, q_in, b1, th_ref, tl_ref, sens, o0, o1, o2, o3, z_out):
    row = lax.axis_index("row")
    rows = iota((BLOCK, LENGTH), 0)
    above = jnp.where(row == 0, 0.0, b1[BLOCK:, 0:LENGTH])
    image = []
    for reim in range(2):
        back = sum_a[reim] + sum_b[reim]
        z_out[BLOCK * reim : BLOCK * (reim + 1), :] = back
        value = w[reim] + w[2 + reim] - 2.0 * TAU * BETA_ONE * q_in[reim] - 2.0 * TAU * back
        image.append(value - 2.0 * TAU * jnp.where(rows == 0, above[reim : reim + 1], 0.0))
    z_out[2 * BLOCK :, :] = above
    parts = []
    for c in range(COIL):
        real = sens[c] * image[0] - sens[COIL + c] * image[1]
        imag = sens[c] * image[1] + sens[COIL + c] * image[0]
        parts.append(jnp.concatenate([real, imag], axis=1))
        parts.append(jnp.concatenate([-imag, real], axis=1))
    out = first_transform(th_ref, tl_ref, jnp.concatenate(parts, axis=0), row)
    for d, ref in enumerate((o0, o1, o2, o3)):
        ref[0:BLOCK, :] = out[BLOCK * d : BLOCK * (d + 1)]
    o3[BLOCK:, LENGTH:] = jnp.zeros((16, 128), F32)
    for field in range(8):
        for reim in range(2):
            plane = 2 * field + reim
            value = w[plane, 0:1, :]
            value += time_term(lambda k: q_in[2 * k + reim, 0:1, :], field)
            value += row_term(lambda k: above[2 * k + reim : 2 * k + reim + 1], field)
            if field == 0:
                value -= 2.0 * TAU * (sum_a[reim, 0:1, :] + sum_b[reim, 0:1, :])
            o3[BLOCK + plane : BLOCK + plane + 1, 0:LENGTH] = value


def finish_kernel(b0, b1, b2, b3, th_ref, tl_ref, kd_ref, measured, lines_ref, out):
    row = lax.axis_index("row")
    both = second_transform(th_ref, tl_ref, (b0, b1, b2, b3), row)
    mask = SIGMA * lines_ref[...].astype(F32)
    scale = 1.0 / (1.0 + SIGMA / LAMBDA_DATA)
    for c in range(COIL):
        real = both[BLOCK * c : BLOCK * (c + 1), :LENGTH]
        imag = -both[BLOCK * c : BLOCK * (c + 1), LENGTH:]
        out[c] = (kd_ref[c] + mask * (real - measured[c])) * scale
        out[COIL + c] = (kd_ref[COIL + c] + mask * (imag - measured[COIL + c])) * scale


def fields_kernel(
    img, spl, v1, v2, g1, g2, s1, s2, w, q_in, w_in, z, z_in, b1, n3,
    img_out, spl_out, v1_out, v2_out, g1_out, g2_out, s1_out, s2_out, bar,
):
    row = lax.axis_index("row")
    last_frame = lax.axis_index("tm") == lax.axis_size("tm") - 1
    refs = dict(g1=g1, g2=g2, s1=s1, s2=s2)
    above = jnp.where(row == 0, 0.0, b1[BLOCK:, 0:LENGTH])
    bar[:, BLOCK:, :] = jnp.zeros((16, 8, LENGTH), F32)
    for plane in range(16):
        bar[plane, BLOCK : BLOCK + 1, :] = n3[BLOCK + plane : BLOCK + plane + 1, 0:LENGTH]

    def span(i):
        return pl.ds(pl.multiple_of(i * 8, 8), 8)

    def first(i, carry):
        rows = iota((8, LENGTH), 0)
        top = (rows == 0) & (i == 0)
        for reim in range(2):
            values = []
            for field in range(8):
                plane = 2 * field + reim
                value = chunk(w, plane, i) + time_term(lambda k: chunk(q_in, 2 * k + reim, i), field)
                extra = row_term(lambda k: above[2 * k + reim : 2 * k + reim + 1], field)
                value += jnp.where(top, extra, 0.0)
                if field == 0:
                    value -= 2.0 * TAU * z[pl.ds(pl.multiple_of(BLOCK * reim + i * 8, 8), 8), :]
                bar[plane, span(i), :] = value
                values.append(value)
            img_out[reim, span(i), :] = 0.5 * (values[0] + values[1] + chunk(img, reim, i))
            spl_out[reim, span(i), :] = 0.5 * (values[1] + chunk(spl, reim, i))
            for k in range(3):
                plane = 2 * k + reim
                v1_out[plane, span(i), :] = 0.5 * (values[2 + k] + chunk(v1, plane, i))
                v2_out[plane, span(i), :] = 0.5 * (values[5 + k] + chunk(v2, plane, i))
        return carry

    lax.fori_loop(0, 8, first, 0)

    def second(i, carry):
        rows = iota((8, LENGTH), 0)
        cols = iota((8, LENGTH), 1)
        top = (rows == 0) & (i == 0)
        end_row = (rows == 7) & (i == 7) & (row == ROWS - 1)

        def along_rows(plane):
            here = chunk(bar, plane, i)
            below = chunk(bar, plane, i + 1)
            ahead = jnp.where(rows == 7, pltpu.roll(below, 7, 0), pltpu.roll(here, 7, 0))
            return jnp.where(end_row, 0.0, ahead - here)

        def along_cols(plane):
            here = chunk(bar, plane, i)
            ahead = pltpu.roll(here, LENGTH - 1, 1)
            return jnp.where(cols == LENGTH - 1, 0.0, ahead - here)

        def along_time(field, reim):
            plane = 2 * field + reim
            value = chunk(w_in, plane, i)
            value += time_term(lambda k: chunk(refs[TIME_PARTS[k][0]], 2 * TIME_PARTS[k][1] + reim, i), field)
            extra = row_term(
                lambda k: z_in[2 * BLOCK + 2 * k + reim : 2 * BLOCK + 2 * k + reim + 1, :], field
            )
            value += jnp.where(top, extra, 0.0)
            if field == 0:
                value -= 2.0 * TAU * z_in[pl.ds(pl.multiple_of(BLOCK * reim + i * 8, 8), 8), :]
            return jnp.where(last_frame, 0.0, value - chunk(bar, plane, i))

        def project(out, duals, radius):
            total = duals[0] * duals[0]
            for value in duals[1:]:
                total += value * value
            scale = 1.0 / jnp.maximum(1.0, jnp.sqrt(total) * (1.0 / radius))
            for plane, value in enumerate(duals):
                out[plane, span(i), :] = value * scale

        for dual, out, field, vec, beta in ((g1, g1_out, 0, 2, BETA_ONE), (g2, g2_out, 1, 5, BETA_TWO)):
            duals = []
            for k in range(3):
                for reim in range(2):
                    if k == 0:
                        diff = beta * along_time(field, reim)
                    else:
                        diff = (along_rows, along_cols)[k - 1](2 * field + reim)
                    diff -= chunk(bar, 2 * (vec + k) + reim, i)
                    duals.append(chunk(dual, 2 * k + reim, i) + SIGMA * diff)
            project(out, duals, ALPHA_ONE)
        for dual, out, vec, beta in ((s1, s1_out, 2, BETA_ONE), (s2, s2_out, 5, BETA_TWO)):
            duals = [None] * 12
            for reim in range(2):
                p0, p1, p2 = (2 * (vec + k) + reim for k in range(3))
                steps = (
                    beta * along_time(vec, reim),
                    along_rows(p1),
                    along_cols(p2),
                    0.5 * (along_rows(p0) + beta * along_time(vec + 1, reim)),
                    0.5 * (along_cols(p0) + beta * along_time(vec + 2, reim)),
                    0.5 * (along_cols(p1) + along_rows(p2)),
                )
                for k, diff in enumerate(steps):
                    duals[2 * k + reim] = chunk(dual, 2 * k + reim, i) + SIGMA * diff
            project(out, duals, ALPHA_ZERO)
        return carry

    lax.fori_loop(0, 8, second, 0)


def shape(*dims):
    return jax.ShapeDtypeStruct(dims, F32)


def call(kernel, outs, ins, flops, in_specs=None, scratch=(), grid=()):
    size = sum(math.prod(x.shape) * x.dtype.itemsize for x in (*ins, *outs))
    return pl.pallas_call(
        kernel,
        out_shape=outs,
        grid=grid,
        in_specs=in_specs or [pl.BlockSpec(memory_space=pltpu.VMEM)] * len(ins),
        out_specs=[pl.BlockSpec(memory_space=pltpu.VMEM)] * len(outs),
        scratch_shapes=list(scratch),
        compiler_params=pltpu.CompilerParams(vmem_limit_bytes=LIMIT),
        cost_estimate=pl.CostEstimate(flops=flops, bytes_accessed=size, transcendentals=0),
    )(*ins)


def turn(block, distance):
    return lax.ppermute(block, "row", [(i, (i + distance) % ROWS) for i in range(ROWS)])


def body(
    image_now, split_now, vector_one, vector_two, kspace_dual, grad_one, grad_two, sym_one, sym_two,
    measured, sensitivity, sampled,
):
    planes = lambda x: x.reshape(-1, BLOCK, LENGTH)
    img, spl, v1, v2, kd = map(planes, (image_now, split_now, vector_one, vector_two, kspace_dual))
    g1, g2, s1, s2, meas, sens = map(planes, (grad_one, grad_two, sym_one, sym_two, measured, sensitivity))
    high, low = map(jnp.asarray, dft_table())
    frames = lax.axis_size("tm")
    vmem = pl.BlockSpec(memory_space=pltpu.VMEM)
    blocks = (shape(BLOCK, 384), shape(BLOCK + 16, 384), shape(BLOCK, 384), shape(BLOCK, 384))

    def bottom(x):
        return pl.BlockSpec((x.shape[0], 8, LENGTH), lambda _: (0, BLOCK // 8 - 1, 0))

    a0, a1, a2, a3 = call(
        start_kernel, blocks, (kd, sampled, high, low, g1, g2, s1, s2), 6 * 256 * 512 * 384,
        in_specs=[vmem] * 4 + [bottom(x) for x in (g1, g2, s1, s2)], grid=(1,),
    )
    b1, b2, b3 = turn(a1, 1), turn(a2, 2), turn(a3, 3)
    q_out, w_out = call(
        plain_kernel, (shape(16, BLOCK, LENGTH), shape(16, BLOCK, LENGTH)),
        (img, spl, v1, v2, g1, g2, s1, s2, a0), 16 * 30 * BLOCK * LENGTH,
        in_specs=[vmem] * 8 + [pl.BlockSpec(memory_space=pl.ANY)],
    )
    q_in = lax.ppermute(q_out, "tm", [(i, i + 1) for i in range(frames - 1)])
    pairs = []
    groups = lax.axis_size("coil")
    for t in range(1, frames):
        for c in range(groups):
            to = c if t % 2 else ((c + 1) % groups if t % 4 == 2 else (c - 1) % groups)
            pairs.append((t * groups + c, (t - 1) * groups + to))
    w_in = lax.ppermute(w_out, ("tm", "coil"), pairs)
    (partial,) = call(
        combine_kernel, (shape(2, BLOCK, LENGTH),), (a0, b1, b2, b3, high, low, sens), 6 * 192 * 512 * 512
    )
    pair = partial + lax.ppermute(partial, "coil", [(0, 1), (1, 0), (2, 3), (3, 2)])
    rest = lax.ppermute(pair, "coil", [(0, 3), (3, 0), (1, 2), (2, 1)])
    c_blocks = (shape(BLOCK, 384), shape(BLOCK, 384), shape(BLOCK, 384), shape(BLOCK + 16, 384))
    c0, c1, c2, c3, z = call(
        predict_kernel, (*c_blocks, shape(2 * BLOCK + 16, LENGTH)),
        (pair, rest, w_out, q_in, b1, high, low, sens), 6 * 256 * 512 * 384,
    )
    n3, n1, n2 = turn(c3, 3), turn(c1, 1), turn(c2, 2)
    z_in = lax.ppermute(z, "tm", [(i + 1, i) for i in range(frames - 1)])
    like = lambda x: shape(*x.shape)
    fields = call(
        fields_kernel, tuple(map(like, (img, spl, v1, v2, g1, g2, s1, s2))),
        (img, spl, v1, v2, g1, g2, s1, s2, w_out, q_in, w_in, z, z_in, b1, n3), 16 * 60 * BLOCK * LENGTH,
        scratch=[pltpu.VMEM((16, BLOCK + 8, LENGTH), F32)],
    )
    (kspace,) = call(
        finish_kernel, (like(kd),), (c0, n1, n2, n3, high, low, kd, meas, sampled), 6 * 192 * 512 * 512
    )
    img_new, spl_new, v1_new, v2_new, g1_new, g2_new, s1_new, s2_new = fields
    news = (img_new, spl_new, v1_new, v2_new, kspace, g1_new, g2_new, s1_new, s2_new)
    olds = (image_now, split_now, vector_one, vector_two, kspace_dual, grad_one, grad_two, sym_one, sym_two)
    return tuple(new.reshape(old.shape) for new, old in zip(news, olds))


def solution(mesh):
    image = P(None, "tm", "row", None)
    vector = P(None, None, "tm", "row", None)
    kspace = P(None, "tm", "coil", "row", None)
    return jax.shard_map(
        body,
        mesh=mesh,
        in_specs=(
            image, image, vector, vector, kspace, vector, vector, vector, vector, kspace,
            P(None, "coil", "row", None), P("tm", None),
        ),
        out_specs=(image, image, vector, vector, kspace, vector, vector, vector, vector),
        check_vma=False,
    )
```

time: 167 us -> 65.8 us (0.39)
  the two profiles are of different devices: /device:TPU:1 before, /device:TPU:80 now
where the time goes in v1:
time: 65.8 us; the launch traced here: 65.3 us
  starting transfers between devices  29.8 us (45%)
  waiting for transfers between devices  18.2 us (28%)
  local copies, waits for them, and re-layouts  9.05 us (14%)
  Pallas kernels  7.39 us (11%)
  between operations  0.82 us (1%)
    ppermute x6, starting transfers between devices, turn(): lax.ppermute(block, 'row', [(i, (i + distance) % ROWS) for i in range(ROW...  10.8 us
    ppermute x6, waiting for transfers between devices, turn(): lax.ppermute(block, 'row', [(i, (i + distance) % ROWS) for i in range(ROW...  10.8 us
    unnamed x40, local copies, waits for them, and re-layouts  9.05 us
    ppermute x1, starting transfers between devices, body(): rest = lax.ppermute(pair, 'coil', [(0, 3), (3, 0), (1, 2), (2, 1)])  7.41 us
    pallas_call x6, Pallas kernels, call(): pl.pallas_call(kernel, out_shape=outs, grid=grid, in_specs=in_specs or [p...  7.39 us
    ppermute x1, starting transfers between devices, body(): lax.ppermute(partial, 'coil', [(0, 1), (1, 0), (2, 3), (3, 2)])  4.96 us
    ppermute x1, waiting for transfers between devices, body(): rest = lax.ppermute(pair, 'coil', [(0, 3), (3, 0), (1, 2), (2, 1)])  4.35 us
    ppermute x1, waiting for transfers between devices, body(): lax.ppermute(partial, 'coil', [(0, 1), (1, 0), (2, 3), (3, 2)])  3.05 us
  transfers between devices with their start and end apart: 11, of which 4 were waited for; matrix products, arithmetic and copies ran while one was open for 0% of the time, Pallas kernels for 4%

profile of v1, /device:TPU:80, one launch (start us, length us, event | category | flops | bytes accessed | tf_op | source)
XLA Modules:
  0.0 65.3 jit_solution(7933587625776777672)
XLA Ops:
  0.7 0.7 %copy-done.19 = s32[1,256]{1,0:T(1,128)S(1)} copy-done((s32[1,256]{1,0:T(1,128)S(1)}, s32[1,256]{1,0:T(1,128)}, u32[]{:S(2)}) %copy-start.19) | copy-done | bytes 1048
  1.3 1.0 %copy-done = bf16[512,512]{1,0:T(8,128)(2,1)S(1)} copy-done((bf16[512,512]{1,0:T(8,128)(2,1)S(1)}, bf16[512,512]{1,0:T(8,128)(2,1)}, u32[]{:S(2)}) %copy-start) | copy-done | bytes 524312
  2.4 1.0 %copy-done.2 = bf16[512,512]{1,0:T(8,128)(2,1)S(1)} copy-done((bf16[512,512]{1,0:T(8,128)(2,1)S(1)}, bf16[512,512]{1,0:T(8,128)(2,1)}, u32[]{:S(2)}) %copy-start.2) | copy-done | bytes 524312
  3.4 1.1 %copy-done.4 = f32[6,2,1,64,256]{4,3,2,1,0:T(8,128)S(1)} copy-done((f32[6,2,1,64,256]{4,3,2,1,0:T(8,128)S(1)}, f32[6,2,1,64,256]{4,3,2,1,0:T(8,128)}, u32[]{:S(2)}) %copy-start.4) | copy-done | bytes 786456
  4.5 1.1 %copy-done.6 = f32[6,2,1,64,256]{4,3,2,1,0:T(8,128)S(1)} copy-done((f32[6,2,1,64,256]{4,3,2,1,0:T(8,128)S(1)}, f32[6,2,1,64,256]{4,3,2,1,0:T(8,128)}, u32[]{:S(2)}) %copy-start.6) | copy-done | bytes 786456
  5.7 1.0 %copy-done.8 = f32[3,2,1,64,256]{4,3,2,1,0:T(8,128)S(1)} copy-done((f32[3,2,1,64,256]{4,3,2,1,0:T(8,128)S(1)}, f32[3,2,1,64,256]{4,3,2,1,0:T(8,128)}, u32[]{:S(2)}) %copy-start.8) | copy-done | bytes 393240
  6.7 1.0 %copy-done.10 = f32[3,2,1,64,256]{4,3,2,1,0:T(8,128)S(1)} copy-done((f32[3,2,1,64,256]{4,3,2,1,0:T(8,128)S(1)}, f32[3,2,1,64,256]{4,3,2,1,0:T(8,128)}, u32[]{:S(2)}) %copy-start.10) | copy-done | bytes 393240
  7.7 1.0 %copy-done.12 = f32[2,1,3,64,256]{4,3,2,1,0:T(8,128)S(1)} copy-done((f32[2,1,3,64,256]{4,3,2,1,0:T(8,128)S(1)}, f32[2,1,3,64,256]{4,3,2,1,0:T(8,128)}, u32[]{:S(2)}) %copy-start.12) | copy-done | bytes 393240
  8.7 0.6 shard_map.205
  9.3 0.5 copy-done.5
  9.8 0.2 copy-done.7
  10.0 0.1 copy-done.13
  10.1 0.1 copy-done.14
  10.3 1.0 %shard_map.206 = (f32[16,64,256]{2,1,0:T(8,128)S(1)}, f32[16,64,256]{2,1,0:T(8,128)S(1)}) custom-call(f32[2,64,256]{2,1,0:T(8,128)S(1)} %bitcast.58, f32[2,64,256]{2,1,0:T(8,128)S(1)} %bitcast.60, f32[6,64,256]{2,1,0:T(8,128)S(1)} %bitcast.52, f32[6,64,256]{2,1,0:T(8,128)S(1)} %bitcast.54, f32[6,64,256]{2,1,0:T(8,128)S(1)} %bitcast.45, ...), custom_call_target="tpu_custom_call" | custom-call | flops 7864320 | bytes 5603328 | tf_op jit(solution)/shard_map/pallas_call | solution.py:355
  11.3 1.9 %collective-permute-start = (f32[16,64,256]{2,1,0:T(8,128)S(1)}, f32[16,64,256]{2,1,0:T(8,128)S(1)}, u32[]{:S(2)}, u32[]{:S(2)}) collective-permute-start(f32[16,64,256]{2,1,0:T(8,128)S(1)} %get-tuple-element.30), channel_id=1, source_target_pairs={{0,16},{16,32},{32,48},{48,64},{64,80},{80,96},{96,112},{112,128},... | collective-permute-start | bytes 3145736 | tf_op jit(solution)/shard_map/ppermute | solution.py:396
  13.2 2.7 %collective-permute-start.1 = (f32[16,64,256]{2,1,0:T(8,128)S(1)}, f32[16,64,256]{2,1,0:T(8,128)S(1)}, u32[]{:S(2)}, u32[]{:S(2)}) collective-permute-start(f32[16,64,256]{2,1,0:T(8,128)S(1)} %get-tuple-element.29.w), channel_id=1, source_target_pairs={{16,0},{17,1},{18,2},{19,3},{32,17},{33,18},{34,19},{35,16},{48,32... | collective-permute-start | bytes 3145736 | tf_op jit(solution)/shard_map/ppermute | solution.py:403
  16.0 1.6 %collective-permute-start.2 = (f32[80,384]{1,0:T(8,128)S(1)}, f32[80,384]{1,0:T(8,128)S(1)}, u32[]{:S(2)}, u32[]{:S(2)}) collective-permute-start(f32[80,384]{1,0:T(8,128)S(1)} %get-tuple-element.31), channel_id=1, source_target_pairs={{0,4},{4,8},{8,12},{12,0},{1,5},{5,9},{9,13},{13,1},{2,6},{6,10},{... | collective-permute-start | bytes 368648 | tf_op jit(solution)/shard_map/ppermute | solution.py:368
  17.6 2.7 %collective-permute-start.3 = (f32[64,384]{1,0:T(8,128)S(1)}, f32[64,384]{1,0:T(8,128)S(1)}, u32[]{:S(2)}, u32[]{:S(2)}) collective-permute-start(f32[64,384]{1,0:T(8,128)S(1)} %get-tuple-element.32), channel_id=1, source_target_pairs={{0,8},{4,12},{8,0},{12,4},{1,9},{5,13},{9,1},{13,5},{2,10},{6,14},... | collective-permute-start | bytes 294920 | tf_op jit(solution)/shard_map/ppermute | solution.py:368
  20.3 1.4 %collective-permute-start.4 = (f32[64,384]{1,0:T(8,128)S(1)}, f32[64,384]{1,0:T(8,128)S(1)}, u32[]{:S(2)}, u32[]{:S(2)}) collective-permute-start(f32[64,384]{1,0:T(8,128)S(1)} %get-tuple-element.33), channel_id=1, source_target_pairs={{0,12},{4,0},{8,4},{12,8},{1,13},{5,1},{9,5},{13,9},{2,14},{6,2},{... | collective-permute-start | bytes 294920 | tf_op jit(solution)/shard_map/ppermute | solution.py:368
  21.7 4.6 %collective-permute-done.3.b2 = f32[64,384]{1,0:T(8,128)S(1)} collective-permute-done((f32[64,384]{1,0:T(8,128)S(1)}, f32[64,384]{1,0:T(8,128)S(1)}, u32[]{:S(2)}, u32[]{:S(2)}) %collective-permute-start.3) | collective-permute-done | bytes 98336 | tf_op jit(solution)/shard_map/ppermute | solution.py:368
  26.4 0.5 shard_map.207
  26.9 5.0 %collective-permute-start.5 = (f32[2,64,256]{2,1,0:T(8,128)S(1)}, f32[2,64,256]{2,1,0:T(8,128)S(1)}, u32[]{:S(2)}, u32[]{:S(2)}) collective-permute-start(f32[2,64,256]{2,1,0:T(8,128)S(1)} %shard_map.207), channel_id=1, source_target_pairs={{0,1},{1,0},{2,3},{3,2},{4,5},{5,4},{6,7},{7,6},{8,9},{9,8},{10,11... | collective-permute-start | bytes 393224 | tf_op jit(solution)/shard_map/ppermute | solution.py:407
  31.8 3.1 %collective-permute-done.5 = f32[2,64,256]{2,1,0:T(8,128)S(1)} collective-permute-done((f32[2,64,256]{2,1,0:T(8,128)S(1)}, f32[2,64,256]{2,1,0:T(8,128)S(1)}, u32[]{:S(2)}, u32[]{:S(2)}) %collective-permute-start.5) | collective-permute-done | bytes 131104 | tf_op jit(solution)/shard_map/ppermute | solution.py:407
  34.9 7.4 %collective-permute-start.6 = (f32[2,64,256]{2,1,0:T(8,128)S(1)}, f32[2,64,256]{2,1,0:T(8,128)S(1)}, u32[]{:S(2)}, u32[]{:S(2)}) collective-permute-start(f32[2,64,256]{2,1,0:T(8,128)S(1)} %add.3.sum_a), channel_id=1, source_target_pairs={{0,3},{3,0},{1,2},{2,1},{4,7},{7,4},{5,6},{6,5},{8,11},{11,8},{9,1... | collective-permute-start | bytes 393224 | tf_op jit(solution)/shard_map/ppermute | solution.py:408
  42.3 4.4 %collective-permute-done.6.sum_b = f32[2,64,256]{2,1,0:T(8,128)S(1)} collective-permute-done((f32[2,64,256]{2,1,0:T(8,128)S(1)}, f32[2,64,256]{2,1,0:T(8,128)S(1)}, u32[]{:S(2)}, u32[]{:S(2)}) %collective-permute-start.6) | collective-permute-done | bytes 131104 | tf_op jit(solution)/shard_map/ppermute | solution.py:408
  46.7 0.7 shard_map.208
  47.3 2.7 %collective-permute-start.8 = (f32[80,384]{1,0:T(8,128)S(1)}, f32[80,384]{1,0:T(8,128)S(1)}, u32[]{:S(2)}, u32[]{:S(2)}) collective-permute-start(f32[80,384]{1,0:T(8,128)S(1)} %get-tuple-element.35), channel_id=1, source_target_pairs={{0,12},{4,0},{8,4},{12,8},{1,13},{5,1},{9,5},{13,9},{2,14},{6,2},{... | collective-permute-start | bytes 368648 | tf_op jit(solution)/shard_map/ppermute | solution.py:368
  50.1 1.9 %collective-permute-start.7 = (f32[144,256]{1,0:T(8,128)S(1)}, f32[144,256]{1,0:T(8,128)S(1)}, u32[]{:S(2)}, u32[]{:S(2)}) collective-permute-start(f32[144,256]{1,0:T(8,128)S(1)} %get-tuple-element.34.z), channel_id=1, source_target_pairs={{16,0},{32,16},{48,32},{64,48},{80,64},{96,80},{112,96},{128,112},... | collective-permute-start | bytes 442376 | tf_op jit(solution)/shard_map/ppermute | solution.py:415
  52.1 2.3 %collective-permute-start.10 = (f32[64,384]{1,0:T(8,128)S(1)}, f32[64,384]{1,0:T(8,128)S(1)}, u32[]{:S(2)}, u32[]{:S(2)}) collective-permute-start(f32[64,384]{1,0:T(8,128)S(1)} %get-tuple-element.42), channel_id=1, source_target_pairs={{0,8},{4,12},{8,0},{12,4},{1,9},{5,13},{9,1},{13,5},{2,10},{6,14},... | collective-permute-start | bytes 294920 | tf_op jit(solution)/shard_map/ppermute | solution.py:368
  54.4 6.2 %collective-permute-done.9.b1 = f32[64,384]{1,0:T(8,128)S(1)} collective-permute-done((f32[64,384]{1,0:T(8,128)S(1)}, f32[64,384]{1,0:T(8,128)S(1)}, u32[]{:S(2)}, u32[]{:S(2)}) %collective-permute-start.9) | collective-permute-done | bytes 98336 | tf_op jit(solution)/shard_map/ppermute | solution.py:368
  60.6 1.3 %shard_map.210 = f32[6,64,256]{2,1,0:T(8,128)} custom-call(f32[64,384]{1,0:T(8,128)S(1)} %get-tuple-element.40.b0, f32[64,384]{1,0:T(8,128)S(1)} %collective-permute-done.9.b1, f32[64,384]{1,0:T(8,128)S(1)} %collective-permute-done.10.b2, f32[80,384]{1,0:T(8,128)S(1)} %collective-permute-done.8.n3.b3, bf16[512,512]{1,0:T(8,128)(2,1)S(1)} %copy-done.1, ...), custom_call_target="tpu_custom_call" | custom-call | flops 301989888 | bytes 2647040 | tf_op jit(solution)/shard_map/pallas_call | solution.py:355
  61.9 3.4 %shard_map.209 = (f32[2,64,256]{2,1,0:T(8,128)}, f32[2,64,256]{2,1,0:T(8,128)}, f32[6,64,256]{2,1,0:T(8,128)}, f32[6,64,256]{2,1,0:T(8,128)}, f32[6,64,256]{2,1,...) custom-call(f32[2,64,256]{2,1,0:T(8,128)S(1)} %bitcast.59, ...), custom_call_target="tpu_custom_call" | custom-call | flops 15728640 | bytes 10502144 | tf_op jit(solution)/shard_map/pallas_call | solution.py:355
  (37 shorter events, 0.2 us)
Async XLA Ops:
  0.6 0.7 %copy-start.19 = (s32[1,256]{1,0:T(1,128)S(1)}, s32[1,256]{1,0:T(1,128)}, u32[]{:S(2)}) copy-start(s32[1,256]{1,0:T(1,128)} %lines_ref.3) | copy-start | bytes 3076
  1.3 1.0 %copy-start = (bf16[512,512]{1,0:T(8,128)(2,1)S(1)}, bf16[512,512]{1,0:T(8,128)(2,1)}, u32[]{:S(2)}) copy-start(bf16[512,512]{1,0:T(8,128)(2,1)} %constant.4.clone.th_ref) | copy-start | bytes 1572868
  2.4 1.0 %copy-start.2 = (bf16[512,512]{1,0:T(8,128)(2,1)S(1)}, bf16[512,512]{1,0:T(8,128)(2,1)}, u32[]{:S(2)}) copy-start(bf16[512,512]{1,0:T(8,128)(2,1)} %constant.5.clone.tl_ref) | copy-start | bytes 1572868
  3.4 1.1 %copy-start.4 = (f32[6,2,1,64,256]{4,3,2,1,0:T(8,128)S(1)}, f32[6,2,1,64,256]{4,3,2,1,0:T(8,128)}, u32[]{:S(2)}) copy-start(f32[6,2,1,64,256]{4,3,2,1,0:T(8,128)} %param.21) | copy-start | bytes 2359300
  4.5 1.1 %copy-start.6 = (f32[6,2,1,64,256]{4,3,2,1,0:T(8,128)S(1)}, f32[6,2,1,64,256]{4,3,2,1,0:T(8,128)}, u32[]{:S(2)}) copy-start(f32[6,2,1,64,256]{4,3,2,1,0:T(8,128)} %param.22) | copy-start | bytes 2359300
  5.7 1.0 %copy-start.8 = (f32[3,2,1,64,256]{4,3,2,1,0:T(8,128)S(1)}, f32[3,2,1,64,256]{4,3,2,1,0:T(8,128)}, u32[]{:S(2)}) copy-start(f32[3,2,1,64,256]{4,3,2,1,0:T(8,128)} %param.19) | copy-start | bytes 1179652
  6.7 1.0 %copy-start.10 = (f32[3,2,1,64,256]{4,3,2,1,0:T(8,128)S(1)}, f32[3,2,1,64,256]{4,3,2,1,0:T(8,128)}, u32[]{:S(2)}) copy-start(f32[3,2,1,64,256]{4,3,2,1,0:T(8,128)} %param.20) | copy-start | bytes 1179652
  7.7 1.0 %copy-start.12 = (f32[2,1,3,64,256]{4,3,2,1,0:T(8,128)S(1)}, f32[2,1,3,64,256]{4,3,2,1,0:T(8,128)}, u32[]{:S(2)}) copy-start(f32[2,1,3,64,256]{4,3,2,1,0:T(8,128)} %param.18) | copy-start | bytes 1179652
  8.7 1.1 %copy-start.5 = (f32[6,2,1,64,256]{4,3,2,1,0:T(8,128)S(1)}, f32[6,2,1,64,256]{4,3,2,1,0:T(8,128)}, u32[]{:S(2)}) copy-start(f32[6,2,1,64,256]{4,3,2,1,0:T(8,128)} %param.21) | copy-start | bytes 2359300
  8.7 1.4 %copy-start.7 = (f32[6,2,1,64,256]{4,3,2,1,0:T(8,128)S(1)}, f32[6,2,1,64,256]{4,3,2,1,0:T(8,128)}, u32[]{:S(2)}) copy-start(f32[6,2,1,64,256]{4,3,2,1,0:T(8,128)} %param.22) | copy-start | bytes 2359300
  8.7 1.5 %copy-start.13 = (f32[3,2,1,64,256]{4,3,2,1,0:T(8,128)S(1)}, f32[3,2,1,64,256]{4,3,2,1,0:T(8,128)}, u32[]{:S(2)}) copy-start(f32[3,2,1,64,256]{4,3,2,1,0:T(8,128)} %param.16) | copy-start | bytes 1179652
  8.7 1.6 %copy-start.14 = (f32[3,2,1,64,256]{4,3,2,1,0:T(8,128)S(1)}, f32[3,2,1,64,256]{4,3,2,1,0:T(8,128)}, u32[]{:S(2)}) copy-start(f32[3,2,1,64,256]{4,3,2,1,0:T(8,128)} %param.17) | copy-start | bytes 1179652
  8.7 1.6 %copy-start.16 = (f32[2,1,64,256]{3,2,1,0:T(8,128)S(1)}, f32[2,1,64,256]{3,2,1,0:T(8,128)}, u32[]{:S(2)}) copy-start(f32[2,1,64,256]{3,2,1,0:T(8,128)} %param.14) | copy-start | bytes 393220
  8.7 1.6 %copy-start.17 = (f32[2,1,64,256]{3,2,1,0:T(8,128)S(1)}, f32[2,1,64,256]{3,2,1,0:T(8,128)}, u32[]{:S(2)}) copy-start(f32[2,1,64,256]{3,2,1,0:T(8,128)} %param.15) | copy-start | bytes 393220
  10.3 16.0 %copy-start.1 = (bf16[512,512]{1,0:T(8,128)(2,1)S(1)}, bf16[512,512]{1,0:T(8,128)(2,1)}, u32[]{:S(2)}) copy-start(bf16[512,512]{1,0:T(8,128)(2,1)} %constant.4.clone.th_ref) | copy-start | bytes 1572868
  10.3 16.0 %copy-start.3 = (bf16[512,512]{1,0:T(8,128)(2,1)S(1)}, bf16[512,512]{1,0:T(8,128)(2,1)}, u32[]{:S(2)}) copy-start(bf16[512,512]{1,0:T(8,128)(2,1)} %constant.5.clone.tl_ref) | copy-start | bytes 1572868
  10.3 16.0 %copy-start.15 = (f32[2,3,64,256]{3,2,1,0:T(8,128)S(1)}, f32[2,3,64,256]{3,2,1,0:T(8,128)}, u32[]{:S(2)}) copy-start(f32[2,3,64,256]{3,2,1,0:T(8,128)} %param.24) | copy-start | bytes 1179652
  11.3 35.4 %collective-permute-start = (f32[16,64,256]{2,1,0:T(8,128)S(1)}, f32[16,64,256]{2,1,0:T(8,128)S(1)}, u32[]{:S(2)}, u32[]{:S(2)}) collective-permute-start(f32[16,64,256]{2,1,0:T(8,128)S(1)} %get-tuple-element.30), channel_id=1, source_target_pairs={{0,16},{16,32},{32,48},{48,64},{64,80},{80,96},{96,112},{112,128},... | collective-permute-start | bytes 3145736 | tf_op jit(solution)/shard_map/ppermute | solution.py:396
  13.2 48.7 %collective-permute-start.1 = (f32[16,64,256]{2,1,0:T(8,128)S(1)}, f32[16,64,256]{2,1,0:T(8,128)S(1)}, u32[]{:S(2)}, u32[]{:S(2)}) collective-permute-start(f32[16,64,256]{2,1,0:T(8,128)S(1)} %get-tuple-element.29.w), channel_id=1, source_target_pairs={{16,0},{17,1},{18,2},{19,3},{32,17},{33,18},{34,19},{35,16},{48,32... | collective-permute-start | bytes 3145736 | tf_op jit(solution)/shard_map/ppermute | solution.py:403
  16.0 10.3 %collective-permute-start.2 = (f32[80,384]{1,0:T(8,128)S(1)}, f32[80,384]{1,0:T(8,128)S(1)}, u32[]{:S(2)}, u32[]{:S(2)}) collective-permute-start(f32[80,384]{1,0:T(8,128)S(1)} %get-tuple-element.31), channel_id=1, source_target_pairs={{0,4},{4,8},{8,12},{12,0},{1,5},{5,9},{9,13},{13,1},{2,6},{6,10},{... | collective-permute-start | bytes 368648 | tf_op jit(solution)/shard_map/ppermute | solution.py:368
  17.6 8.8 %collective-permute-start.3 = (f32[64,384]{1,0:T(8,128)S(1)}, f32[64,384]{1,0:T(8,128)S(1)}, u32[]{:S(2)}, u32[]{:S(2)}) collective-permute-start(f32[64,384]{1,0:T(8,128)S(1)} %get-tuple-element.32), channel_id=1, source_target_pairs={{0,8},{4,12},{8,0},{12,4},{1,9},{5,13},{9,1},{13,5},{2,10},{6,14},... | collective-permute-start | bytes 294920 | tf_op jit(solution)/shard_map/ppermute | solution.py:368
  20.3 6.0 %collective-permute-start.4 = (f32[64,384]{1,0:T(8,128)S(1)}, f32[64,384]{1,0:T(8,128)S(1)}, u32[]{:S(2)}, u32[]{:S(2)}) collective-permute-start(f32[64,384]{1,0:T(8,128)S(1)} %get-tuple-element.33), channel_id=1, source_target_pairs={{0,12},{4,0},{8,4},{12,8},{1,13},{5,1},{9,5},{13,9},{2,14},{6,2},{... | collective-permute-start | bytes 294920 | tf_op jit(solution)/shard_map/ppermute | solution.py:368
  26.9 8.0 %collective-permute-start.5 = (f32[2,64,256]{2,1,0:T(8,128)S(1)}, f32[2,64,256]{2,1,0:T(8,128)S(1)}, u32[]{:S(2)}, u32[]{:S(2)}) collective-permute-start(f32[2,64,256]{2,1,0:T(8,128)S(1)} %shard_map.207), channel_id=1, source_target_pairs={{0,1},{1,0},{2,3},{3,2},{4,5},{5,4},{6,7},{7,6},{8,9},{9,8},{10,11... | collective-permute-start | bytes 393224 | tf_op jit(solution)/shard_map/ppermute | solution.py:407
  34.9 25.7 %copy-start.18 = (f32[2,1,3,64,256]{4,3,2,1,0:T(8,128)S(1)}, f32[2,1,3,64,256]{4,3,2,1,0:T(8,128)}, u32[]{:S(2)}) copy-start(f32[2,1,3,64,256]{4,3,2,1,0:T(8,128)} %param.23) | copy-start | bytes 1179652
  34.9 11.8 %collective-permute-start.6 = (f32[2,64,256]{2,1,0:T(8,128)S(1)}, f32[2,64,256]{2,1,0:T(8,128)S(1)}, u32[]{:S(2)}, u32[]{:S(2)}) collective-permute-start(f32[2,64,256]{2,1,0:T(8,128)S(1)} %add.3.sum_a), channel_id=1, source_target_pairs={{0,3},{3,0},{1,2},{2,1},{4,7},{7,4},{5,6},{6,5},{8,11},{11,8},{9,1... | collective-permute-start | bytes 393224 | tf_op jit(solution)/shard_map/ppermute | solution.py:408
  47.3 13.2 %collective-permute-start.8 = (f32[80,384]{1,0:T(8,128)S(1)}, f32[80,384]{1,0:T(8,128)S(1)}, u32[]{:S(2)}, u32[]{:S(2)}) collective-permute-start(f32[80,384]{1,0:T(8,128)S(1)} %get-tuple-element.35), channel_id=1, source_target_pairs={{0,12},{4,0},{8,4},{12,8},{1,13},{5,1},{9,5},{13,9},{2,14},{6,2},{... | collective-permute-start | bytes 368648 | tf_op jit(solution)/shard_map/ppermute | solution.py:368
  50.1 11.8 %collective-permute-start.7 = (f32[144,256]{1,0:T(8,128)S(1)}, f32[144,256]{1,0:T(8,128)S(1)}, u32[]{:S(2)}, u32[]{:S(2)}) collective-permute-start(f32[144,256]{1,0:T(8,128)S(1)} %get-tuple-element.34.z), channel_id=1, source_target_pairs={{16,0},{32,16},{48,32},{64,48},{80,64},{96,80},{112,96},{128,112},... | collective-permute-start | bytes 442376 | tf_op jit(solution)/shard_map/ppermute | solution.py:415
  52.0 8.6 %collective-permute-start.9 = (f32[64,384]{1,0:T(8,128)S(1)}, f32[64,384]{1,0:T(8,128)S(1)}, u32[]{:S(2)}, u32[]{:S(2)}) collective-permute-start(f32[64,384]{1,0:T(8,128)S(1)} %get-tuple-element.41), channel_id=1, source_target_pairs={{0,4},{4,8},{8,12},{12,0},{1,5},{5,9},{9,13},{13,1},{2,6},{6,10},{... | collective-permute-start | bytes 294920 | tf_op jit(solution)/shard_map/ppermute | solution.py:368
  52.1 8.5 %collective-permute-start.10 = (f32[64,384]{1,0:T(8,128)S(1)}, f32[64,384]{1,0:T(8,128)S(1)}, u32[]{:S(2)}, u32[]{:S(2)}) collective-permute-start(f32[64,384]{1,0:T(8,128)S(1)} %get-tuple-element.42), channel_id=1, source_target_pairs={{0,8},{4,12},{8,0},{12,4},{1,9},{5,13},{9,1},{13,5},{2,10},{6,14},... | collective-permute-start | bytes 294920 | tf_op jit(solution)/shard_map/ppermute | solution.py:368
  60.6 1.3 %copy-start.9 = (f32[3,2,1,64,256]{4,3,2,1,0:T(8,128)S(1)}, f32[3,2,1,64,256]{4,3,2,1,0:T(8,128)}, u32[]{:S(2)}) copy-start(f32[3,2,1,64,256]{4,3,2,1,0:T(8,128)} %param.19) | copy-start | bytes 1179652
  60.6 1.3 %copy-start.11 = (f32[3,2,1,64,256]{4,3,2,1,0:T(8,128)S(1)}, f32[3,2,1,64,256]{4,3,2,1,0:T(8,128)}, u32[]{:S(2)}) copy-start(f32[3,2,1,64,256]{4,3,2,1,0:T(8,128)} %param.20) | copy-start | bytes 1179652

commit v2 on v1

v2 whole, which is shorter than its diff:
```python
import functools
import math

import jax
import jax.numpy as jnp
import ml_dtypes
import numpy as np
from jax import lax
from jax.experimental import pallas as pl
from jax.experimental.pallas import tpu as pltpu
from jax.sharding import PartitionSpec as P

TAU = 0.25
SIGMA = 0.25
LAMBDA_DATA = 2.0
ALPHA_ONE = 2.0
ALPHA_ZERO = 1.2
BETA_ONE = 2.0
BETA_TWO = 0.5

LENGTH = 256
COIL = 3
BLOCK = 64
ROWS = 4
F32 = jnp.float32
BF16 = jnp.bfloat16
LIMIT = 12 * 1024 * 1024


def halves(table):
    high = table.astype(ml_dtypes.bfloat16)
    return high, (table - high.astype(np.float64)).astype(ml_dtypes.bfloat16)


def dft_tables():
    positions = np.arange(LENGTH)
    angles = (positions[:, None] * positions[None, :] % LENGTH) * (2.0 * math.pi / LENGTH)
    real = np.cos(angles) / math.sqrt(LENGTH)
    imag = np.sin(angles) / math.sqrt(LENGTH)
    of_real = np.concatenate([real, imag], axis=1).reshape(ROWS, 1, BLOCK, 2 * LENGTH)
    of_imag = np.concatenate([-imag, real], axis=1).reshape(ROWS, 1, BLOCK, 2 * LENGTH)
    table = np.concatenate([of_real, of_imag], axis=1).reshape(2 * LENGTH, 2 * LENGTH)
    return halves(of_real.reshape(LENGTH, 2 * LENGTH)) + halves(table)


def split(values):
    high = values.astype(BF16)
    return high, (values - high.astype(F32)).astype(BF16)


def dot_nt(a, b):
    return lax.dot_general(a, b, (((1,), (1,)), ((), ())), preferred_element_type=F32)


def dot_nn(a, b):
    return lax.dot_general(a, b, (((1,), (0,)), ((), ())), preferred_element_type=F32)


def first_transform(table_high, table_low, right, row):
    def blocks(ref):
        return jnp.concatenate(
            [ref[pl.ds(pl.multiple_of(lax.rem(row + d, ROWS) * BLOCK, BLOCK), BLOCK), :] for d in range(ROWS)], axis=0
        )

    high, low = split(right)
    left_high = blocks(table_high)
    return dot_nt(left_high, high) + (dot_nt(left_high, low) + dot_nt(blocks(table_low), high))


def second_transform(table_high, table_low, received, row):
    def blocks(ref):
        return jnp.concatenate(
            [ref[pl.ds(pl.multiple_of(lax.rem(row + ROWS - d, ROWS) * 128, 128), 128), :] for d in range(ROWS)], axis=0
        )

    left = jnp.concatenate(
        [
            jnp.concatenate([block[:BLOCK, 128 * c : 128 * (c + 1)] for block in received], axis=1)
            for c in range(COIL)
        ],
        axis=0,
    )
    high, low = split(left)
    right_high = blocks(table_high)
    return dot_nn(high, right_high) + (dot_nn(low, right_high) + dot_nn(high, blocks(table_low)))


def iota(shape, dimension):
    return lax.broadcasted_iota(jnp.int32, shape, dimension)


ROW_PARTS = (("g1", 1), ("g2", 1), ("s1", 1), ("s1", 3), ("s1", 5), ("s2", 1), ("s2", 3), ("s2", 5))
TIME_PARTS = (("g1", 0), ("g2", 0), ("s1", 0), ("s1", 3), ("s1", 4), ("s2", 0), ("s2", 3), ("s2", 4))


def start_kernel(
    kd_hbm, lines_hbm, th_hbm, tl_hbm, g1, g2, s1, s2, o0, o1, o2, o3,
    kd_ref, lines_ref, th_ref, tl_ref, ends, sems
):
    row = lax.axis_index("row")
    copies = [
        pltpu.make_async_copy(source, target, sems.at[k])
        for k, (source, target) in enumerate(
            ((kd_hbm, kd_ref), (lines_hbm, lines_ref), (th_hbm, th_ref), (tl_hbm, tl_ref))
        )
    ]
    refs = dict(g1=g1, g2=g2, s1=s1, s2=s2)
    for index, (name, part) in enumerate(ROW_PARTS):
        copies.append(
            pltpu.make_async_copy(
                refs[name].at[2 * part : 2 * part + 2, BLOCK - 8 : BLOCK, :],
                ends.at[2 * index : 2 * index + 2],
                sems.at[4 + index],
            )
        )
    for copy in copies:
        copy.start()
    for copy in copies[:4]:
        copy.wait()
    mask = lines_ref[...].astype(F32)
    parts = []
    for c in range(COIL):
        real = kd_ref[c] * mask
        imag = kd_ref[COIL + c] * mask
        parts.append(jnp.concatenate([real, -imag], axis=1))
        parts.append(jnp.concatenate([imag, real], axis=1))
    out = first_transform(th_ref, tl_ref, jnp.concatenate(parts, axis=0), row)
    for d, ref in enumerate((o0, o1, o2, o3)):
        ref[0:BLOCK, :] = out[BLOCK * d : BLOCK * (d + 1)]
    for copy in copies[4:]:
        copy.wait()
    o1[BLOCK:, LENGTH:] = jnp.zeros((16, 128), F32)
    for plane in range(16):
        o1[BLOCK + plane : BLOCK + plane + 1, 0:LENGTH] = ends[plane, 7:8, :]


def chunk(ref, plane, i):
    return ref[plane, pl.ds(i * 8 if isinstance(i, int) else pl.multiple_of(i * 8, 8), 8), :]


def pack_kernel(g1, g2, s1, s2, order, q_first, q_out):
    refs = dict(g1=g1, g2=g2, s1=s1, s2=s2)
    for reim in range(2):
        q_first[BLOCK * reim : BLOCK * (reim + 1), :] = g1[reim]
        tops = [refs[name][2 * part + reim, 0:1, :] for name, part in TIME_PARTS]
        for field in range(8):
            place = 2 * BLOCK + 2 * field + reim
            q_first[place : place + 1, :] = time_term(lambda k: tops[k], field)
        for index, (name, part) in enumerate(TIME_PARTS[1:]):
            q_out[2 * index + reim] = refs[name][2 * part + reim]


def plain_kernel(img, spl, v1, v2, g1, g2, s1, s2, b1, order, w_out, w_top):
    row = lax.axis_index("row")
    keep_time = (lax.axis_index("tm") != lax.axis_size("tm") - 1).astype(F32)
    refs = dict(g1=g1, g2=g2, s1=s1, s2=s2)
    edge = jnp.where(row == 0, 0.0, b1[BLOCK:, 0:LENGTH])
    where = {part: 2 * index for index, part in enumerate(ROW_PARTS)}

    def step(i, carry):
        rows = iota((8, LENGTH), 0)
        cols = iota((8, LENGTH), 1)
        drop_row = (rows == 7) & (i == 7) & (row == ROWS - 1)

        def adj_rows(name, plane):
            ref = refs[name]
            here = chunk(ref, plane, i)
            above = chunk(ref, plane, jnp.maximum(i - 1, 0))
            at = where[name, plane // 2] + plane % 2
            above = jnp.where(i == 0, edge[at : at + 1], above)
            behind = jnp.where(rows == 0, pltpu.roll(above, 1, 0), pltpu.roll(here, 1, 0))
            return behind - jnp.where(drop_row, 0.0, here)

        def adj_cols(ref, plane):
            here = chunk(ref, plane, i)
            behind = jnp.where(cols == 0, 0.0, pltpu.roll(here, 1, 1))
            return behind - jnp.where(cols == LENGTH - 1, 0.0, here)

        def put(ref, plane, value):
            ref[plane, pl.ds(pl.multiple_of(i * 8, 8), 8), :] = value

        for reim in range(2):
            z, y, x = reim, 2 + reim, 4 + reim
            one = -BETA_ONE * keep_time * chunk(g1, z, i) + adj_rows("g1", y) + adj_cols(g1, x)
            two = -BETA_TWO * keep_time * chunk(g2, z, i) + adj_rows("g2", y) + adj_cols(g2, x)
            image = chunk(img, reim, i) - 2.0 * TAU * one
            other = chunk(spl, reim, i) - 2.0 * TAU * (two - one)
            put(w_out, reim, image - other)
            put(w_out, 2 + reim, other)
            for base, vec, grad, name, beta in ((4, v1, g1, "s1", BETA_ONE), (10, v2, g2, "s2", BETA_TWO)):
                sym = refs[name]
                p0, p1, p2, p3, p4, p5 = (2 * k + reim for k in range(6))
                first = -beta * keep_time * chunk(sym, p0, i) + 0.5 * (adj_rows(name, p3) + adj_cols(sym, p4))
                second = adj_rows(name, p1) - 0.5 * beta * keep_time * chunk(sym, p3, i) + 0.5 * adj_cols(sym, p5)
                third = adj_cols(sym, p2) - 0.5 * beta * keep_time * chunk(sym, p4, i) + 0.5 * adj_rows(name, p5)
                for k, adjoint in enumerate((first, second, third)):
                    value = chunk(vec, 2 * k + reim, i) - 2.0 * TAU * (adjoint - chunk(grad, 2 * k + reim, i))
                    put(w_out, base + 2 * k + reim, value)
        return carry

    lax.fori_loop(0, 8, step, 0)
    for plane in range(16):
        w_top[plane : plane + 1, :] = w_out[plane, 0:1, :]


def combine_kernel(b0, b1, b2, b3, th_ref, tl_ref, sens, out):
    row = lax.axis_index("row")
    both = second_transform(th_ref, tl_ref, (b0, b1, b2, b3), row)
    real_sum = None
    for c in range(COIL):
        real = both[BLOCK * c : BLOCK * (c + 1), :LENGTH]
        imag = both[BLOCK * c : BLOCK * (c + 1), LENGTH:]
        real_term = sens[c] * real + sens[COIL + c] * imag
        imag_term = sens[c] * imag - sens[COIL + c] * real
        real_sum = real_term if real_sum is None else real_sum + real_term
        imag_sum = imag_term if c == 0 else imag_sum + imag_term
    out[0] = real_sum
    out[1] = imag_sum


def time_term(q, field):
    if field == 0:
        return -2.0 * TAU * (2.0 * BETA_ONE * q(0) - BETA_TWO * q(1))
    if field == 1:
        return -2.0 * TAU * (BETA_TWO * q(1) - BETA_ONE * q(0))
    beta = BETA_ONE if field < 5 else BETA_TWO
    return (-2.0 * TAU * beta * (1.0 if field in (2, 5) else 0.5)) * q(field)


def predict_kernel(sum_a, sum_b, w, w_top, q_first, th_ref, tl_ref, sens, o0, o1, o2, o3, z_out, q0_out):
    row = lax.axis_index("row")
    image = []
    for reim in range(2):
        back = sum_a[reim] + sum_b[reim]
        z_out[reim] = back
        before = q_first[BLOCK * reim : BLOCK * (reim + 1), :]
        q0_out[reim] = before
        image.append(w[reim] + w[2 + reim] - 2.0 * TAU * BETA_ONE * before - 2.0 * TAU * back)
    parts = []
    for c in range(COIL):
        real = sens[c] * image[0] - sens[COIL + c] * image[1]
        imag = sens[c] * image[1] + sens[COIL + c] * image[0]
        parts.append(jnp.concatenate([real, imag], axis=1))
        parts.append(jnp.concatenate([-imag, real], axis=1))
    out = first_transform(th_ref, tl_ref, jnp.concatenate(parts, axis=0), row)
    for d, ref in enumerate((o0, o1, o2, o3)):
        ref[0:BLOCK, :] = out[BLOCK * d : BLOCK * (d + 1)]
    o3[BLOCK:, LENGTH:] = jnp.zeros((16, 128), F32)
    o3[BLOCK:, 0:LENGTH] = w_top[...] + q_first[2 * BLOCK :, :]
    for reim in range(2):
        o3[BLOCK + reim : BLOCK + reim + 1, 0:LENGTH] -= 2.0 * TAU * (sum_a[reim, 0:1, :] + sum_b[reim, 0:1, :])


def finish_kernel(b0, b1, b2, b3, th_ref, tl_ref, kd_ref, measured, lines_hbm, out_hbm, lines_ref, out, sems):
    row = lax.axis_index("row")
    lines = pltpu.make_async_copy(lines_hbm, lines_ref, sems.at[0])
    lines.start()
    both = second_transform(th_ref, tl_ref, (b0, b1, b2, b3), row)
    lines.wait()
    mask = SIGMA * lines_ref[...].astype(F32)
    scale = 1.0 / (1.0 + SIGMA / LAMBDA_DATA)
    copies = []
    for c in range(COIL):
        real = both[BLOCK * c : BLOCK * (c + 1), :LENGTH]
        imag = -both[BLOCK * c : BLOCK * (c + 1), LENGTH:]
        for plane, value in ((c, real), (COIL + c, imag)):
            out[plane] = (kd_ref[plane] + mask * (value - measured[plane])) * scale
            copies.append(pltpu.make_async_copy(out.at[plane], out_hbm.at[plane], sems.at[1 + plane]))
            copies[-1].start()
    for copy in copies:
        copy.wait()


def fields_kernel(
    img, spl, v1, v2, g1, g2, s1, s2, w, q0, q_in, w_in, z, z_in, n3,
    img_hbm, spl_hbm, v1_hbm, v2_hbm, g1_hbm, g2_hbm, s1_hbm, s2_hbm,
    bar, img_out, spl_out, v1_out, v2_out, g1_out, g2_out, s1_out, s2_out, sems,
):
    row = lax.axis_index("row")
    keep_time = (lax.axis_index("tm") != lax.axis_size("tm") - 1).astype(F32)
    refs = dict(g1=g1, g2=g2, s1=s1, s2=s2)
    copies = [
        pltpu.make_async_copy(source, target, sems.at[k])
        for k, (source, target) in enumerate(
            ((img_out, img_hbm), (spl_out, spl_hbm), (v1_out, v1_hbm), (v2_out, v2_hbm))
        )
    ]

    def span(i):
        return pl.ds(i * 8 if isinstance(i, int) else pl.multiple_of(i * 8, 8), 8)

    def first(i, carry):
        for reim in range(2):

            def before(k):
                if k == 0:
                    return chunk(q0, reim, i)
                return chunk(q_in, 2 * (k - 1) + reim, i)

            values = []
            for field in range(8):
                plane = 2 * field + reim
                value = chunk(w, plane, i) + time_term(before, field)
                if field == 0:
                    value -= 2.0 * TAU * chunk(z, reim, i)
                bar[plane, span(i), :] = value
                values.append(value)
            img_out[reim, span(i), :] = 0.5 * (values[0] + values[1] + chunk(img, reim, i))
            spl_out[reim, span(i), :] = 0.5 * (values[1] + chunk(spl, reim, i))
            for k in range(3):
                plane = 2 * k + reim
                v1_out[plane, span(i), :] = 0.5 * (values[2 + k] + chunk(v1, plane, i))
                v2_out[plane, span(i), :] = 0.5 * (values[5 + k] + chunk(v2, plane, i))
        return carry

    lax.fori_loop(0, 8, first, 0, unroll=2)
    for copy in copies:
        copy.start()
    for plane in range(16):
        below = n3[BLOCK + plane : BLOCK + plane + 1, 0:LENGTH]
        bar[plane, BLOCK : BLOCK + 1, :] = jnp.where(row == ROWS - 1, bar[plane, BLOCK - 1 : BLOCK, :], below)

    def along_rows(plane, i):
        here = chunk(bar, plane, i)
        below = chunk(bar, plane, i + 1)
        rows = iota((8, LENGTH), 0)
        return jnp.where(rows == 7, pltpu.roll(below, 7, 0), pltpu.roll(here, 7, 0)) - here

    def along_cols(plane, i):
        here = chunk(bar, plane, i)
        cols = iota((8, LENGTH), 1)
        return jnp.where(cols == LENGTH - 1, 0.0, pltpu.roll(here, LENGTH - 1, 1) - here)

    def along_time(field, reim, i):
        plane = 2 * field + reim
        value = chunk(w_in, plane, i)
        value += time_term(lambda k: chunk(refs[TIME_PARTS[k][0]], 2 * TIME_PARTS[k][1] + reim, i), field)
        if field == 0:
            value -= 2.0 * TAU * chunk(z_in, reim, i)
        return value - chunk(bar, plane, i)

    def project(out, duals, radius, i):
        total = duals[0] * duals[0]
        for value in duals[1:]:
            total += value * value
        scale = jnp.minimum(1.0, radius * lax.rsqrt(total))
        for plane, value in enumerate(duals):
            out[plane, span(i), :] = value * scale

    def gradient(i, dual, out, field, vec, beta):
        duals = []
        for k in range(3):
            for reim in range(2):
                if k == 0:
                    diff = (beta * keep_time) * along_time(field, reim, i)
                else:
                    diff = (along_rows, along_cols)[k - 1](2 * field + reim, i)
                diff -= chunk(bar, 2 * (vec + k) + reim, i)
                duals.append(chunk(dual, 2 * k + reim, i) + SIGMA * diff)
        project(out, duals, ALPHA_ONE, i)

    def symmetric(i, dual, out, vec, beta):
        duals = [None] * 12
        for reim in range(2):
            p0, p1, p2 = (2 * (vec + k) + reim for k in range(3))
            steps = (
                (SIGMA * beta * keep_time) * along_time(vec, reim, i),
                SIGMA * along_rows(p1, i),
                SIGMA * along_cols(p2, i),
                0.5 * SIGMA * along_rows(p0, i) + (0.5 * SIGMA * beta * keep_time) * along_time(vec + 1, reim, i),
                0.5 * SIGMA * along_cols(p0, i) + (0.5 * SIGMA * beta * keep_time) * along_time(vec + 2, reim, i),
                0.5 * SIGMA * (along_cols(p1, i) + along_rows(p2, i)),
            )
            for k, diff in enumerate(steps):
                duals[2 * k + reim] = chunk(dual, 2 * k + reim, i) + diff
        project(out, duals, ALPHA_ZERO, i)

    def second(i):
        gradient(i, g1, g1_out, 0, 2, BETA_ONE)
        gradient(i, g2, g2_out, 1, 5, BETA_TWO)
        symmetric(i, s1, s1_out, 2, BETA_ONE)
        symmetric(i, s2, s2_out, 5, BETA_TWO)

    for part in range(4):
        rows = pl.ds(16 * part, 16)
        second(2 * part)
        second(2 * part + 1)
        for k, (source, target) in enumerate(((g1_out, g1_hbm), (g2_out, g2_hbm), (s1_out, s1_hbm), (s2_out, s2_hbm))):
            copy = pltpu.make_async_copy(source.at[:, rows, :], target.at[:, rows, :], sems.at[4 + 4 * part + k])
            copy.start()
            copies.append(copy)
    for copy in copies:
        copy.wait()


def shape(*dims):
    return jax.ShapeDtypeStruct(dims, F32)


def call(kernel, outs, ins, cost, in_specs=None, scratch=(), out_space=pltpu.VMEM):
    return pl.pallas_call(
        kernel,
        out_shape=outs,
        in_specs=in_specs or [pl.BlockSpec(memory_space=pltpu.VMEM)] * len(ins),
        out_specs=[pl.BlockSpec(memory_space=out_space)] * len(outs),
        scratch_shapes=list(scratch),
        compiler_params=pltpu.CompilerParams(vmem_limit_bytes=LIMIT),
        cost_estimate=pl.CostEstimate(flops=500 * cost, bytes_accessed=cost, transcendentals=0),
    )(*ins)


def turn(block, distance):
    return lax.ppermute(block, "row", [(i, (i + distance) % ROWS) for i in range(ROWS)])


def body(
    image_now, split_now, vector_one, vector_two, kspace_dual, grad_one, grad_two, sym_one, sym_two,
    measured, sensitivity, sampled,
):
    planes = lambda x: x.reshape(-1, BLOCK, LENGTH)
    img, spl, v1, v2, kd = map(planes, (image_now, split_now, vector_one, vector_two, kspace_dual))
    g1, g2, s1, s2, meas, sens = map(planes, (grad_one, grad_two, sym_one, sym_two, measured, sensitivity))
    first_high, first_low, high, low = map(jnp.asarray, dft_tables())
    frames = lax.axis_size("tm")
    groups = lax.axis_size("coil")
    blocks = (shape(BLOCK, 384), shape(BLOCK + 16, 384), shape(BLOCK, 384), shape(BLOCK, 384))
    hbm = pl.BlockSpec(memory_space=pltpu.HBM)
    a0, a1, a2, a3 = call(
        start_kernel, blocks,
        [pltpu.with_memory_space_constraint(x, pltpu.HBM) for x in (kd, sampled, first_high, first_low, g1, g2, s1, s2)],
        1,
        in_specs=[hbm] * 8,
        scratch=[
            pltpu.VMEM((2 * COIL, BLOCK, LENGTH), F32), pltpu.VMEM((1, LENGTH), jnp.int32),
            pltpu.VMEM((LENGTH, 2 * LENGTH), BF16), pltpu.VMEM((LENGTH, 2 * LENGTH), BF16),
            pltpu.VMEM((16, 8, LENGTH), F32), pltpu.SemaphoreType.DMA((12,)),
        ],
    )
    b2, b1, b3 = turn(a2, 2), turn(a1, 1), turn(a3, 3)
    after = [(i, i + 1) for i in range(frames - 1)]
    q_first, q_out = call(
        pack_kernel, (shape(2 * BLOCK + 16, LENGTH), shape(14, BLOCK, LENGTH)), (g1, g2, s1, s2, a0), 100_000_000,
        in_specs=[pl.BlockSpec(memory_space=pltpu.VMEM)] * 4 + [pl.BlockSpec(memory_space=pl.ANY)],
    )
    q_first = lax.ppermute(q_first, "tm", after)
    (partial,) = call(combine_kernel, (shape(2, BLOCK, LENGTH),), (a0, b1, b2, b3, high, low, sens), 200_000_000)
    partner = ((1, 0, 3, 2), (3, 2, 1, 0))
    swaps = [
        [(t * groups + c, t * groups + partner[(t + turn) % 2][c]) for t in range(frames) for c in range(groups)]
        for turn in range(2)
    ]
    w_out, w_top = call(
        plain_kernel, (shape(16, BLOCK, LENGTH), shape(16, LENGTH)),
        (img, spl, v1, v2, g1, g2, s1, s2, b1, partial), 100_000_000,
        in_specs=[pl.BlockSpec(memory_space=pltpu.VMEM)] * 9 + [pl.BlockSpec(memory_space=pl.ANY)],
    )
    pairs = []
    for t in range(1, frames):
        for c in range(groups):
            to = c if t % 2 else ((c + 1) % groups if t % 4 == 2 else (c - 1) % groups)
            pairs.append((t * groups + c, (t - 1) * groups + to))
    received = lax.ppermute(partial, ("tm", "coil"), swaps[0])
    partial, received, w_out = lax.optimization_barrier((partial, received, w_out))
    pair = partial + received
    rest = lax.ppermute(pair, ("tm", "coil"), swaps[1])
    q_in = lax.ppermute(q_out, "tm", after)
    w_in = lax.ppermute(w_out, ("tm", "coil"), pairs)
    c_blocks = (shape(BLOCK, 384), shape(BLOCK, 384), shape(BLOCK, 384), shape(BLOCK + 16, 384))
    c0, c1, c2, c3, z, q0 = call(
        predict_kernel, (*c_blocks, shape(2, BLOCK, LENGTH), shape(2, BLOCK, LENGTH)),
        (pair, rest, w_out, w_top, q_first, first_high, first_low, sens), 200_000_000,
    )
    n2, n1, n3 = turn(c2, 2), turn(c1, 1), turn(c3, 3)
    z_in = lax.ppermute(z, "tm", [(i + 1, i) for i in range(frames - 1)])
    like = lambda x: shape(*x.shape)
    fields = call(
        fields_kernel, tuple(map(like, (img, spl, v1, v2, g1, g2, s1, s2))),
        (img, spl, v1, v2, g1, g2, s1, s2, w_out, q0, q_in, w_in, z, z_in, n3), 1,
        scratch=[
            pltpu.VMEM((16, BLOCK + 8, LENGTH), F32),
            *(pltpu.VMEM(x.shape, F32) for x in (img, spl, v1, v2, g1, g2, s1, s2)),
            pltpu.SemaphoreType.DMA((20,)),
        ],
        out_space=pltpu.HBM,
    )
    vmem = pl.BlockSpec(memory_space=pltpu.VMEM)
    (kspace,) = call(
        finish_kernel, (like(kd),),
        (c0, n1, n2, n3, high, low, kd, meas, pltpu.with_memory_space_constraint(sampled, pltpu.HBM)), 4_000_000,
        in_specs=[vmem] * 8 + [hbm],
        scratch=[
            pltpu.VMEM((1, LENGTH), jnp.int32), pltpu.VMEM(kd.shape, F32), pltpu.SemaphoreType.DMA((1 + 2 * COIL,)),
        ],
        out_space=pltpu.HBM,
    )
    img_new, spl_new, v1_new, v2_new, g1_new, g2_new, s1_new, s2_new = fields
    news = (img_new, spl_new, v1_new, v2_new, kspace, g1_new, g2_new, s1_new, s2_new)
    olds = (image_now, split_now, vector_one, vector_two, kspace_dual, grad_one, grad_two, sym_one, sym_two)
    return tuple(new.reshape(old.shape) for new, old in zip(news, olds))


def solution(mesh):
    image = P(None, "tm", "row", None)
    vector = P(None, None, "tm", "row", None)
    kspace = P(None, "tm", "coil", "row", None)
    return jax.shard_map(
        body,
        mesh=mesh,
        in_specs=(
            image, image, vector, vector, kspace, vector, vector, vector, vector, kspace,
            P(None, "coil", "row", None), P("tm", None),
        ),
        out_specs=(image, image, vector, vector, kspace, vector, vector, vector, vector),
        check_vma=False,
    )
```

time: 65.8 us -> 52.6 us (0.80)
  the two profiles are of different devices: /device:TPU:80 before, /device:TPU:1 now
where the time goes in v2:
time: 52.6 us; the launch traced here: 52.3 us
  starting transfers between devices  30.2 us (57%)
  waiting for transfers between devices  11.1 us (21%)
  Pallas kernels  9.86 us (19%)
  between operations  0.98 us (2%)
    pallas_call x7, Pallas kernels, call(): pl.pallas_call(kernel, out_shape=outs, in_specs=in_specs or [pl.BlockSpec...  9.86 us
    ppermute x6, starting transfers between devices, turn(): lax.ppermute(block, 'row', [(i, (i + distance) % ROWS) for i in range(ROW...  8.9 us
    ppermute x6, waiting for transfers between devices, turn(): lax.ppermute(block, 'row', [(i, (i + distance) % ROWS) for i in range(ROW...  6.14 us
    ppermute x1, starting transfers between devices, body(): q_in = lax.ppermute(q_out, 'tm', after)  6.03 us
    ppermute x1, starting transfers between devices, body(): received = lax.ppermute(partial, ('tm', 'coil'), swaps[0])  5.21 us
    ppermute x1, starting transfers between devices, body(): q_first = lax.ppermute(q_first, 'tm', after)  4.94 us
    ppermute x1, waiting for transfers between devices, body(): received = lax.ppermute(partial, ('tm', 'coil'), swaps[0])  2.5 us
    ppermute x1, waiting for transfers between devices, body(): z_in = lax.ppermute(z, 'tm', [(i + 1, i) for i in range(frames - 1)])  2.48 us
  transfers between devices with their start and end apart: 12, of which 3 were waited for; matrix products, arithmetic and copies ran while one was open for 0% of the time, Pallas kernels for 11%

profile of v2, /device:TPU:1, one launch (start us, length us, event | category | flops | bytes accessed | tf_op | source)
XLA Modules:
  0.0 52.3 jit_solution(7635857637221356390)
XLA Ops:
  0.7 2.0 %shard_map.223 = (f32[64,384]{1,0:T(8,128)S(1)}, f32[80,384]{1,0:T(8,128)S(1)}, f32[64,384]{1,0:T(8,128)S(1)}, f32[64,384]{1,0:T(8,128)S(1)}) custom-call(f32[6,64,256]{2,1,0:T(8,128)} %bitcast.54, s32[1,256]{1,0:T(1,128)} %lines_hbm.3, bf16[256,512]{1,0:T(8,128)(2,1)} %constant.8.clone.th_hbm.th_ref, bf16[256,512]{1,0:T(8,128)(2,1)} %constant.9.clone.tl_hbm.tl_ref, ...), custom_call_target="tpu_custom_call" | custom-call | flops 500 | bytes 1 | tf_op jit(solution)/shard_map/pallas_call | solution.py:401
  2.7 2.1 %collective-permute-start = (f32[80,384]{1,0:T(8,128)S(1)}, f32[80,384]{1,0:T(8,128)S(1)}, u32[]{:S(2)}, u32[]{:S(2)}) collective-permute-start(f32[80,384]{1,0:T(8,128)S(1)} %get-tuple-element.35), channel_id=1, source_target_pairs={{0,4},{4,8},{8,12},{12,0},{1,5},{5,9},{9,13},{13,1},{2,6},{6,10},{... | collective-permute-start | bytes 368648 | tf_op jit(solution)/shard_map/ppermute | solution.py:413
  4.9 2.4 %collective-permute-start.1 = (f32[64,384]{1,0:T(8,128)S(1)}, f32[64,384]{1,0:T(8,128)S(1)}, u32[]{:S(2)}, u32[]{:S(2)}) collective-permute-start(f32[64,384]{1,0:T(8,128)S(1)} %get-tuple-element.36), channel_id=1, source_target_pairs={{0,8},{4,12},{8,0},{12,4},{1,9},{5,13},{9,1},{13,5},{2,10},{6,14},... | collective-permute-start | bytes 294920 | tf_op jit(solution)/shard_map/ppermute | solution.py:413
  7.3 1.2 %collective-permute-start.2 = (f32[64,384]{1,0:T(8,128)S(1)}, f32[64,384]{1,0:T(8,128)S(1)}, u32[]{:S(2)}, u32[]{:S(2)}) collective-permute-start(f32[64,384]{1,0:T(8,128)S(1)} %get-tuple-element.37), channel_id=1, source_target_pairs={{0,12},{4,0},{8,4},{12,8},{1,13},{5,1},{9,5},{13,9},{2,14},{6,2},{... | collective-permute-start | bytes 294920 | tf_op jit(solution)/shard_map/ppermute | solution.py:413
  8.5 0.0 copy-start.11
  8.5 0.0 copy-start.13
  8.5 0.0 copy-start.15
  8.5 0.7 %shard_map.226 = (f32[144,256]{1,0:T(8,128)}, f32[14,64,256]{2,1,0:T(8,128)S(1)}) custom-call(f32[6,64,256]{2,1,0:T(8,128)S(1)} %bitcast.47, f32[6,64,256]{2,1,0:T(8,128)S(1)} %bitcast.51, f32[12,64,256]{2,1,0:T(8,128)S(1)} %bitcast.39, f32[12,64,256]{2,1,0:T(8,128)S(1)} %bitcast.43, f32[64,384]{1,0:T(8,128)S(1)} %get-tuple-element.34.b0.order), custom_call_target="tpu_custom_call" | custom-call | flops 49999998976 | bytes 100000000 | tf_op jit(solution)/shard_map/pallas_call | solution.py:401
  9.2 4.9 %collective-permute-start.5 = (f32[144,256]{1,0:T(8,128)}, f32[144,256]{1,0:T(8,128)}, u32[]{:S(2)}, u32[]{:S(2)}) collective-permute-start(f32[144,256]{1,0:T(8,128)} %get-tuple-element.43), channel_id=1, source_target_pairs={{0,16},{16,32},{32,48},{48,64},{64,80},{80,96},{96,112},{112,128},... | collective-permute-start | bytes 442376 | tf_op jit(solution)/shard_map/ppermute | solution.py:445
  14.3 0.0 copy-start.5
  14.3 0.0 copy-start.6
  14.3 0.0 copy-start.9
  14.3 0.0 copy-start.10
  14.3 0.5 shard_map.224.order
  14.8 5.2 %collective-permute-start.3 = (f32[2,64,256]{2,1,0:T(8,128)S(1)}, f32[2,64,256]{2,1,0:T(8,128)S(1)}, u32[]{:S(2)}, u32[]{:S(2)}) collective-permute-start(f32[2,64,256]{2,1,0:T(8,128)S(1)} %shard_map.224.order), channel_id=1, source_target_pairs={{0,1},{1,0},{2,3},{3,2},{16,19},{17,18},{18,17},{19,16},{32,33},{3... | collective-permute-start | bytes 393224 | tf_op jit(solution)/shard_map/ppermute | solution.py:462
  20.0 0.0 copy-start.8
  20.1 1.0 %shard_map.225 = (f32[16,64,256]{2,1,0:T(8,128)S(1)}, f32[16,256]{1,0:T(8,128)S(1)}) custom-call(f32[2,64,256]{2,1,0:T(8,128)S(1)} %bitcast.60, f32[2,64,256]{2,1,0:T(8,128)S(1)} %bitcast.62, f32[6,64,256]{2,1,0:T(8,128)S(1)} %bitcast.56, f32[6,64,256]{2,1,0:T(8,128)S(1)} %bitcast.58, f32[6,64,256]{2,1,0:T(8,128)S(1)} %bitcast.48, ...), custom_call_target="tpu_custom_call" | custom-call | flops 49999998976 | bytes 100000000 | tf_op jit(solution)/shard_map/pallas_call | solution.py:401
  21.0 0.0 copy-start.7
  21.0 2.5 %collective-permute-done.3 = f32[2,64,256]{2,1,0:T(8,128)S(1)} collective-permute-done((f32[2,64,256]{2,1,0:T(8,128)S(1)}, f32[2,64,256]{2,1,0:T(8,128)S(1)}, u32[]{:S(2)}, u32[]{:S(2)}) %collective-permute-start.3) | collective-permute-done | bytes 131104 | tf_op jit(solution)/shard_map/ppermute | solution.py:462
  23.6 1.0 %collective-permute-start.4 = (f32[2,64,256]{2,1,0:T(8,128)S(1)}, f32[2,64,256]{2,1,0:T(8,128)S(1)}, u32[]{:S(2)}, u32[]{:S(2)}) collective-permute-start(f32[2,64,256]{2,1,0:T(8,128)S(1)} %add.3.sum_a), channel_id=1, source_target_pairs={{0,3},{1,2},{2,1},{3,0},{16,17},{17,16},{18,19},{19,18},{32,35},{3... | collective-permute-start | bytes 393224 | tf_op jit(solution)/shard_map/ppermute | solution.py:465
  24.5 6.0 %collective-permute-start.6 = (f32[14,64,256]{2,1,0:T(8,128)S(1)}, f32[14,64,256]{2,1,0:T(8,128)S(1)}, u32[]{:S(2)}, u32[]{:S(2)}) collective-permute-start(f32[14,64,256]{2,1,0:T(8,128)S(1)} %get-tuple-element.45), channel_id=1, source_target_pairs={{0,16},{16,32},{32,48},{48,64},{64,80},{80,96},{96,112},{112,128},... | collective-permute-start | bytes 2752520 | tf_op jit(solution)/shard_map/ppermute | solution.py:466
  30.6 1.9 %collective-permute-start.7 = (f32[16,64,256]{2,1,0:T(8,128)S(1)}, f32[16,64,256]{2,1,0:T(8,128)S(1)}, u32[]{:S(2)}, u32[]{:S(2)}) collective-permute-start(f32[16,64,256]{2,1,0:T(8,128)S(1)} %get-tuple-element.39.w), channel_id=1, source_target_pairs={{16,0},{17,1},{18,2},{19,3},{32,17},{33,18},{34,19},{35,16},{48,32... | collective-permute-start | bytes 3145736 | tf_op jit(solution)/shard_map/ppermute | solution.py:467
  32.5 0.0 copy-start.4
  32.6 0.0 copy-start.14
  32.6 1.7 %shard_map.227 = (f32[64,384]{1,0:T(8,128)S(1)}, f32[64,384]{1,0:T(8,128)S(1)}, f32[64,384]{1,0:T(8,128)S(1)}, f32[80,384]{1,0:T(8,128)S(1)}, f32[2,64,256]{2,1,0:T(8,128)S(1)}, /*index=5*/f32[2,64,256]{2,1,0:T(8,128)S(1)}) custom-call(f32[2,64,256]{2,1,0:T(8,128)S(1)} %add.3.sum_a, f32[2,64,256]{2,1,0:T(8,128)S(1)} %collective-permute-done.4.sum_b, ...), custom_call_target="tpu_custom_call" | custom-call | flops 99999997952 | bytes 200000000 | tf_op jit(solution)/shard_map/pallas_call | solution.py:401
  34.3 1.9 %collective-permute-start.9 = (f32[80,384]{1,0:T(8,128)S(1)}, f32[80,384]{1,0:T(8,128)S(1)}, u32[]{:S(2)}, u32[]{:S(2)}) collective-permute-start(f32[80,384]{1,0:T(8,128)S(1)} %get-tuple-element.47), channel_id=1, source_target_pairs={{0,12},{4,0},{8,4},{12,8},{1,13},{5,1},{9,5},{13,9},{2,14},{6,2},{... | collective-permute-start | bytes 368648 | tf_op jit(solution)/shard_map/ppermute | solution.py:413
  36.1 1.3 %collective-permute-start.11 = (f32[64,384]{1,0:T(8,128)S(1)}, f32[64,384]{1,0:T(8,128)S(1)}, u32[]{:S(2)}, u32[]{:S(2)}) collective-permute-start(f32[64,384]{1,0:T(8,128)S(1)} %get-tuple-element.54), channel_id=1, source_target_pairs={{0,8},{4,12},{8,0},{12,4},{1,9},{5,13},{9,1},{13,5},{2,10},{6,14},... | collective-permute-start | bytes 294920 | tf_op jit(solution)/shard_map/ppermute | solution.py:413
  37.4 6.1 %collective-permute-done.10.b1 = f32[64,384]{1,0:T(8,128)S(1)} collective-permute-done((f32[64,384]{1,0:T(8,128)S(1)}, f32[64,384]{1,0:T(8,128)S(1)}, u32[]{:S(2)}, u32[]{:S(2)}) %collective-permute-start.10) | collective-permute-done | bytes 98336 | tf_op jit(solution)/shard_map/ppermute | solution.py:413
  43.6 2.3 %collective-permute-start.8 = (f32[2,64,256]{2,1,0:T(8,128)S(1)}, f32[2,64,256]{2,1,0:T(8,128)S(1)}, u32[]{:S(2)}, u32[]{:S(2)}) collective-permute-start(f32[2,64,256]{2,1,0:T(8,128)S(1)} %get-tuple-element.46.z), channel_id=1, source_target_pairs={{16,0},{32,16},{48,32},{64,48},{80,64},{96,80},{112,96},{128,112},... | collective-permute-start | bytes 393224 | tf_op jit(solution)/shard_map/ppermute | solution.py:474
  45.9 1.8 %shard_map.229 = f32[6,64,256]{2,1,0:T(8,128)} custom-call(f32[64,384]{1,0:T(8,128)S(1)} %get-tuple-element.52.b0, f32[64,384]{1,0:T(8,128)S(1)} %collective-permute-done.10.b1, f32[64,384]{1,0:T(8,128)S(1)} %collective-permute-done.11.b2, f32[80,384]{1,0:T(8,128)S(1)} %collective-permute-done.9.n3.b3, bf16[512,512]{1,0:T(8,128)(2,1)S(1)} %copy-done.14, ...), custom_call_target="tpu_custom_call" | custom-call | flops 2000000000 | bytes 4000000 | tf_op jit(solution)/shard_map/pallas_call | solution.py:401
  47.7 2.5 %collective-permute-done.8.z_in = f32[2,64,256]{2,1,0:T(8,128)S(1)} collective-permute-done((f32[2,64,256]{2,1,0:T(8,128)S(1)}, f32[2,64,256]{2,1,0:T(8,128)S(1)}, u32[]{:S(2)}, u32[]{:S(2)}) %collective-permute-start.8) | collective-permute-done | bytes 131104 | tf_op jit(solution)/shard_map/ppermute | solution.py:474
  50.1 2.2 %shard_map.228 = (f32[2,64,256]{2,1,0:T(8,128)}, f32[2,64,256]{2,1,0:T(8,128)}, f32[6,64,256]{2,1,0:T(8,128)}, f32[6,64,256]{2,1,0:T(8,128)}, f32[6,64,256]{2,1,...) custom-call(f32[2,64,256]{2,1,0:T(8,128)S(1)} %bitcast.61, ...), custom_call_target="tpu_custom_call" | custom-call | flops 500 | bytes 1 | tf_op jit(solution)/shard_map/pallas_call | solution.py:401
  (32 shorter events, 0.1 us)
Async XLA Ops:
  0.6 7.8 %copy-start = (f32[6,2,1,64,256]{4,3,2,1,0:T(8,128)S(1)}, f32[6,2,1,64,256]{4,3,2,1,0:T(8,128)}, u32[]{:S(2)}) copy-start(f32[6,2,1,64,256]{4,3,2,1,0:T(8,128)} %param.23) | copy-start | bytes 2359300
  0.7 7.8 %copy-start.1 = (f32[6,2,1,64,256]{4,3,2,1,0:T(8,128)S(1)}, f32[6,2,1,64,256]{4,3,2,1,0:T(8,128)}, u32[]{:S(2)}) copy-start(f32[6,2,1,64,256]{4,3,2,1,0:T(8,128)} %param.24) | copy-start | bytes 2359300
  0.7 7.8 %copy-start.2 = (f32[3,2,1,64,256]{4,3,2,1,0:T(8,128)S(1)}, f32[3,2,1,64,256]{4,3,2,1,0:T(8,128)}, u32[]{:S(2)}) copy-start(f32[3,2,1,64,256]{4,3,2,1,0:T(8,128)} %param.21) | copy-start | bytes 1179652
  0.7 7.8 %copy-start.3 = (f32[3,2,1,64,256]{4,3,2,1,0:T(8,128)S(1)}, f32[3,2,1,64,256]{4,3,2,1,0:T(8,128)}, u32[]{:S(2)}) copy-start(f32[3,2,1,64,256]{4,3,2,1,0:T(8,128)} %param.22) | copy-start | bytes 1179652
  2.7 11.5 %collective-permute-start = (f32[80,384]{1,0:T(8,128)S(1)}, f32[80,384]{1,0:T(8,128)S(1)}, u32[]{:S(2)}, u32[]{:S(2)}) collective-permute-start(f32[80,384]{1,0:T(8,128)S(1)} %get-tuple-element.35), channel_id=1, source_target_pairs={{0,4},{4,8},{8,12},{12,0},{1,5},{5,9},{9,13},{13,1},{2,6},{6,10},{... | collective-permute-start | bytes 368648 | tf_op jit(solution)/shard_map/ppermute | solution.py:413
  4.9 9.3 %collective-permute-start.1 = (f32[64,384]{1,0:T(8,128)S(1)}, f32[64,384]{1,0:T(8,128)S(1)}, u32[]{:S(2)}, u32[]{:S(2)}) collective-permute-start(f32[64,384]{1,0:T(8,128)S(1)} %get-tuple-element.36), channel_id=1, source_target_pairs={{0,8},{4,12},{8,0},{12,4},{1,9},{5,13},{9,1},{13,5},{2,10},{6,14},... | collective-permute-start | bytes 294920 | tf_op jit(solution)/shard_map/ppermute | solution.py:413
  7.3 6.9 %collective-permute-start.2 = (f32[64,384]{1,0:T(8,128)S(1)}, f32[64,384]{1,0:T(8,128)S(1)}, u32[]{:S(2)}, u32[]{:S(2)}) collective-permute-start(f32[64,384]{1,0:T(8,128)S(1)} %get-tuple-element.37), channel_id=1, source_target_pairs={{0,12},{4,0},{8,4},{12,8},{1,13},{5,1},{9,5},{13,9},{2,14},{6,2},{... | collective-permute-start | bytes 294920 | tf_op jit(solution)/shard_map/ppermute | solution.py:413
  8.5 5.8 %copy-start.11 = (f32[2,3,64,256]{3,2,1,0:T(8,128)S(1)}, f32[2,3,64,256]{3,2,1,0:T(8,128)}, u32[]{:S(2)}) copy-start(f32[2,3,64,256]{3,2,1,0:T(8,128)} %param.26) | copy-start | bytes 1179652
  8.5 5.8 %copy-start.13 = (bf16[512,512]{1,0:T(8,128)(2,1)S(1)}, bf16[512,512]{1,0:T(8,128)(2,1)}, u32[]{:S(2)}) copy-start(bf16[512,512]{1,0:T(8,128)(2,1)} %constant.10.clone.th_ref) | copy-start | bytes 1572868
  8.5 5.7 %copy-start.15 = (bf16[512,512]{1,0:T(8,128)(2,1)S(1)}, bf16[512,512]{1,0:T(8,128)(2,1)}, u32[]{:S(2)}) copy-start(bf16[512,512]{1,0:T(8,128)(2,1)} %constant.11.clone.tl_ref) | copy-start | bytes 1572868
  9.2 23.3 %collective-permute-start.5 = (f32[144,256]{1,0:T(8,128)}, f32[144,256]{1,0:T(8,128)}, u32[]{:S(2)}, u32[]{:S(2)}) collective-permute-start(f32[144,256]{1,0:T(8,128)} %get-tuple-element.43), channel_id=1, source_target_pairs={{0,16},{16,32},{32,48},{48,64},{64,80},{80,96},{96,112},{112,128},... | collective-permute-start | bytes 442376 | tf_op jit(solution)/shard_map/ppermute | solution.py:445
  14.3 5.8 %copy-start.5 = (f32[3,2,1,64,256]{4,3,2,1,0:T(8,128)S(1)}, f32[3,2,1,64,256]{4,3,2,1,0:T(8,128)}, u32[]{:S(2)}) copy-start(f32[3,2,1,64,256]{4,3,2,1,0:T(8,128)} %param.18) | copy-start | bytes 1179652
  14.3 5.8 %copy-start.6 = (f32[3,2,1,64,256]{4,3,2,1,0:T(8,128)S(1)}, f32[3,2,1,64,256]{4,3,2,1,0:T(8,128)}, u32[]{:S(2)}) copy-start(f32[3,2,1,64,256]{4,3,2,1,0:T(8,128)} %param.19) | copy-start | bytes 1179652
  14.3 5.8 %copy-start.9 = (f32[2,1,64,256]{3,2,1,0:T(8,128)S(1)}, f32[2,1,64,256]{3,2,1,0:T(8,128)}, u32[]{:S(2)}) copy-start(f32[2,1,64,256]{3,2,1,0:T(8,128)} %param.16) | copy-start | bytes 393220
  14.3 5.7 %copy-start.10 = (f32[2,1,64,256]{3,2,1,0:T(8,128)S(1)}, f32[2,1,64,256]{3,2,1,0:T(8,128)}, u32[]{:S(2)}) copy-start(f32[2,1,64,256]{3,2,1,0:T(8,128)} %param.17) | copy-start | bytes 393220
  14.8 8.7 %collective-permute-start.3 = (f32[2,64,256]{2,1,0:T(8,128)S(1)}, f32[2,64,256]{2,1,0:T(8,128)S(1)}, u32[]{:S(2)}, u32[]{:S(2)}) collective-permute-start(f32[2,64,256]{2,1,0:T(8,128)S(1)} %shard_map.224.order), channel_id=1, source_target_pairs={{0,1},{1,0},{2,3},{3,2},{16,19},{17,18},{18,17},{19,16},{32,33},{3... | collective-permute-start | bytes 393224 | tf_op jit(solution)/shard_map/ppermute | solution.py:462
  20.0 12.5 %copy-start.8 = (bf16[256,512]{1,0:T(8,128)(2,1)S(1)}, bf16[256,512]{1,0:T(8,128)(2,1)}, u32[]{:S(2)}) copy-start(bf16[256,512]{1,0:T(8,128)(2,1)} %constant.9.clone.tl_hbm.tl_ref) | copy-start | bytes 786436
  21.0 11.5 %copy-start.7 = (bf16[256,512]{1,0:T(8,128)(2,1)S(1)}, bf16[256,512]{1,0:T(8,128)(2,1)}, u32[]{:S(2)}) copy-start(bf16[256,512]{1,0:T(8,128)(2,1)} %constant.8.clone.th_hbm.th_ref) | copy-start | bytes 786436
  23.6 9.0 %collective-permute-start.4 = (f32[2,64,256]{2,1,0:T(8,128)S(1)}, f32[2,64,256]{2,1,0:T(8,128)S(1)}, u32[]{:S(2)}, u32[]{:S(2)}) collective-permute-start(f32[2,64,256]{2,1,0:T(8,128)S(1)} %add.3.sum_a), channel_id=1, source_target_pairs={{0,3},{1,2},{2,1},{3,0},{16,17},{17,16},{18,19},{19,18},{32,35},{3... | collective-permute-start | bytes 393224 | tf_op jit(solution)/shard_map/ppermute | solution.py:465
  24.5 25.6 %collective-permute-start.6 = (f32[14,64,256]{2,1,0:T(8,128)S(1)}, f32[14,64,256]{2,1,0:T(8,128)S(1)}, u32[]{:S(2)}, u32[]{:S(2)}) collective-permute-start(f32[14,64,256]{2,1,0:T(8,128)S(1)} %get-tuple-element.45), channel_id=1, source_target_pairs={{0,16},{16,32},{32,48},{48,64},{64,80},{80,96},{96,112},{112,128},... | collective-permute-start | bytes 2752520 | tf_op jit(solution)/shard_map/ppermute | solution.py:466
  30.6 19.6 %collective-permute-start.7 = (f32[16,64,256]{2,1,0:T(8,128)S(1)}, f32[16,64,256]{2,1,0:T(8,128)S(1)}, u32[]{:S(2)}, u32[]{:S(2)}) collective-permute-start(f32[16,64,256]{2,1,0:T(8,128)S(1)} %get-tuple-element.39.w), channel_id=1, source_target_pairs={{16,0},{17,1},{18,2},{19,3},{32,17},{33,18},{34,19},{35,16},{48,32... | collective-permute-start | bytes 3145736 | tf_op jit(solution)/shard_map/ppermute | solution.py:467
  32.5 13.3 %copy-start.4 = (f32[2,1,3,64,256]{4,3,2,1,0:T(8,128)S(1)}, f32[2,1,3,64,256]{4,3,2,1,0:T(8,128)}, u32[]{:S(2)}) copy-start(f32[2,1,3,64,256]{4,3,2,1,0:T(8,128)} %param.20) | copy-start | bytes 1179652
  32.6 13.3 %copy-start.12 = (f32[2,1,3,64,256]{4,3,2,1,0:T(8,128)S(1)}, f32[2,1,3,64,256]{4,3,2,1,0:T(8,128)}, u32[]{:S(2)}) copy-start(f32[2,1,3,64,256]{4,3,2,1,0:T(8,128)} %param.25) | copy-start | bytes 1179652
  32.6 13.3 %copy-start.14 = (bf16[512,512]{1,0:T(8,128)(2,1)S(1)}, bf16[512,512]{1,0:T(8,128)(2,1)}, u32[]{:S(2)}) copy-start(bf16[512,512]{1,0:T(8,128)(2,1)} %constant.10.clone.th_ref) | copy-start | bytes 1572868
  34.3 11.6 %collective-permute-start.9 = (f32[80,384]{1,0:T(8,128)S(1)}, f32[80,384]{1,0:T(8,128)S(1)}, u32[]{:S(2)}, u32[]{:S(2)}) collective-permute-start(f32[80,384]{1,0:T(8,128)S(1)} %get-tuple-element.47), channel_id=1, source_target_pairs={{0,12},{4,0},{8,4},{12,8},{1,13},{5,1},{9,5},{13,9},{2,14},{6,2},{... | collective-permute-start | bytes 368648 | tf_op jit(solution)/shard_map/ppermute | solution.py:413
  36.1 7.4 %collective-permute-start.10 = (f32[64,384]{1,0:T(8,128)S(1)}, f32[64,384]{1,0:T(8,128)S(1)}, u32[]{:S(2)}, u32[]{:S(2)}) collective-permute-start(f32[64,384]{1,0:T(8,128)S(1)} %get-tuple-element.53), channel_id=1, source_target_pairs={{0,4},{4,8},{8,12},{12,0},{1,5},{5,9},{9,13},{13,1},{2,6},{6,10},{... | collective-permute-start | bytes 294920 | tf_op jit(solution)/shard_map/ppermute | solution.py:413
  36.1 9.7 %collective-permute-start.11 = (f32[64,384]{1,0:T(8,128)S(1)}, f32[64,384]{1,0:T(8,128)S(1)}, u32[]{:S(2)}, u32[]{:S(2)}) collective-permute-start(f32[64,384]{1,0:T(8,128)S(1)} %get-tuple-element.54), channel_id=1, source_target_pairs={{0,8},{4,12},{8,0},{12,4},{1,9},{5,13},{9,1},{13,5},{2,10},{6,14},... | collective-permute-start | bytes 294920 | tf_op jit(solution)/shard_map/ppermute | solution.py:413
  43.6 6.6 %collective-permute-start.8 = (f32[2,64,256]{2,1,0:T(8,128)S(1)}, f32[2,64,256]{2,1,0:T(8,128)S(1)}, u32[]{:S(2)}, u32[]{:S(2)}) collective-permute-start(f32[2,64,256]{2,1,0:T(8,128)S(1)} %get-tuple-element.46.z), channel_id=1, source_target_pairs={{16,0},{32,16},{48,32},{64,48},{80,64},{96,80},{112,96},{128,112},... | collective-permute-start | bytes 393224 | tf_op jit(solution)/shard_map/ppermute | solution.py:474

commit v3 on v2

--- a/solution.py
+++ b/solution.py
@@ -94,7 +94,7 @@
 
 
 def start_kernel(
-    kd_hbm, lines_hbm, th_hbm, tl_hbm, g1, g2, s1, s2, o0, o1, o2, o3,
+    kd_hbm, lines_hbm, th_hbm, tl_hbm, g1, g2, s1, s2, o0, o1, o2, o3, mask_out,
     kd_ref, lines_ref, th_ref, tl_ref, ends, sems
 ):
     row = lax.axis_index("row")
@@ -118,6 +118,7 @@
     for copy in copies[:4]:
         copy.wait()
     mask = lines_ref[...].astype(F32)
+    mask_out[...] = mask
     parts = []
     for c in range(COIL):
         real = kd_ref[c] * mask
@@ -138,7 +139,7 @@
     return ref[plane, pl.ds(i * 8 if isinstance(i, int) else pl.multiple_of(i * 8, 8), 8), :]
 
 
-def pack_kernel(g1, g2, s1, s2, order, q_first, q_out):
+def pack_kernel(g1, g2, s1, s2, order, q_first):
     refs = dict(g1=g1, g2=g2, s1=s1, s2=s2)
     for reim in range(2):
         q_first[BLOCK * reim : BLOCK * (reim + 1), :] = g1[reim]
@@ -146,11 +147,10 @@
         for field in range(8):
             place = 2 * BLOCK + 2 * field + reim
             q_first[place : place + 1, :] = time_term(lambda k: tops[k], field)
-        for index, (name, part) in enumerate(TIME_PARTS[1:]):
-            q_out[2 * index + reim] = refs[name][2 * part + reim]
-
-
-def plain_kernel(img, spl, v1, v2, g1, g2, s1, s2, b1, order, w_out, w_top):
+
+
+def plain_kernel(img, spl, v1, v2, g1, g2, s1, s2, b1, q_first, order, w_out, image_out, tops, to_core, to_chip):
+    odd = lax.rem(lax.axis_index("tm"), 2)
     row = lax.axis_index("row")
     keep_time = (lax.axis_index("tm") != lax.axis_size("tm") - 1).astype(F32)
     refs = dict(g1=g1, g2=g2, s1=s1, s2=s2)
@@ -185,6 +185,8 @@
             two = -BETA_TWO * keep_time * chunk(g2, z, i) + adj_rows("g2", y) + adj_cols(g2, x)
             image = chunk(img, reim, i) - 2.0 * TAU * one
             other = chunk(spl, reim, i) - 2.0 * TAU * (two - one)
+            before = q_first[pl.ds(pl.multiple_of(BLOCK * reim + i * 8, 8), 8), :]
+            put(image_out, reim, image - 2.0 * TAU * BETA_ONE * before)
             put(w_out, reim, image - other)
             put(w_out, 2 + reim, other)
             for base, vec, grad, name, beta in ((4, v1, g1, "s1", BETA_ONE), (10, v2, g2, "s2", BETA_TWO)):
@@ -200,7 +202,16 @@
 
     lax.fori_loop(0, 8, step, 0)
     for plane in range(16):
-        w_top[plane : plane + 1, :] = w_out[plane, 0:1, :]
+        place = 2 * BLOCK + plane
+        tops[plane : plane + 1, :] = w_out[plane, 0:1, :] + q_first[place : place + 1, :]
+
+    def messages(q_to, w_to):
+        for index, (name, part) in enumerate(TIME_PARTS):
+            q_to[2 * index : 2 * index + 2] = refs[name][2 * part : 2 * part + 2]
+        w_to[...] = w_out[...]
+
+    pl.when(odd == 0)(lambda: messages(to_core, to_chip))
+    pl.when(odd == 1)(lambda: messages(to_chip, to_core))
 
 
 def combine_kernel(b0, b1, b2, b3, th_ref, tl_ref, sens, out):
@@ -227,15 +238,13 @@
     return (-2.0 * TAU * beta * (1.0 if field in (2, 5) else 0.5)) * q(field)
 
 
-def predict_kernel(sum_a, sum_b, w, w_top, q_first, th_ref, tl_ref, sens, o0, o1, o2, o3, z_out, q0_out):
+def predict_kernel(sum_a, sum_b, base, tops, th_ref, tl_ref, sens, o0, o1, o2, o3, z_out):
     row = lax.axis_index("row")
     image = []
     for reim in range(2):
         back = sum_a[reim] + sum_b[reim]
         z_out[reim] = back
-        before = q_first[BLOCK * reim : BLOCK * (reim + 1), :]
-        q0_out[reim] = before
-        image.append(w[reim] + w[2 + reim] - 2.0 * TAU * BETA_ONE * before - 2.0 * TAU * back)
+        image.append(base[reim] - 2.0 * TAU * back)
     parts = []
     for c in range(COIL):
         real = sens[c] * image[0] - sens[COIL + c] * image[1]
@@ -246,18 +255,15 @@
     for d, ref in enumerate((o0, o1, o2, o3)):
         ref[0:BLOCK, :] = out[BLOCK * d : BLOCK * (d + 1)]
     o3[BLOCK:, LENGTH:] = jnp.zeros((16, 128), F32)
-    o3[BLOCK:, 0:LENGTH] = w_top[...] + q_first[2 * BLOCK :, :]
+    o3[BLOCK:, 0:LENGTH] = tops[...]
     for reim in range(2):
         o3[BLOCK + reim : BLOCK + reim + 1, 0:LENGTH] -= 2.0 * TAU * (sum_a[reim, 0:1, :] + sum_b[reim, 0:1, :])
 
 
-def finish_kernel(b0, b1, b2, b3, th_ref, tl_ref, kd_ref, measured, lines_hbm, out_hbm, lines_ref, out, sems):
+def finish_kernel(b0, b1, b2, b3, th_ref, tl_ref, kd_ref, measured, mask_ref, out_hbm, out, sems):
     row = lax.axis_index("row")
-    lines = pltpu.make_async_copy(lines_hbm, lines_ref, sems.at[0])
-    lines.start()
     both = second_transform(th_ref, tl_ref, (b0, b1, b2, b3), row)
-    lines.wait()
-    mask = SIGMA * lines_ref[...].astype(F32)
+    mask = SIGMA * mask_ref[...]
     scale = 1.0 / (1.0 + SIGMA / LAMBDA_DATA)
     copies = []
     for c in range(COIL):
@@ -265,132 +271,135 @@
         imag = -both[BLOCK * c : BLOCK * (c + 1), LENGTH:]
         for plane, value in ((c, real), (COIL + c, imag)):
             out[plane] = (kd_ref[plane] + mask * (value - measured[plane])) * scale
-            copies.append(pltpu.make_async_copy(out.at[plane], out_hbm.at[plane], sems.at[1 + plane]))
+            copies.append(pltpu.make_async_copy(out.at[plane], out_hbm.at[plane], sems.at[plane]))
             copies[-1].start()
     for copy in copies:
         copy.wait()
 
 
 def fields_kernel(
-    img, spl, v1, v2, g1, g2, s1, s2, w, q0, q_in, w_in, z, z_in, n3,
+    img, spl, v1, v2, g1, g2, s1, s2, w, from_core, from_chip, z, z_in, n3,
     img_hbm, spl_hbm, v1_hbm, v2_hbm, g1_hbm, g2_hbm, s1_hbm, s2_hbm,
     bar, img_out, spl_out, v1_out, v2_out, g1_out, g2_out, s1_out, s2_out, sems,
 ):
-    row = lax.axis_index("row")
-    keep_time = (lax.axis_index("tm") != lax.axis_size("tm") - 1).astype(F32)
-    refs = dict(g1=g1, g2=g2, s1=s1, s2=s2)
-    copies = [
-        pltpu.make_async_copy(source, target, sems.at[k])
-        for k, (source, target) in enumerate(
-            ((img_out, img_hbm), (spl_out, spl_hbm), (v1_out, v1_hbm), (v2_out, v2_hbm))
-        )
-    ]
-
-    def span(i):
-        return pl.ds(i * 8 if isinstance(i, int) else pl.multiple_of(i * 8, 8), 8)
-
-    def first(i, carry):
-        for reim in range(2):
-
-            def before(k):
-                if k == 0:
-                    return chunk(q0, reim, i)
-                return chunk(q_in, 2 * (k - 1) + reim, i)
-
-            values = []
-            for field in range(8):
-                plane = 2 * field + reim
-                value = chunk(w, plane, i) + time_term(before, field)
-                if field == 0:
-                    value -= 2.0 * TAU * chunk(z, reim, i)
-                bar[plane, span(i), :] = value
-                values.append(value)
-            img_out[reim, span(i), :] = 0.5 * (values[0] + values[1] + chunk(img, reim, i))
-            spl_out[reim, span(i), :] = 0.5 * (values[1] + chunk(spl, reim, i))
+    def run(q_in, w_in):
+        row = lax.axis_index("row")
+        keep_time = (lax.axis_index("tm") != lax.axis_size("tm") - 1).astype(F32)
+        refs = dict(g1=g1, g2=g2, s1=s1, s2=s2)
+        copies = [
+            pltpu.make_async_copy(source, target, sems.at[k])
+            for k, (source, target) in enumerate(
+                ((img_out, img_hbm), (spl_out, spl_hbm), (v1_out, v1_hbm), (v2_out, v2_hbm))
+            )
+        ]
+
+        def span(i):
+            return pl.ds(i * 8 if isinstance(i, int) else pl.multiple_of(i * 8, 8), 8)
+
+        def first(i, carry):
+            for reim in range(2):
+
+                def before(k):
+                    return chunk(q_in, 2 * k + reim, i)
+
+                values = []
+                for field in range(8):
+                    plane = 2 * field + reim
+                    value = chunk(w, plane, i) + time_term(before, field)
+                    if field == 0:
+                        value -= 2.0 * TAU * chunk(z, reim, i)
+                    bar[plane, span(i), :] = value
+                    values.append(value)
+                img_out[reim, span(i), :] = 0.5 * (values[0] + values[1] + chunk(img, reim, i))
+                spl_out[reim, span(i), :] = 0.5 * (values[1] + chunk(spl, reim, i))
+                for k in range(3):
+                    plane = 2 * k + reim
+                    v1_out[plane, span(i), :] = 0.5 * (values[2 + k] + chunk(v1, plane, i))
+                    v2_out[plane, span(i), :] = 0.5 * (values[5 + k] + chunk(v2, plane, i))
+            return carry
+
+        lax.fori_loop(0, 8, first, 0, unroll=2)
+        for copy in copies:
+            copy.start()
+        for plane in range(16):
+            below = n3[BLOCK + plane : BLOCK + plane + 1, 0:LENGTH]
+            bar[plane, BLOCK : BLOCK + 1, :] = jnp.where(row == ROWS - 1, bar[plane, BLOCK - 1 : BLOCK, :], below)
+
+        def along_rows(plane, i):
+            here = chunk(bar, plane, i)
+            below = chunk(bar, plane, i + 1)
+            rows = iota((8, LENGTH), 0)
+            return jnp.where(rows == 7, pltpu.roll(below, 7, 0), pltpu.roll(here, 7, 0)) - here
+
+        def along_cols(plane, i):
+            here = chunk(bar, plane, i)
+            cols = iota((8, LENGTH), 1)
+            return jnp.where(cols == LENGTH - 1, 0.0, pltpu.roll(here, LENGTH - 1, 1) - here)
+
+        def along_time(field, reim, i):
+            plane = 2 * field + reim
+            value = chunk(w_in, plane, i)
+            value += time_term(lambda k: chunk(refs[TIME_PARTS[k][0]], 2 * TIME_PARTS[k][1] + reim, i), field)
+            if field == 0:
+                value -= 2.0 * TAU * chunk(z_in, reim, i)
+            return value - chunk(bar, plane, i)
+
+        def project(out, duals, radius, i):
+            total = duals[0] * duals[0]
+            for value in duals[1:]:
+                total += value * value
+            scale = jnp.minimum(1.0, radius * lax.rsqrt(total))
+            for plane, value in enumerate(duals):
+                out[plane, span(i), :] = value * scale
+
+        def gradient(i, dual, out, field, vec, beta):
+            duals = []
             for k in range(3):
-                plane = 2 * k + reim
-                v1_out[plane, span(i), :] = 0.5 * (values[2 + k] + chunk(v1, plane, i))
-                v2_out[plane, span(i), :] = 0.5 * (values[5 + k] + chunk(v2, plane, i))
-        return carry
-
-    lax.fori_loop(0, 8, first, 0, unroll=2)
-    for copy in copies:
-        copy.start()
-    for plane in range(16):
-        below = n3[BLOCK + plane : BLOCK + plane + 1, 0:LENGTH]
-        bar[plane, BLOCK : BLOCK + 1, :] = jnp.where(row == ROWS - 1, bar[plane, BLOCK - 1 : BLOCK, :], below)
-
-    def along_rows(plane, i):
-        here = chunk(bar, plane, i)
-        below = chunk(bar, plane, i + 1)
-        rows = iota((8, LENGTH), 0)
-        return jnp.where(rows == 7, pltpu.roll(below, 7, 0), pltpu.roll(here, 7, 0)) - here
-
-    def along_cols(plane, i):
-        here = chunk(bar, plane, i)
-        cols = iota((8, LENGTH), 1)
-        return jnp.where(cols == LENGTH - 1, 0.0, pltpu.roll(here, LENGTH - 1, 1) - here)
-
-    def along_time(field, reim, i):
-        plane = 2 * field + reim
-        value = chunk(w_in, plane, i)
-        value += time_term(lambda k: chunk(refs[TIME_PARTS[k][0]], 2 * TIME_PARTS[k][1] + reim, i), field)
-        if field == 0:
-            value -= 2.0 * TAU * chunk(z_in, reim, i)
-        return value - chunk(bar, plane, i)
-
-    def project(out, duals, radius, i):
-        total = duals[0] * duals[0]
-        for value in duals[1:]:
-            total += value * value
-        scale = jnp.minimum(1.0, radius * lax.rsqrt(total))
-        for plane, value in enumerate(duals):
-            out[plane, span(i), :] = value * scale
-
-    def gradient(i, dual, out, field, vec, beta):
-        duals = []
-        for k in range(3):
+                for reim in range(2):
+                    if k == 0:
+                        diff = (beta * keep_time) * along_time(field, reim, i)
+                    else:
+                        diff = (along_rows, along_cols)[k - 1](2 * field + reim, i)
+                    diff -= chunk(bar, 2 * (vec + k) + reim, i)
+                    duals.append(chunk(dual, 2 * k + reim, i) + SIGMA * diff)
+            project(out, duals, ALPHA_ONE, i)
+
+        def symmetric(i, dual, out, vec, beta):
+            duals = [None] * 12
             for reim in range(2):
-                if k == 0:
-                    diff = (beta * keep_time) * along_time(field, reim, i)
-                else:
-                    diff = (along_rows, along_cols)[k - 1](2 * field + reim, i)
-                diff -= chunk(bar, 2 * (vec + k) + reim, i)
-                duals.append(chunk(dual, 2 * k + reim, i) + SIGMA * diff)
-        project(out, duals, ALPHA_ONE, i)
-
-    def symmetric(i, dual, out, vec, beta):
-        duals = [None] * 12
-        for reim in range(2):
-            p0, p1, p2 = (2 * (vec + k) + reim for k in range(3))
-            steps = (
-                (SIGMA * beta * keep_time) * along_time(vec, reim, i),
-                SIGMA * along_rows(p1, i),
-                SIGMA * along_cols(p2, i),
-                0.5 * SIGMA * along_rows(p0, i) + (0.5 * SIGMA * beta * keep_time) * along_time(vec + 1, reim, i),
-                0.5 * SIGMA * along_cols(p0, i) + (0.5 * SIGMA * beta * keep_time) * along_time(vec + 2, reim, i),
-                0.5 * SIGMA * (along_cols(p1, i) + along_rows(p2, i)),
-            )
-            for k, diff in enumerate(steps):
-                duals[2 * k + reim] = chunk(dual, 2 * k + reim, i) + diff
-        project(out, duals, ALPHA_ZERO, i)
-
-    def second(i):
-        gradient(i, g1, g1_out, 0, 2, BETA_ONE)
-        gradient(i, g2, g2_out, 1, 5, BETA_TWO)
-        symmetric(i, s1, s1_out, 2, BETA_ONE)
-        symmetric(i, s2, s2_out, 5, BETA_TWO)
-
-    for part in range(4):
-        rows = pl.ds(16 * part, 16)
-        second(2 * part)
-        second(2 * part + 1)
-        for k, (source, target) in enumerate(((g1_out, g1_hbm), (g2_out, g2_hbm), (s1_out, s1_hbm), (s2_out, s2_hbm))):
-            copy = pltpu.make_async_copy(source.at[:, rows, :], target.at[:, rows, :], sems.at[4 + 4 * part + k])
-            copy.start()
-            copies.append(copy)
-    for copy in copies:
-        copy.wait()
+                p0, p1, p2 = (2 * (vec + k) + reim for k in range(3))
+                steps = (
+                    (SIGMA * beta * keep_time) * along_time(vec, reim, i),
+                    SIGMA * along_rows(p1, i),
+                    SIGMA * along_cols(p2, i),
+                    0.5 * SIGMA * along_rows(p0, i) + (0.5 * SIGMA * beta * keep_time) * along_time(vec + 1, reim, i),
+                    0.5 * SIGMA * along_cols(p0, i) + (0.5 * SIGMA * beta * keep_time) * along_time(vec + 2, reim, i),
+                    0.5 * SIGMA * (along_cols(p1, i) + along_rows(p2, i)),
+                )
+                for k, diff in enumerate(steps):
+                    duals[2 * k + reim] = chunk(dual, 2 * k + reim, i) + diff
+            project(out, duals, ALPHA_ZERO, i)
+
+        def second(i):
+            gradient(i, g1, g1_out, 0, 2, BETA_ONE)
+            gradient(i, g2, g2_out, 1, 5, BETA_TWO)
+            symmetric(i, s1, s1_out, 2, BETA_ONE)
+            symmetric(i, s2, s2_out, 5, BETA_TWO)
+
+        for part in range(4):
+            rows = pl.ds(16 * part, 16)
+            second(2 * part)
+            second(2 * part + 1)
+            for k, (source, target) in enumerate(((g1_out, g1_hbm), (g2_out, g2_hbm), (s1_out, s1_hbm), (s2_out, s2_hbm))):
+                copy = pltpu.make_async_copy(source.at[:, rows, :], target.at[:, rows, :], sems.at[4 + 4 * part + k])
+                copy.start()
+                copies.append(copy)
+        for copy in copies:
+            copy.wait()
+
+    odd = lax.rem(lax.axis_index("tm"), 2)
+    pl.when(odd == 0)(lambda: run(from_chip, from_core))
+    pl.when(odd == 1)(lambda: run(from_core, from_chip))
 
 
 def shape(*dims):
@@ -425,8 +434,8 @@
     groups = lax.axis_size("coil")
     blocks = (shape(BLOCK, 384), shape(BLOCK + 16, 384), shape(BLOCK, 384), shape(BLOCK, 384))
     hbm = pl.BlockSpec(memory_space=pltpu.HBM)
-    a0, a1, a2, a3 = call(
-        start_kernel, blocks,
+    a0, a1, a2, a3, mask = call(
+        start_kernel, (*blocks, shape(1, LENGTH)),
         [pltpu.with_memory_space_constraint(x, pltpu.HBM) for x in (kd, sampled, first_high, first_low, g1, g2, s1, s2)],
         1,
         in_specs=[hbm] * 8,
@@ -438,8 +447,8 @@
     )
     b2, b1, b3 = turn(a2, 2), turn(a1, 1), turn(a3, 3)
     after = [(i, i + 1) for i in range(frames - 1)]
-    q_first, q_out = call(
-        pack_kernel, (shape(2 * BLOCK + 16, LENGTH), shape(14, BLOCK, LENGTH)), (g1, g2, s1, s2, a0), 100_000_000,
+    (q_first,) = call(
+        pack_kernel, (shape(2 * BLOCK + 16, LENGTH),), (g1, g2, s1, s2, a0), 100_000_000,
         in_specs=[pl.BlockSpec(memory_space=pltpu.VMEM)] * 4 + [pl.BlockSpec(memory_space=pl.ANY)],
     )
     q_first = lax.ppermute(q_first, "tm", after)
@@ -449,33 +458,36 @@
         [(t * groups + c, t * groups + partner[(t + turn) % 2][c]) for t in range(frames) for c in range(groups)]
         for turn in range(2)
     ]
-    w_out, w_top = call(
-        plain_kernel, (shape(16, BLOCK, LENGTH), shape(16, LENGTH)),
-        (img, spl, v1, v2, g1, g2, s1, s2, b1, partial), 100_000_000,
-        in_specs=[pl.BlockSpec(memory_space=pltpu.VMEM)] * 9 + [pl.BlockSpec(memory_space=pl.ANY)],
-    )
-    pairs = []
-    for t in range(1, frames):
-        for c in range(groups):
-            to = c if t % 2 else ((c + 1) % groups if t % 4 == 2 else (c - 1) % groups)
-            pairs.append((t * groups + c, (t - 1) * groups + to))
+    stack = shape(16, BLOCK, LENGTH)
+    w_out, base, tops, to_core, to_chip = call(
+        plain_kernel, (stack, shape(2, BLOCK, LENGTH), shape(16, LENGTH), stack, stack),
+        (img, spl, v1, v2, g1, g2, s1, s2, b1, q_first, partial), 100_000_000,
+        in_specs=[pl.BlockSpec(memory_space=pltpu.VMEM)] * 10 + [pl.BlockSpec(memory_space=pl.ANY)],
+    )
     received = lax.ppermute(partial, ("tm", "coil"), swaps[0])
     partial, received, w_out = lax.optimization_barrier((partial, received, w_out))
     pair = partial + received
     rest = lax.ppermute(pair, ("tm", "coil"), swaps[1])
-    q_in = lax.ppermute(q_out, "tm", after)
-    w_in = lax.ppermute(w_out, ("tm", "coil"), pairs)
+    pairs = []
+    for t in range(1, frames - 1, 2):
+        for c in range(groups):
+            there = c if t % 4 == 1 else (c + 1) % groups
+            pairs.append((t * groups + c, (t + 1) * groups + there))
+            pairs.append(((t + 1) * groups + there, t * groups + c))
+    from_chip = lax.ppermute(to_chip, ("tm", "coil"), pairs)
+    from_core = lax.ppermute(to_core, "tm", [(t, t ^ 1) for t in range(frames)])
     c_blocks = (shape(BLOCK, 384), shape(BLOCK, 384), shape(BLOCK, 384), shape(BLOCK + 16, 384))
-    c0, c1, c2, c3, z, q0 = call(
-        predict_kernel, (*c_blocks, shape(2, BLOCK, LENGTH), shape(2, BLOCK, LENGTH)),
-        (pair, rest, w_out, w_top, q_first, first_high, first_low, sens), 200_000_000,
+    c0, c1, c2, c3, z = call(
+        predict_kernel, (*c_blocks, shape(2, BLOCK, LENGTH)),
+        (pair, rest, base, tops, first_high, first_low, sens), 200_000_000,
     )
     n2, n1, n3 = turn(c2, 2), turn(c1, 1), turn(c3, 3)
+    z, from_core = lax.optimization_barrier((z, from_core))
     z_in = lax.ppermute(z, "tm", [(i + 1, i) for i in range(frames - 1)])
     like = lambda x: shape(*x.shape)
     fields = call(
         fields_kernel, tuple(map(like, (img, spl, v1, v2, g1, g2, s1, s2))),
-        (img, spl, v1, v2, g1, g2, s1, s2, w_out, q0, q_in, w_in, z, z_in, n3), 1,
+        (img, spl, v1, v2, g1, g2, s1, s2, w_out, from_core, from_chip, z, z_in, n3), 1,
         scratch=[
             pltpu.VMEM((16, BLOCK + 8, LENGTH), F32),
             *(pltpu.VMEM(x.shape, F32) for x in (img, spl, v1, v2, g1, g2, s1, s2)),
@@ -483,14 +495,9 @@
         ],
         out_space=pltpu.HBM,
     )
-    vmem = pl.BlockSpec(memory_space=pltpu.VMEM)
     (kspace,) = call(
-        finish_kernel, (like(kd),),
-        (c0, n1, n2, n3, high, low, kd, meas, pltpu.with_memory_space_constraint(sampled, pltpu.HBM)), 4_000_000,
-        in_specs=[vmem] * 8 + [hbm],
-        scratch=[
-            pltpu.VMEM((1, LENGTH), jnp.int32), pltpu.VMEM(kd.shape, F32), pltpu.SemaphoreType.DMA((1 + 2 * COIL,)),
-        ],
+        finish_kernel, (like(kd),), (c0, n1, n2, n3, high, low, kd, meas, mask), 4_000_000,
+        scratch=[pltpu.VMEM(kd.shape, F32), pltpu.SemaphoreType.DMA((2 * COIL,))],
         out_space=pltpu.HBM,
     )
     img_new, spl_new, v1_new, v2_new, g1_new, g2_new, s1_new, s2_new = fields

time: 52.6 us -> 47.1 us (0.90)
  waiting for transfers between devices: 11.1 us -> 7.1 us
  Pallas kernels: 9.86 us -> 7.73 us
    ppermute x6, waiting for transfers between devices: 6.14 us -> 1.24 us  [turn(): lax.ppermute(block, 'row', [(i, (i + distance) % ROWS) for i in range(ROW...]
    ppermute x2, waiting for transfers between devices: 0.01 us -> 2.32 us  [the longest x1 2.32 us: body(): from_chip = lax.ppermute(to_chip, ('tm', 'coil'), pairs)]
    pallas_call x7, Pallas kernels: 9.86 us -> 7.73 us  [call(): pl.pallas_call(kernel, out_shape=outs, in_specs=in_specs or [pl.BlockSpec...]
    ppermute x2, starting transfers between devices: 7.95 us -> 6.54 us  [the longest x1 3.83 us: body(): from_chip = lax.ppermute(to_chip, ('tm', 'coil'), pairs)]
    ppermute x1, starting transfers between devices: 2.25 us -> 3.49 us  [body(): z_in = lax.ppermute(z, 'tm', [(i + 1, i) for i in range(frames - 1)])]
    ppermute x1, waiting for transfers between devices: 2.48 us -> 1.4 us  [body(): z_in = lax.ppermute(z, 'tm', [(i + 1, i) for i in range(frames - 1)])]
  transfers between devices with their start and end apart: 12 -> 12, of which waited for: 3 -> 4; matrix products, arithmetic and copies ran while one was open for 0% -> 0% of each run, Pallas kernels for 11% -> 8%
where the time goes in v3:
time: 47.1 us; the launch traced here: 46.6 us
  starting transfers between devices  30.7 us (65%)
  Pallas kernels  7.73 us (16%)
  waiting for transfers between devices  7.1 us (15%)
  between operations  0.98 us (2%)
    ppermute x6, starting transfers between devices, turn(): lax.ppermute(block, 'row', [(i, (i + distance) % ROWS) for i in range(ROW...  9.1 us
    pallas_call x7, Pallas kernels, call(): pl.pallas_call(kernel, out_shape=outs, in_specs=in_specs or [pl.BlockSpec...  7.73 us
    ppermute x1, starting transfers between devices, body(): received = lax.ppermute(partial, ('tm', 'coil'), swaps[0])  5.2 us
    ppermute x1, starting transfers between devices, body(): q_first = lax.ppermute(q_first, 'tm', after)  5.08 us
    ppermute x1, starting transfers between devices, body(): from_chip = lax.ppermute(to_chip, ('tm', 'coil'), pairs)  3.83 us
    ppermute x1, starting transfers between devices, body(): z_in = lax.ppermute(z, 'tm', [(i + 1, i) for i in range(frames - 1)])  3.49 us
    ppermute x1, starting transfers between devices, body(): from_core = lax.ppermute(to_core, 'tm', [(t, t ^ 1) for t in range(frames)])  2.71 us
    ppermute x1, waiting for transfers between devices, body(): from_chip = lax.ppermute(to_chip, ('tm', 'coil'), pairs)  2.32 us
  transfers between devices with their start and end apart: 12, of which 4 were waited for; matrix products, arithmetic and copies ran while one was open for 0% of the time, Pallas kernels for 8%

profile of v3, /device:TPU:1, one launch (start us, length us, event | category | flops | bytes accessed | tf_op | source)
XLA Modules:
  0.0 46.6 jit_solution(13849902401641487992)
XLA Ops:
  0.7 2.0 %shard_map.223 = (f32[64,384]{1,0:T(8,128)S(1)}, f32[80,384]{1,0:T(8,128)S(1)}, f32[64,384]{1,0:T(8,128)S(1)}, f32[64,384]{1,0:T(8,128)S(1)}, f32[1,256]{1,0:T(1,128)S(1)}) custom-call(f32[6,64,256]{2,1,0:T(8,128)} %bitcast.54, s32[1,256]{1,0:T(1,128)} %lines_hbm.1, bf16[256,512]{1,0:T(8,128)(2,1)} %constant.8.clone.th_hbm.th_ref, ...), custom_call_target="tpu_custom_call" | custom-call | flops 500 | bytes 1 | tf_op jit(solution)/shard_map/pallas_call | solution.py:410
  2.7 2.1 %collective-permute-start = (f32[80,384]{1,0:T(8,128)S(1)}, f32[80,384]{1,0:T(8,128)S(1)}, u32[]{:S(2)}, u32[]{:S(2)}) collective-permute-start(f32[80,384]{1,0:T(8,128)S(1)} %get-tuple-element.38), channel_id=1, source_target_pairs={{0,4},{4,8},{8,12},{12,0},{1,5},{5,9},{9,13},{13,1},{2,6},{6,10},{... | collective-permute-start | bytes 368648 | tf_op jit(solution)/shard_map/ppermute | solution.py:422
  4.9 2.4 %collective-permute-start.1 = (f32[64,384]{1,0:T(8,128)S(1)}, f32[64,384]{1,0:T(8,128)S(1)}, u32[]{:S(2)}, u32[]{:S(2)}) collective-permute-start(f32[64,384]{1,0:T(8,128)S(1)} %get-tuple-element.39), channel_id=1, source_target_pairs={{0,8},{4,12},{8,0},{12,4},{1,9},{5,13},{9,1},{13,5},{2,10},{6,14},... | collective-permute-start | bytes 294920 | tf_op jit(solution)/shard_map/ppermute | solution.py:422
  7.3 1.2 %collective-permute-start.2 = (f32[64,384]{1,0:T(8,128)S(1)}, f32[64,384]{1,0:T(8,128)S(1)}, u32[]{:S(2)}, u32[]{:S(2)}) collective-permute-start(f32[64,384]{1,0:T(8,128)S(1)} %get-tuple-element.40), channel_id=1, source_target_pairs={{0,12},{4,0},{8,4},{12,8},{1,13},{5,1},{9,5},{13,9},{2,14},{6,2},{... | collective-permute-start | bytes 294920 | tf_op jit(solution)/shard_map/ppermute | solution.py:422
  8.5 0.0 copy-start.11
  8.5 0.0 copy-start.13
  8.5 0.0 copy-start.15
  8.5 5.1 %collective-permute-start.4 = (f32[144,256]{1,0:T(8,128)S(1)}, f32[144,256]{1,0:T(8,128)S(1)}, u32[]{:S(2)}, u32[]{:S(2)}) collective-permute-start(f32[144,256]{1,0:T(8,128)S(1)} %shard_map.225), channel_id=1, source_target_pairs={{0,16},{16,32},{32,48},{48,64},{64,80},{80,96},{96,112},{112,128},... | collective-permute-start | bytes 442376 | tf_op jit(solution)/shard_map/ppermute | solution.py:454
  13.7 0.0 copy-start.5
  13.7 0.0 copy-start.6
  13.7 0.0 copy-start.9
  13.7 0.0 copy-start.10
  13.7 0.5 %shard_map.224.order = f32[2,64,256]{2,1,0:T(8,128)S(1)} custom-call(f32[64,384]{1,0:T(8,128)S(1)} %get-tuple-element.37.b0.order, f32[80,384]{1,0:T(8,128)S(1)} %collective-permute-done.b1, f32[64,384]{1,0:T(8,128)S(1)} %collective-permute-done.1.b2, f32[64,384]{1,0:T(8,128)S(1)} %collective-permute-done.2.b3, bf16[512,512]{1,0:T(8,128)(2,1)S(1)} %copy-done.13, ...), custom_call_target="tpu_custom_call" | custom-call | flops 99999997952 | bytes 200000000 | tf_op jit(solution)/shard_map/pallas_call | solution.py:410
  14.3 5.2 %collective-permute-start.3 = (f32[2,64,256]{2,1,0:T(8,128)S(1)}, f32[2,64,256]{2,1,0:T(8,128)S(1)}, u32[]{:S(2)}, u32[]{:S(2)}) collective-permute-start(f32[2,64,256]{2,1,0:T(8,128)S(1)} %shard_map.224.order), channel_id=1, source_target_pairs={{0,1},{1,0},{2,3},{3,2},{16,19},{17,18},{18,17},{19,16},{32,33},{3... | collective-permute-start | bytes 393224 | tf_op jit(solution)/shard_map/ppermute | solution.py:467
  19.5 0.0 copy-start.8
  19.5 1.1 %shard_map.226 = (f32[16,64,256]{2,1,0:T(8,128)S(1)}, f32[2,64,256]{2,1,0:T(8,128)S(1)}, f32[16,256]{1,0:T(8,128)S(1)}, f32[16,64,256]{2,1,0:T(8,128)S(1)}, f32[16,64,256]{2,1,0:T(8,128)S(1)}) custom-call(f32[2,64,256]{2,1,0:T(8,128)S(1)} %bitcast.60, f32[2,64,256]{2,1,0:T(8,128)S(1)} %bitcast.62, f32[6,64,256]{2,1,0:T(8,128)S(1)} %bitcast.56, ...), custom_call_target="tpu_custom_call" | custom-call | flops 49999998976 | bytes 100000000 | tf_op jit(solution)/shard_map/pallas_call | solution.py:410
  20.6 0.0 copy-start.7
  20.6 2.1 %collective-permute-done.3 = f32[2,64,256]{2,1,0:T(8,128)S(1)} collective-permute-done((f32[2,64,256]{2,1,0:T(8,128)S(1)}, f32[2,64,256]{2,1,0:T(8,128)S(1)}, u32[]{:S(2)}, u32[]{:S(2)}) %collective-permute-start.3) | collective-permute-done | bytes 131104 | tf_op jit(solution)/shard_map/ppermute | solution.py:467
  22.8 1.3 %collective-permute-start.5 = (f32[2,64,256]{2,1,0:T(8,128)S(1)}, f32[2,64,256]{2,1,0:T(8,128)S(1)}, u32[]{:S(2)}, u32[]{:S(2)}) collective-permute-start(f32[2,64,256]{2,1,0:T(8,128)S(1)} %add.3.sum_a), channel_id=1, source_target_pairs={{0,3},{1,2},{2,1},{3,0},{16,17},{17,16},{18,19},{19,18},{32,35},{3... | collective-permute-start | bytes 393224 | tf_op jit(solution)/shard_map/ppermute | solution.py:470
  24.0 2.7 %collective-permute-start.6 = (f32[16,64,256]{2,1,0:T(8,128)S(1)}, f32[16,64,256]{2,1,0:T(8,128)S(1)}, u32[]{:S(2)}, u32[]{:S(2)}) collective-permute-start(f32[16,64,256]{2,1,0:T(8,128)S(1)} %get-tuple-element.48), channel_id=1, source_target_pairs={{0,16},{16,0},{32,48},{48,32},{64,80},{80,64},{96,112},{112,96},{1... | collective-permute-start | bytes 3145736 | tf_op jit(solution)/shard_map/ppermute | solution.py:478
  26.7 3.8 %collective-permute-start.7 = (f32[16,64,256]{2,1,0:T(8,128)S(1)}, f32[16,64,256]{2,1,0:T(8,128)S(1)}, u32[]{:S(2)}, u32[]{:S(2)}) collective-permute-start(f32[16,64,256]{2,1,0:T(8,128)S(1)} %get-tuple-element.50), channel_id=1, source_target_pairs={{16,32},{32,16},{17,33},{33,17},{18,34},{34,18},{19,35},{35,19},{4... | collective-permute-start | bytes 3145736 | tf_op jit(solution)/shard_map/ppermute | solution.py:477
  30.6 0.0 copy-start.14
  30.6 0.0 copy-start.16
  30.7 0.6 %shard_map.227 = (f32[64,384]{1,0:T(8,128)S(1)}, f32[64,384]{1,0:T(8,128)S(1)}, f32[64,384]{1,0:T(8,128)S(1)}, f32[80,384]{1,0:T(8,128)S(1)}, f32[2,64,256]{2,1,0:T(8,128)S(1)}) custom-call(f32[2,64,256]{2,1,0:T(8,128)S(1)} %add.3.sum_a, f32[2,64,256]{2,1,0:T(8,128)S(1)} %collective-permute-done.5.sum_b, f32[2,64,256]{2,1,0:T(8,128)S(1)} %get-tuple-element.45.base, ...), custom_call_target="tpu_custom_call" | custom-call | flops 99999997952 | bytes 200000000 | tf_op jit(solution)/shard_map/pallas_call | solution.py:410
  31.3 1.9 %collective-permute-start.9 = (f32[80,384]{1,0:T(8,128)S(1)}, f32[80,384]{1,0:T(8,128)S(1)}, u32[]{:S(2)}, u32[]{:S(2)}) collective-permute-start(f32[80,384]{1,0:T(8,128)S(1)} %get-tuple-element.52), channel_id=1, source_target_pairs={{0,12},{4,0},{8,4},{12,8},{1,13},{5,1},{9,5},{13,9},{2,14},{6,2},{... | collective-permute-start | bytes 368648 | tf_op jit(solution)/shard_map/ppermute | solution.py:422
  33.2 1.5 %collective-permute-start.11 = (f32[64,384]{1,0:T(8,128)S(1)}, f32[64,384]{1,0:T(8,128)S(1)}, u32[]{:S(2)}, u32[]{:S(2)}) collective-permute-start(f32[64,384]{1,0:T(8,128)S(1)} %get-tuple-element.59), channel_id=1, source_target_pairs={{0,8},{4,12},{8,0},{12,4},{1,9},{5,13},{9,1},{13,5},{2,10},{6,14},... | collective-permute-start | bytes 294920 | tf_op jit(solution)/shard_map/ppermute | solution.py:422
  34.7 3.5 %collective-permute-start.8 = (f32[2,64,256]{2,1,0:T(8,128)S(1)}, f32[2,64,256]{2,1,0:T(8,128)S(1)}, u32[]{:S(2)}, u32[]{:S(2)}) collective-permute-start(f32[2,64,256]{2,1,0:T(8,128)S(1)} %get-tuple-element.51.z), channel_id=1, source_target_pairs={{16,0},{32,16},{48,32},{64,48},{80,64},{96,80},{112,96},{128,112},... | collective-permute-start | bytes 393224 | tf_op jit(solution)/shard_map/ppermute | solution.py:486
  38.2 1.2 %collective-permute-done.10.b1 = f32[64,384]{1,0:T(8,128)S(1)} collective-permute-done((f32[64,384]{1,0:T(8,128)S(1)}, f32[64,384]{1,0:T(8,128)S(1)}, u32[]{:S(2)}, u32[]{:S(2)}) %collective-permute-start.10) | collective-permute-done | bytes 98336 | tf_op jit(solution)/shard_map/ppermute | solution.py:422
  39.4 1.3 %shard_map.229 = f32[6,64,256]{2,1,0:T(8,128)} custom-call(f32[64,384]{1,0:T(8,128)S(1)} %get-tuple-element.57.b0, f32[64,384]{1,0:T(8,128)S(1)} %collective-permute-done.10.b1, f32[64,384]{1,0:T(8,128)S(1)} %collective-permute-done.11.b2, f32[80,384]{1,0:T(8,128)S(1)} %collective-permute-done.9.n3.b3, bf16[512,512]{1,0:T(8,128)(2,1)S(1)} %copy-done.14, ...), custom_call_target="tpu_custom_call" | custom-call | flops 2000000000 | bytes 4000000 | tf_op jit(solution)/shard_map/pallas_call | solution.py:410
  40.7 2.3 %collective-permute-done.7.from_chip = f32[16,64,256]{2,1,0:T(8,128)S(1)} collective-permute-done((f32[16,64,256]{2,1,0:T(8,128)S(1)}, f32[16,64,256]{2,1,0:T(8,128)S(1)}, u32[]{:S(2)}, u32[]{:S(2)}) %collective-permute-start.7) | collective-permute-done | bytes 1048608 | tf_op jit(solution)/shard_map/ppermute | solution.py:477
  43.0 1.4 %collective-permute-done.8.z_in = f32[2,64,256]{2,1,0:T(8,128)S(1)} collective-permute-done((f32[2,64,256]{2,1,0:T(8,128)S(1)}, f32[2,64,256]{2,1,0:T(8,128)S(1)}, u32[]{:S(2)}, u32[]{:S(2)}) %collective-permute-start.8) | collective-permute-done | bytes 131104 | tf_op jit(solution)/shard_map/ppermute | solution.py:486
  44.5 2.1 %shard_map.228 = (f32[2,64,256]{2,1,0:T(8,128)}, f32[2,64,256]{2,1,0:T(8,128)}, f32[6,64,256]{2,1,0:T(8,128)}, f32[6,64,256]{2,1,0:T(8,128)}, f32[6,64,256]{2,1,...) custom-call(f32[2,64,256]{2,1,0:T(8,128)S(1)} %bitcast.61, ...), custom_call_target="tpu_custom_call" | custom-call | flops 500 | bytes 1 | tf_op jit(solution)/shard_map/pallas_call | solution.py:410
  (34 shorter events, 0.1 us)
Async XLA Ops:
  0.6 7.8 %copy-start = (f32[6,2,1,64,256]{4,3,2,1,0:T(8,128)S(1)}, f32[6,2,1,64,256]{4,3,2,1,0:T(8,128)}, u32[]{:S(2)}) copy-start(f32[6,2,1,64,256]{4,3,2,1,0:T(8,128)} %param.23) | copy-start | bytes 2359300
  0.7 7.8 %copy-start.1 = (f32[6,2,1,64,256]{4,3,2,1,0:T(8,128)S(1)}, f32[6,2,1,64,256]{4,3,2,1,0:T(8,128)}, u32[]{:S(2)}) copy-start(f32[6,2,1,64,256]{4,3,2,1,0:T(8,128)} %param.24) | copy-start | bytes 2359300
  0.7 7.8 %copy-start.2 = (f32[3,2,1,64,256]{4,3,2,1,0:T(8,128)S(1)}, f32[3,2,1,64,256]{4,3,2,1,0:T(8,128)}, u32[]{:S(2)}) copy-start(f32[3,2,1,64,256]{4,3,2,1,0:T(8,128)} %param.21) | copy-start | bytes 1179652
  0.7 7.8 %copy-start.3 = (f32[3,2,1,64,256]{4,3,2,1,0:T(8,128)S(1)}, f32[3,2,1,64,256]{4,3,2,1,0:T(8,128)}, u32[]{:S(2)}) copy-start(f32[3,2,1,64,256]{4,3,2,1,0:T(8,128)} %param.22) | copy-start | bytes 1179652
  2.7 10.9 %collective-permute-start = (f32[80,384]{1,0:T(8,128)S(1)}, f32[80,384]{1,0:T(8,128)S(1)}, u32[]{:S(2)}, u32[]{:S(2)}) collective-permute-start(f32[80,384]{1,0:T(8,128)S(1)} %get-tuple-element.38), channel_id=1, source_target_pairs={{0,4},{4,8},{8,12},{12,0},{1,5},{5,9},{9,13},{13,1},{2,6},{6,10},{... | collective-permute-start | bytes 368648 | tf_op jit(solution)/shard_map/ppermute | solution.py:422
  4.9 8.8 %collective-permute-start.1 = (f32[64,384]{1,0:T(8,128)S(1)}, f32[64,384]{1,0:T(8,128)S(1)}, u32[]{:S(2)}, u32[]{:S(2)}) collective-permute-start(f32[64,384]{1,0:T(8,128)S(1)} %get-tuple-element.39), channel_id=1, source_target_pairs={{0,8},{4,12},{8,0},{12,4},{1,9},{5,13},{9,1},{13,5},{2,10},{6,14},... | collective-permute-start | bytes 294920 | tf_op jit(solution)/shard_map/ppermute | solution.py:422
  7.3 6.3 %collective-permute-start.2 = (f32[64,384]{1,0:T(8,128)S(1)}, f32[64,384]{1,0:T(8,128)S(1)}, u32[]{:S(2)}, u32[]{:S(2)}) collective-permute-start(f32[64,384]{1,0:T(8,128)S(1)} %get-tuple-element.40), channel_id=1, source_target_pairs={{0,12},{4,0},{8,4},{12,8},{1,13},{5,1},{9,5},{13,9},{2,14},{6,2},{... | collective-permute-start | bytes 294920 | tf_op jit(solution)/shard_map/ppermute | solution.py:422
  8.5 5.2 %copy-start.11 = (f32[2,3,64,256]{3,2,1,0:T(8,128)S(1)}, f32[2,3,64,256]{3,2,1,0:T(8,128)}, u32[]{:S(2)}) copy-start(f32[2,3,64,256]{3,2,1,0:T(8,128)} %param.26) | copy-start | bytes 1179652
  8.5 5.2 %copy-start.13 = (bf16[512,512]{1,0:T(8,128)(2,1)S(1)}, bf16[512,512]{1,0:T(8,128)(2,1)}, u32[]{:S(2)}) copy-start(bf16[512,512]{1,0:T(8,128)(2,1)} %constant.10.clone.th_ref) | copy-start | bytes 1572868
  8.5 5.2 %copy-start.15 = (bf16[512,512]{1,0:T(8,128)(2,1)S(1)}, bf16[512,512]{1,0:T(8,128)(2,1)}, u32[]{:S(2)}) copy-start(bf16[512,512]{1,0:T(8,128)(2,1)} %constant.11.clone.tl_ref) | copy-start | bytes 1572868
  8.5 10.9 %collective-permute-start.4 = (f32[144,256]{1,0:T(8,128)S(1)}, f32[144,256]{1,0:T(8,128)S(1)}, u32[]{:S(2)}, u32[]{:S(2)}) collective-permute-start(f32[144,256]{1,0:T(8,128)S(1)} %shard_map.225), channel_id=1, source_target_pairs={{0,16},{16,32},{32,48},{48,64},{64,80},{80,96},{96,112},{112,128},... | collective-permute-start | bytes 442376 | tf_op jit(solution)/shard_map/ppermute | solution.py:454
  13.7 5.8 %copy-start.5 = (f32[3,2,1,64,256]{4,3,2,1,0:T(8,128)S(1)}, f32[3,2,1,64,256]{4,3,2,1,0:T(8,128)}, u32[]{:S(2)}) copy-start(f32[3,2,1,64,256]{4,3,2,1,0:T(8,128)} %param.18) | copy-start | bytes 1179652
  13.7 5.8 %copy-start.6 = (f32[3,2,1,64,256]{4,3,2,1,0:T(8,128)S(1)}, f32[3,2,1,64,256]{4,3,2,1,0:T(8,128)}, u32[]{:S(2)}) copy-start(f32[3,2,1,64,256]{4,3,2,1,0:T(8,128)} %param.19) | copy-start | bytes 1179652
  13.7 5.8 %copy-start.9 = (f32[2,1,64,256]{3,2,1,0:T(8,128)S(1)}, f32[2,1,64,256]{3,2,1,0:T(8,128)}, u32[]{:S(2)}) copy-start(f32[2,1,64,256]{3,2,1,0:T(8,128)} %param.16) | copy-start | bytes 393220
  13.7 5.8 %copy-start.10 = (f32[2,1,64,256]{3,2,1,0:T(8,128)S(1)}, f32[2,1,64,256]{3,2,1,0:T(8,128)}, u32[]{:S(2)}) copy-start(f32[2,1,64,256]{3,2,1,0:T(8,128)} %param.17) | copy-start | bytes 393220
  14.3 8.5 %collective-permute-start.3 = (f32[2,64,256]{2,1,0:T(8,128)S(1)}, f32[2,64,256]{2,1,0:T(8,128)S(1)}, u32[]{:S(2)}, u32[]{:S(2)}) collective-permute-start(f32[2,64,256]{2,1,0:T(8,128)S(1)} %shard_map.224.order), channel_id=1, source_target_pairs={{0,1},{1,0},{2,3},{3,2},{16,19},{17,18},{18,17},{19,16},{32,33},{3... | collective-permute-start | bytes 393224 | tf_op jit(solution)/shard_map/ppermute | solution.py:467
  19.5 11.1 %copy-start.8 = (bf16[256,512]{1,0:T(8,128)(2,1)S(1)}, bf16[256,512]{1,0:T(8,128)(2,1)}, u32[]{:S(2)}) copy-start(bf16[256,512]{1,0:T(8,128)(2,1)} %constant.9.clone.tl_hbm.tl_ref) | copy-start | bytes 786436
  20.6 10.0 %copy-start.7 = (bf16[256,512]{1,0:T(8,128)(2,1)S(1)}, bf16[256,512]{1,0:T(8,128)(2,1)}, u32[]{:S(2)}) copy-start(bf16[256,512]{1,0:T(8,128)(2,1)} %constant.8.clone.th_hbm.th_ref) | copy-start | bytes 786436
  22.8 7.8 %collective-permute-start.5 = (f32[2,64,256]{2,1,0:T(8,128)S(1)}, f32[2,64,256]{2,1,0:T(8,128)S(1)}, u32[]{:S(2)}, u32[]{:S(2)}) collective-permute-start(f32[2,64,256]{2,1,0:T(8,128)S(1)} %add.3.sum_a), channel_id=1, source_target_pairs={{0,3},{1,2},{2,1},{3,0},{16,17},{17,16},{18,19},{19,18},{32,35},{3... | collective-permute-start | bytes 393224 | tf_op jit(solution)/shard_map/ppermute | solution.py:470
  24.0 10.6 %collective-permute-start.6 = (f32[16,64,256]{2,1,0:T(8,128)S(1)}, f32[16,64,256]{2,1,0:T(8,128)S(1)}, u32[]{:S(2)}, u32[]{:S(2)}) collective-permute-start(f32[16,64,256]{2,1,0:T(8,128)S(1)} %get-tuple-element.48), channel_id=1, source_target_pairs={{0,16},{16,0},{32,48},{48,32},{64,80},{80,64},{96,112},{112,96},{1... | collective-permute-start | bytes 3145736 | tf_op jit(solution)/shard_map/ppermute | solution.py:478
  26.7 16.3 %collective-permute-start.7 = (f32[16,64,256]{2,1,0:T(8,128)S(1)}, f32[16,64,256]{2,1,0:T(8,128)S(1)}, u32[]{:S(2)}, u32[]{:S(2)}) collective-permute-start(f32[16,64,256]{2,1,0:T(8,128)S(1)} %get-tuple-element.50), channel_id=1, source_target_pairs={{16,32},{32,16},{17,33},{33,17},{18,34},{34,18},{19,35},{35,19},{4... | collective-permute-start | bytes 3145736 | tf_op jit(solution)/shard_map/ppermute | solution.py:477
  30.6 8.8 %copy-start.4 = (f32[2,1,3,64,256]{4,3,2,1,0:T(8,128)S(1)}, f32[2,1,3,64,256]{4,3,2,1,0:T(8,128)}, u32[]{:S(2)}) copy-start(f32[2,1,3,64,256]{4,3,2,1,0:T(8,128)} %param.20) | copy-start | bytes 1179652
  30.6 8.8 %copy-start.12 = (f32[2,1,3,64,256]{4,3,2,1,0:T(8,128)S(1)}, f32[2,1,3,64,256]{4,3,2,1,0:T(8,128)}, u32[]{:S(2)}) copy-start(f32[2,1,3,64,256]{4,3,2,1,0:T(8,128)} %param.25) | copy-start | bytes 1179652
  30.6 8.8 %copy-start.14 = (bf16[512,512]{1,0:T(8,128)(2,1)S(1)}, bf16[512,512]{1,0:T(8,128)(2,1)}, u32[]{:S(2)}) copy-start(bf16[512,512]{1,0:T(8,128)(2,1)} %constant.10.clone.th_ref) | copy-start | bytes 1572868
  30.6 8.8 %copy-start.16 = (bf16[512,512]{1,0:T(8,128)(2,1)S(1)}, bf16[512,512]{1,0:T(8,128)(2,1)}, u32[]{:S(2)}) copy-start(bf16[512,512]{1,0:T(8,128)(2,1)} %constant.11.clone.tl_ref) | copy-start | bytes 1572868
  31.3 8.1 %collective-permute-start.9 = (f32[80,384]{1,0:T(8,128)S(1)}, f32[80,384]{1,0:T(8,128)S(1)}, u32[]{:S(2)}, u32[]{:S(2)}) collective-permute-start(f32[80,384]{1,0:T(8,128)S(1)} %get-tuple-element.52), channel_id=1, source_target_pairs={{0,12},{4,0},{8,4},{12,8},{1,13},{5,1},{9,5},{13,9},{2,14},{6,2},{... | collective-permute-start | bytes 368648 | tf_op jit(solution)/shard_map/ppermute | solution.py:422
  33.2 6.2 %collective-permute-start.10 = (f32[64,384]{1,0:T(8,128)S(1)}, f32[64,384]{1,0:T(8,128)S(1)}, u32[]{:S(2)}, u32[]{:S(2)}) collective-permute-start(f32[64,384]{1,0:T(8,128)S(1)} %get-tuple-element.58), channel_id=1, source_target_pairs={{0,4},{4,8},{8,12},{12,0},{1,5},{5,9},{9,13},{13,1},{2,6},{6,10},{... | collective-permute-start | bytes 294920 | tf_op jit(solution)/shard_map/ppermute | solution.py:422
  33.2 6.2 %collective-permute-start.11 = (f32[64,384]{1,0:T(8,128)S(1)}, f32[64,384]{1,0:T(8,128)S(1)}, u32[]{:S(2)}, u32[]{:S(2)}) collective-permute-start(f32[64,384]{1,0:T(8,128)S(1)} %get-tuple-element.59), channel_id=1, source_target_pairs={{0,8},{4,12},{8,0},{12,4},{1,9},{5,13},{9,1},{13,5},{2,10},{6,14},... | collective-permute-start | bytes 294920 | tf_op jit(solution)/shard_map/ppermute | solution.py:422
  34.7 9.8 %collective-permute-start.8 = (f32[2,64,256]{2,1,0:T(8,128)S(1)}, f32[2,64,256]{2,1,0:T(8,128)S(1)}, u32[]{:S(2)}, u32[]{:S(2)}) collective-permute-start(f32[2,64,256]{2,1,0:T(8,128)S(1)} %get-tuple-element.51.z), channel_id=1, source_target_pairs={{16,0},{32,16},{48,32},{64,48},{80,64},{96,80},{112,96},{128,112},... | collective-permute-start | bytes 393224 | tf_op jit(solution)/shard_map/ppermute | solution.py:486

commit v4 on v3

--- a/solution.py
+++ b/solution.py
@@ -135,8 +135,12 @@
         o1[BLOCK + plane : BLOCK + plane + 1, 0:LENGTH] = ends[plane, 7:8, :]
 
 
+def rows_at(start):
+    return pl.ds(start if isinstance(start, int) else pl.multiple_of(start, 8), 8)
+
+
 def chunk(ref, plane, i):
-    return ref[plane, pl.ds(i * 8 if isinstance(i, int) else pl.multiple_of(i * 8, 8), 8), :]
+    return ref[plane, rows_at(i * 8), :]
 
 
 def pack_kernel(g1, g2, s1, s2, order, q_first):
@@ -149,7 +153,7 @@
             q_first[place : place + 1, :] = time_term(lambda k: tops[k], field)
 
 
-def plain_kernel(img, spl, v1, v2, g1, g2, s1, s2, b1, q_first, order, w_out, image_out, tops, to_core, to_chip):
+def plain_kernel(img, spl, v1, v2, g1, g2, s1, s2, b1, q_first, order, w_out, image_out, tops, q0_out, to_core, to_chip):
     odd = lax.rem(lax.axis_index("tm"), 2)
     row = lax.axis_index("row")
     keep_time = (lax.axis_index("tm") != lax.axis_size("tm") - 1).astype(F32)
@@ -186,6 +190,7 @@
             image = chunk(img, reim, i) - 2.0 * TAU * one
             other = chunk(spl, reim, i) - 2.0 * TAU * (two - one)
             before = q_first[pl.ds(pl.multiple_of(BLOCK * reim + i * 8, 8), 8), :]
+            put(q0_out, reim, before)
             put(image_out, reim, image - 2.0 * TAU * BETA_ONE * before)
             put(w_out, reim, image - other)
             put(w_out, 2 + reim, other)
@@ -206,9 +211,9 @@
         tops[plane : plane + 1, :] = w_out[plane, 0:1, :] + q_first[place : place + 1, :]
 
     def messages(q_to, w_to):
-        for index, (name, part) in enumerate(TIME_PARTS):
+        for index, (name, part) in enumerate(TIME_PARTS[1:]):
             q_to[2 * index : 2 * index + 2] = refs[name][2 * part : 2 * part + 2]
-        w_to[...] = w_out[...]
+        w_to[...] = w_out[2:]
 
     pl.when(odd == 0)(lambda: messages(to_core, to_chip))
     pl.when(odd == 1)(lambda: messages(to_chip, to_core))
@@ -238,12 +243,12 @@
     return (-2.0 * TAU * beta * (1.0 if field in (2, 5) else 0.5)) * q(field)
 
 
-def predict_kernel(sum_a, sum_b, base, tops, th_ref, tl_ref, sens, o0, o1, o2, o3, z_out):
+def predict_kernel(sum_a, sum_b, base, tops, w, th_ref, tl_ref, sens, o0, o1, o2, o3, z_out):
     row = lax.axis_index("row")
     image = []
     for reim in range(2):
         back = sum_a[reim] + sum_b[reim]
-        z_out[reim] = back
+        z_out[reim] = w[reim] - 2.0 * TAU * back
         image.append(base[reim] - 2.0 * TAU * back)
     parts = []
     for c in range(COIL):
@@ -277,15 +282,65 @@
         copy.wait()
 
 
+def along_rows(bar, plane, i):
+    here = chunk(bar, plane, i)
+    below = chunk(bar, plane, i + 1)
+    rows = iota((8, LENGTH), 0)
+    return jnp.where(rows == 7, pltpu.roll(below, 7, 0), pltpu.roll(here, 7, 0)) - here
+
+
+def along_cols(bar, plane, i):
+    here = chunk(bar, plane, i)
+    cols = iota((8, LENGTH), 1)
+    return jnp.where(cols == LENGTH - 1, 0.0, pltpu.roll(here, LENGTH - 1, 1) - here)
+
+
+def project(out, duals, radius, i):
+    total = duals[0] * duals[0]
+    for value in duals[1:]:
+        total += value * value
+    scale = jnp.minimum(1.0, radius * lax.rsqrt(total))
+    for plane, value in enumerate(duals):
+        out[plane, 8 * i : 8 * i + 8, :] = value * scale
+
+
+def by_frame(run, from_core, from_chip):
+    odd = lax.rem(lax.axis_index("tm"), 2)
+    pl.when(odd == 0)(lambda: run(from_chip, from_core))
+    pl.when(odd == 1)(lambda: run(from_core, from_chip))
+
+
+def fill_below(bar, n3, first_plane, count):
+    row = lax.axis_index("row")
+    for plane in range(count):
+        place = BLOCK + first_plane + plane
+        bar[plane, BLOCK : BLOCK + 1, :] = jnp.where(
+            row == ROWS - 1, bar[plane, BLOCK - 1 : BLOCK, :], n3[place : place + 1, 0:LENGTH]
+        )
+
+
+def in_parts(second, pairs, copies, sems):
+    for part in range(4):
+        rows = pl.ds(16 * part, 16)
+        second(2 * part)
+        second(2 * part + 1)
+        for k, (source, target) in enumerate(pairs):
+            copy = pltpu.make_async_copy(source.at[:, rows, :], target.at[:, rows, :], sems.at[4 + 4 * part + k])
+            copy.start()
+            copies.append(copy)
+    for copy in copies:
+        copy.wait()
+
+
 def fields_kernel(
-    img, spl, v1, v2, g1, g2, s1, s2, w, from_core, from_chip, z, z_in, n3,
+    img, spl, v1, v2, g1, g2, s1, s2, w, q0, from_core, from_chip, z, z_in, n3,
     img_hbm, spl_hbm, v1_hbm, v2_hbm, g1_hbm, g2_hbm, s1_hbm, s2_hbm,
     bar, img_out, spl_out, v1_out, v2_out, g1_out, g2_out, s1_out, s2_out, sems,
 ):
+    keep_time = (lax.axis_index("tm") != lax.axis_size("tm") - 1).astype(F32)
+    refs = dict(g1=g1, g2=g2, s1=s1, s2=s2)
+
     def run(q_in, w_in):
-        row = lax.axis_index("row")
-        keep_time = (lax.axis_index("tm") != lax.axis_size("tm") - 1).astype(F32)
-        refs = dict(g1=g1, g2=g2, s1=s1, s2=s2)
         copies = [
             pltpu.make_async_copy(source, target, sems.at[k])
             for k, (source, target) in enumerate(
@@ -293,113 +348,74 @@
             )
         ]
 
-        def span(i):
-            return pl.ds(i * 8 if isinstance(i, int) else pl.multiple_of(i * 8, 8), 8)
-
         def first(i, carry):
             for reim in range(2):
 
-                def before(k):
-                    return chunk(q_in, 2 * k + reim, i)
+                def before(f):
+                    return chunk(q0, reim, i) if f == 0 else chunk(q_in, 2 * (f - 1) + reim, i)
 
                 values = []
                 for field in range(8):
                     plane = 2 * field + reim
-                    value = chunk(w, plane, i) + time_term(before, field)
-                    if field == 0:
-                        value -= 2.0 * TAU * chunk(z, reim, i)
-                    bar[plane, span(i), :] = value
-                    values.append(value)
-                img_out[reim, span(i), :] = 0.5 * (values[0] + values[1] + chunk(img, reim, i))
-                spl_out[reim, span(i), :] = 0.5 * (values[1] + chunk(spl, reim, i))
+                    start = chunk(w, plane, i) if field else chunk(z, reim, i)
+                    values.append(start + time_term(before, field))
+                    bar[plane, rows_at(8 * i), :] = values[-1]
+                img_out[reim, rows_at(8 * i), :] = 0.5 * (values[0] + values[1] + chunk(img, reim, i))
+                spl_out[reim, rows_at(8 * i), :] = 0.5 * (values[1] + chunk(spl, reim, i))
                 for k in range(3):
                     plane = 2 * k + reim
-                    v1_out[plane, span(i), :] = 0.5 * (values[2 + k] + chunk(v1, plane, i))
-                    v2_out[plane, span(i), :] = 0.5 * (values[5 + k] + chunk(v2, plane, i))
+                    v1_out[plane, rows_at(8 * i), :] = 0.5 * (values[2 + k] + chunk(v1, plane, i))
+                    v2_out[plane, rows_at(8 * i), :] = 0.5 * (values[5 + k] + chunk(v2, plane, i))
             return carry
 
         lax.fori_loop(0, 8, first, 0, unroll=2)
         for copy in copies:
             copy.start()
-        for plane in range(16):
-            below = n3[BLOCK + plane : BLOCK + plane + 1, 0:LENGTH]
-            bar[plane, BLOCK : BLOCK + 1, :] = jnp.where(row == ROWS - 1, bar[plane, BLOCK - 1 : BLOCK, :], below)
-
-        def along_rows(plane, i):
-            here = chunk(bar, plane, i)
-            below = chunk(bar, plane, i + 1)
-            rows = iota((8, LENGTH), 0)
-            return jnp.where(rows == 7, pltpu.roll(below, 7, 0), pltpu.roll(here, 7, 0)) - here
-
-        def along_cols(plane, i):
-            here = chunk(bar, plane, i)
-            cols = iota((8, LENGTH), 1)
-            return jnp.where(cols == LENGTH - 1, 0.0, pltpu.roll(here, LENGTH - 1, 1) - here)
+        fill_below(bar, n3, 0, 16)
 
         def along_time(field, reim, i):
             plane = 2 * field + reim
-            value = chunk(w_in, plane, i)
-            value += time_term(lambda k: chunk(refs[TIME_PARTS[k][0]], 2 * TIME_PARTS[k][1] + reim, i), field)
-            if field == 0:
-                value -= 2.0 * TAU * chunk(z_in, reim, i)
-            return value - chunk(bar, plane, i)
-
-        def project(out, duals, radius, i):
-            total = duals[0] * duals[0]
-            for value in duals[1:]:
-                total += value * value
-            scale = jnp.minimum(1.0, radius * lax.rsqrt(total))
-            for plane, value in enumerate(duals):
-                out[plane, span(i), :] = value * scale
-
-        def gradient(i, dual, out, field, vec, beta):
-            duals = []
-            for k in range(3):
+
+            def own(f):
+                name, part = TIME_PARTS[f]
+                return chunk(refs[name], 2 * part + reim, i)
+
+            ahead = chunk(w_in, plane - 2, i) if field else chunk(z_in, reim, i)
+            return ahead + time_term(own, field) - chunk(bar, plane, i)
+
+        def second(i):
+            for dual, out, field, beta in ((g1, g1_out, 0, BETA_ONE), (g2, g2_out, 1, BETA_TWO)):
+                duals = []
+                for k in range(3):
+                    for reim in range(2):
+                        if k == 0:
+                            diff = (beta * keep_time) * along_time(field, reim, i)
+                        else:
+                            diff = (along_rows, along_cols)[k - 1](bar, 2 * field + reim, i)
+                        diff -= chunk(bar, 2 * (2 + 3 * field + k) + reim, i)
+                        duals.append(chunk(dual, 2 * k + reim, i) + SIGMA * diff)
+                project(out, duals, ALPHA_ONE, i)
+            for dual, out, vec, beta in ((s1, s1_out, 2, BETA_ONE), (s2, s2_out, 5, BETA_TWO)):
+                duals = [None] * 12
+                factor = SIGMA * beta * keep_time
                 for reim in range(2):
-                    if k == 0:
-                        diff = (beta * keep_time) * along_time(field, reim, i)
-                    else:
-                        diff = (along_rows, along_cols)[k - 1](2 * field + reim, i)
-                    diff -= chunk(bar, 2 * (vec + k) + reim, i)
-                    duals.append(chunk(dual, 2 * k + reim, i) + SIGMA * diff)
-            project(out, duals, ALPHA_ONE, i)
-
-        def symmetric(i, dual, out, vec, beta):
-            duals = [None] * 12
-            for reim in range(2):
-                p0, p1, p2 = (2 * (vec + k) + reim for k in range(3))
-                steps = (
-                    (SIGMA * beta * keep_time) * along_time(vec, reim, i),
-                    SIGMA * along_rows(p1, i),
-                    SIGMA * along_cols(p2, i),
-                    0.5 * SIGMA * along_rows(p0, i) + (0.5 * SIGMA * beta * keep_time) * along_time(vec + 1, reim, i),
-                    0.5 * SIGMA * along_cols(p0, i) + (0.5 * SIGMA * beta * keep_time) * along_time(vec + 2, reim, i),
-                    0.5 * SIGMA * (along_cols(p1, i) + along_rows(p2, i)),
-                )
-                for k, diff in enumerate(steps):
-                    duals[2 * k + reim] = chunk(dual, 2 * k + reim, i) + diff
-            project(out, duals, ALPHA_ZERO, i)
-
-        def second(i):
-            gradient(i, g1, g1_out, 0, 2, BETA_ONE)
-            gradient(i, g2, g2_out, 1, 5, BETA_TWO)
-            symmetric(i, s1, s1_out, 2, BETA_ONE)
-            symmetric(i, s2, s2_out, 5, BETA_TWO)
-
-        for part in range(4):
-            rows = pl.ds(16 * part, 16)
-            second(2 * part)
-            second(2 * part + 1)
-            for k, (source, target) in enumerate(((g1_out, g1_hbm), (g2_out, g2_hbm), (s1_out, s1_hbm), (s2_out, s2_hbm))):
-                copy = pltpu.make_async_copy(source.at[:, rows, :], target.at[:, rows, :], sems.at[4 + 4 * part + k])
-                copy.start()
-                copies.append(copy)
-        for copy in copies:
-            copy.wait()
-
-    odd = lax.rem(lax.axis_index("tm"), 2)
-    pl.when(odd == 0)(lambda: run(from_chip, from_core))
-    pl.when(odd == 1)(lambda: run(from_core, from_chip))
+                    p0, p1, p2 = (2 * (vec + k) + reim for k in range(3))
+                    steps = (
+                        factor * along_time(vec, reim, i),
+                        SIGMA * along_rows(bar, p1, i),
+                        SIGMA * along_cols(bar, p2, i),
+                        0.5 * SIGMA * along_rows(bar, p0, i) + (0.5 * factor) * along_time(vec + 1, reim, i),
+                        0.5 * SIGMA * along_cols(bar, p0, i) + (0.5 * factor) * along_time(vec + 2, reim, i),
+                        0.5 * SIGMA * (along_cols(bar, p1, i) + along_rows(bar, p2, i)),
+                    )
+                    for k, diff in enumerate(steps):
+                        duals[2 * k + reim] = chunk(dual, 2 * k + reim, i) + diff
+                project(out, duals, ALPHA_ZERO, i)
+
+        pairs = ((g1_out, g1_hbm), (g2_out, g2_hbm), (s1_out, s1_hbm), (s2_out, s2_hbm))
+        in_parts(second, pairs, copies, sems)
+
+    by_frame(run, from_core, from_chip)
 
 
 def shape(*dims):
@@ -458,9 +474,9 @@
         [(t * groups + c, t * groups + partner[(t + turn) % 2][c]) for t in range(frames) for c in range(groups)]
         for turn in range(2)
     ]
-    stack = shape(16, BLOCK, LENGTH)
-    w_out, base, tops, to_core, to_chip = call(
-        plain_kernel, (stack, shape(2, BLOCK, LENGTH), shape(16, LENGTH), stack, stack),
+    stack, pair_of = shape(14, BLOCK, LENGTH), shape(2, BLOCK, LENGTH)
+    w_out, base, tops, q0, to_core, to_chip = call(
+        plain_kernel, (shape(16, BLOCK, LENGTH), pair_of, shape(16, LENGTH), pair_of, stack, stack),
         (img, spl, v1, v2, g1, g2, s1, s2, b1, q_first, partial), 100_000_000,
         in_specs=[pl.BlockSpec(memory_space=pltpu.VMEM)] * 10 + [pl.BlockSpec(memory_space=pl.ANY)],
     )
@@ -479,15 +495,15 @@
     c_blocks = (shape(BLOCK, 384), shape(BLOCK, 384), shape(BLOCK, 384), shape(BLOCK + 16, 384))
     c0, c1, c2, c3, z = call(
         predict_kernel, (*c_blocks, shape(2, BLOCK, LENGTH)),
-        (pair, rest, base, tops, first_high, first_low, sens), 200_000_000,
+        (pair, rest, base, tops, w_out, first_high, first_low, sens), 200_000_000,
     )
     n2, n1, n3 = turn(c2, 2), turn(c1, 1), turn(c3, 3)
     z, from_core = lax.optimization_barrier((z, from_core))
     z_in = lax.ppermute(z, "tm", [(i + 1, i) for i in range(frames - 1)])
     like = lambda x: shape(*x.shape)
-    fields = call(
+    img_new, spl_new, v1_new, v2_new, g1_new, g2_new, s1_new, s2_new = call(
         fields_kernel, tuple(map(like, (img, spl, v1, v2, g1, g2, s1, s2))),
-        (img, spl, v1, v2, g1, g2, s1, s2, w_out, from_core, from_chip, z, z_in, n3), 1,
+        (img, spl, v1, v2, g1, g2, s1, s2, w_out, q0, from_core, from_chip, z, z_in, n3), 1,
         scratch=[
             pltpu.VMEM((16, BLOCK + 8, LENGTH), F32),
             *(pltpu.VMEM(x.shape, F32) for x in (img, spl, v1, v2, g1, g2, s1, s2)),
@@ -500,7 +516,6 @@
         scratch=[pltpu.VMEM(kd.shape, F32), pltpu.SemaphoreType.DMA((2 * COIL,))],
         out_space=pltpu.HBM,
     )
-    img_new, spl_new, v1_new, v2_new, g1_new, g2_new, s1_new, s2_new = fields
     news = (img_new, spl_new, v1_new, v2_new, kspace, g1_new, g2_new, s1_new, s2_new)
     olds = (image_now, split_now, vector_one, vector_two, kspace_dual, grad_one, grad_two, sym_one, sym_two)
     return tuple(new.reshape(old.shape) for new, old in zip(news, olds))

time: 47.1 us -> 45.7 us (0.970)
  waiting for transfers between devices: 7.1 us -> 5.71 us
    ppermute x1, waiting for transfers between devices: 2.32 us -> 0.9 us  [body(): from_chip = lax.ppermute(to_chip, ('tm', 'coil'), pairs)]
where the time goes in v4:
time: 45.7 us; the launch traced here: 45.2 us
  starting transfers between devices  30.7 us (67%)
  Pallas kernels  7.72 us (17%)
  waiting for transfers between devices  5.71 us (12%)
  between operations  0.98 us (2%)
    ppermute x6, starting transfers between devices, turn(): lax.ppermute(block, 'row', [(i, (i + distance) % ROWS) for i in range(ROW...  9.1 us
    pallas_call x7, Pallas kernels, call(): pl.pallas_call(kernel, out_shape=outs, in_specs=in_specs or [pl.BlockSpec...  7.72 us
    ppermute x1, starting transfers between devices, body(): received = lax.ppermute(partial, ('tm', 'coil'), swaps[0])  5.21 us
    ppermute x1, starting transfers between devices, body(): q_first = lax.ppermute(q_first, 'tm', after)  5.08 us
    ppermute x1, starting transfers between devices, body(): from_chip = lax.ppermute(to_chip, ('tm', 'coil'), pairs)  3.83 us
    ppermute x1, starting transfers between devices, body(): z_in = lax.ppermute(z, 'tm', [(i + 1, i) for i in range(frames - 1)])  3.5 us
    ppermute x1, starting transfers between devices, body(): from_core = lax.ppermute(to_core, 'tm', [(t, t ^ 1) for t in range(frames)])  2.71 us
    ppermute x1, waiting for transfers between devices, body(): received = lax.ppermute(partial, ('tm', 'coil'), swaps[0])  2.14 us
  transfers between devices with their start and end apart: 12, of which 4 were waited for; matrix products, arithmetic and copies ran while one was open for 0% of the time, Pallas kernels for 8%

profile of v4, /device:TPU:1, one launch (start us, length us, event | category | flops | bytes accessed | tf_op | source)
XLA Modules:
  0.0 45.2 jit_solution(11176728117382092755)
XLA Ops:
  0.7 2.0 %shard_map.223 = (f32[64,384]{1,0:T(8,128)S(1)}, f32[80,384]{1,0:T(8,128)S(1)}, f32[64,384]{1,0:T(8,128)S(1)}, f32[64,384]{1,0:T(8,128)S(1)}, f32[1,256]{1,0:T(1,128)S(1)}) custom-call(f32[6,64,256]{2,1,0:T(8,128)} %bitcast.54, s32[1,256]{1,0:T(1,128)} %lines_hbm.1, bf16[256,512]{1,0:T(8,128)(2,1)} %constant.8.clone.th_hbm.th_ref, ...), custom_call_target="tpu_custom_call" | custom-call | flops 500 | bytes 1 | tf_op jit(solution)/shard_map/pallas_call | solution.py:426
  2.7 2.1 %collective-permute-start = (f32[80,384]{1,0:T(8,128)S(1)}, f32[80,384]{1,0:T(8,128)S(1)}, u32[]{:S(2)}, u32[]{:S(2)}) collective-permute-start(f32[80,384]{1,0:T(8,128)S(1)} %get-tuple-element.39), channel_id=1, source_target_pairs={{0,4},{4,8},{8,12},{12,0},{1,5},{5,9},{9,13},{13,1},{2,6},{6,10},{... | collective-permute-start | bytes 368648 | tf_op jit(solution)/shard_map/ppermute | solution.py:438
  4.9 2.4 %collective-permute-start.1 = (f32[64,384]{1,0:T(8,128)S(1)}, f32[64,384]{1,0:T(8,128)S(1)}, u32[]{:S(2)}, u32[]{:S(2)}) collective-permute-start(f32[64,384]{1,0:T(8,128)S(1)} %get-tuple-element.40), channel_id=1, source_target_pairs={{0,8},{4,12},{8,0},{12,4},{1,9},{5,13},{9,1},{13,5},{2,10},{6,14},... | collective-permute-start | bytes 294920 | tf_op jit(solution)/shard_map/ppermute | solution.py:438
  7.3 1.2 %collective-permute-start.2 = (f32[64,384]{1,0:T(8,128)S(1)}, f32[64,384]{1,0:T(8,128)S(1)}, u32[]{:S(2)}, u32[]{:S(2)}) collective-permute-start(f32[64,384]{1,0:T(8,128)S(1)} %get-tuple-element.41), channel_id=1, source_target_pairs={{0,12},{4,0},{8,4},{12,8},{1,13},{5,1},{9,5},{13,9},{2,14},{6,2},{... | collective-permute-start | bytes 294920 | tf_op jit(solution)/shard_map/ppermute | solution.py:438
  8.5 0.0 copy-start.11
  8.5 0.0 copy-start.13
  8.5 0.0 copy-start.15
  8.5 5.1 %collective-permute-start.4 = (f32[144,256]{1,0:T(8,128)S(1)}, f32[144,256]{1,0:T(8,128)S(1)}, u32[]{:S(2)}, u32[]{:S(2)}) collective-permute-start(f32[144,256]{1,0:T(8,128)S(1)} %shard_map.225), channel_id=1, source_target_pairs={{0,16},{16,32},{32,48},{48,64},{64,80},{80,96},{96,112},{112,128},... | collective-permute-start | bytes 442376 | tf_op jit(solution)/shard_map/ppermute | solution.py:470
  13.7 0.0 copy-start.5
  13.7 0.0 copy-start.9
  13.7 0.0 copy-start.10
  13.7 0.5 %shard_map.224.order = f32[2,64,256]{2,1,0:T(8,128)S(1)} custom-call(f32[64,384]{1,0:T(8,128)S(1)} %get-tuple-element.38.b0.order, f32[80,384]{1,0:T(8,128)S(1)} %collective-permute-done.b1, f32[64,384]{1,0:T(8,128)S(1)} %collective-permute-done.1.b2, f32[64,384]{1,0:T(8,128)S(1)} %collective-permute-done.2.b3, bf16[512,512]{1,0:T(8,128)(2,1)S(1)} %copy-done.13, ...), custom_call_target="tpu_custom_call" | custom-call | flops 99999997952 | bytes 200000000 | tf_op jit(solution)/shard_map/pallas_call | solution.py:426
  14.3 5.2 %collective-permute-start.3 = (f32[2,64,256]{2,1,0:T(8,128)S(1)}, f32[2,64,256]{2,1,0:T(8,128)S(1)}, u32[]{:S(2)}, u32[]{:S(2)}) collective-permute-start(f32[2,64,256]{2,1,0:T(8,128)S(1)} %shard_map.224.order), channel_id=1, source_target_pairs={{0,1},{1,0},{2,3},{3,2},{16,19},{17,18},{18,17},{19,16},{32,33},{3... | collective-permute-start | bytes 393224 | tf_op jit(solution)/shard_map/ppermute | solution.py:483
  19.5 0.0 copy-start.8
  19.5 1.1 %shard_map.226 = (f32[16,64,256]{2,1,0:T(8,128)S(1)}, f32[2,64,256]{2,1,0:T(8,128)S(1)}, f32[16,256]{1,0:T(8,128)S(1)}, f32[2,64,256]{2,1,0:T(8,128)S(1)}, f32[1...) custom-call(f32[2,64,256]{2,1,0:T(8,128)S(1)} %bitcast.60, f32[2,64,256]{2,1,0:T(8,128)S(1)} %bitcast.62, ...), custom_call_target="tpu_custom_call" | custom-call | flops 49999998976 | bytes 100000000 | tf_op jit(solution)/shard_map/pallas_call | solution.py:426
  20.6 0.0 copy-start.7
  20.6 2.1 %collective-permute-done.3 = f32[2,64,256]{2,1,0:T(8,128)S(1)} collective-permute-done((f32[2,64,256]{2,1,0:T(8,128)S(1)}, f32[2,64,256]{2,1,0:T(8,128)S(1)}, u32[]{:S(2)}, u32[]{:S(2)}) %collective-permute-start.3) | collective-permute-done | bytes 131104 | tf_op jit(solution)/shard_map/ppermute | solution.py:483
  22.8 1.3 %collective-permute-start.5 = (f32[2,64,256]{2,1,0:T(8,128)S(1)}, f32[2,64,256]{2,1,0:T(8,128)S(1)}, u32[]{:S(2)}, u32[]{:S(2)}) collective-permute-start(f32[2,64,256]{2,1,0:T(8,128)S(1)} %add.3.sum_a), channel_id=1, source_target_pairs={{0,3},{1,2},{2,1},{3,0},{16,17},{17,16},{18,19},{19,18},{32,35},{3... | collective-permute-start | bytes 393224 | tf_op jit(solution)/shard_map/ppermute | solution.py:486
  24.0 2.7 %collective-permute-start.6 = (f32[14,64,256]{2,1,0:T(8,128)S(1)}, f32[14,64,256]{2,1,0:T(8,128)S(1)}, u32[]{:S(2)}, u32[]{:S(2)}) collective-permute-start(f32[14,64,256]{2,1,0:T(8,128)S(1)} %get-tuple-element.50), channel_id=1, source_target_pairs={{0,16},{16,0},{32,48},{48,32},{64,80},{80,64},{96,112},{112,96},{1... | collective-permute-start | bytes 2752520 | tf_op jit(solution)/shard_map/ppermute | solution.py:494
  26.7 3.8 %collective-permute-start.7 = (f32[14,64,256]{2,1,0:T(8,128)S(1)}, f32[14,64,256]{2,1,0:T(8,128)S(1)}, u32[]{:S(2)}, u32[]{:S(2)}) collective-permute-start(f32[14,64,256]{2,1,0:T(8,128)S(1)} %get-tuple-element.52), channel_id=1, source_target_pairs={{16,32},{32,16},{17,33},{33,17},{18,34},{34,18},{19,35},{35,19},{4... | collective-permute-start | bytes 2752520 | tf_op jit(solution)/shard_map/ppermute | solution.py:493
  30.6 0.0 copy-start.12
  30.6 0.0 copy-start.14
  30.7 0.0 copy-start.16
  30.7 0.6 %shard_map.227 = (f32[64,384]{1,0:T(8,128)S(1)}, f32[64,384]{1,0:T(8,128)S(1)}, f32[64,384]{1,0:T(8,128)S(1)}, f32[80,384]{1,0:T(8,128)S(1)}, f32[2,64,256]{2,1,0:T(8,128)S(1)}) custom-call(f32[2,64,256]{2,1,0:T(8,128)S(1)} %add.3.sum_a, f32[2,64,256]{2,1,0:T(8,128)S(1)} %collective-permute-done.5.sum_b, f32[2,64,256]{2,1,0:T(8,128)S(1)} %get-tuple-element.47.base, ...), custom_call_target="tpu_custom_call" | custom-call | flops 99999997952 | bytes 200000000 | tf_op jit(solution)/shard_map/pallas_call | solution.py:426
  31.3 1.9 %collective-permute-start.9 = (f32[80,384]{1,0:T(8,128)S(1)}, f32[80,384]{1,0:T(8,128)S(1)}, u32[]{:S(2)}, u32[]{:S(2)}) collective-permute-start(f32[80,384]{1,0:T(8,128)S(1)} %get-tuple-element.54), channel_id=1, source_target_pairs={{0,12},{4,0},{8,4},{12,8},{1,13},{5,1},{9,5},{13,9},{2,14},{6,2},{... | collective-permute-start | bytes 368648 | tf_op jit(solution)/shard_map/ppermute | solution.py:438
  33.2 1.5 %collective-permute-start.11 = (f32[64,384]{1,0:T(8,128)S(1)}, f32[64,384]{1,0:T(8,128)S(1)}, u32[]{:S(2)}, u32[]{:S(2)}) collective-permute-start(f32[64,384]{1,0:T(8,128)S(1)} %get-tuple-element.61), channel_id=1, source_target_pairs={{0,8},{4,12},{8,0},{12,4},{1,9},{5,13},{9,1},{13,5},{2,10},{6,14},... | collective-permute-start | bytes 294920 | tf_op jit(solution)/shard_map/ppermute | solution.py:438
  34.7 3.5 %collective-permute-start.8 = (f32[2,64,256]{2,1,0:T(8,128)S(1)}, f32[2,64,256]{2,1,0:T(8,128)S(1)}, u32[]{:S(2)}, u32[]{:S(2)}) collective-permute-start(f32[2,64,256]{2,1,0:T(8,128)S(1)} %get-tuple-element.53.z), channel_id=1, source_target_pairs={{16,0},{32,16},{48,32},{64,48},{80,64},{96,80},{112,96},{128,112},... | collective-permute-start | bytes 393224 | tf_op jit(solution)/shard_map/ppermute | solution.py:502
  38.2 1.2 %collective-permute-done.10.b1 = f32[64,384]{1,0:T(8,128)S(1)} collective-permute-done((f32[64,384]{1,0:T(8,128)S(1)}, f32[64,384]{1,0:T(8,128)S(1)}, u32[]{:S(2)}, u32[]{:S(2)}) %collective-permute-start.10) | collective-permute-done | bytes 98336 | tf_op jit(solution)/shard_map/ppermute | solution.py:438
  39.5 1.3 %shard_map.229 = f32[6,64,256]{2,1,0:T(8,128)} custom-call(f32[64,384]{1,0:T(8,128)S(1)} %get-tuple-element.59.b0, f32[64,384]{1,0:T(8,128)S(1)} %collective-permute-done.10.b1, f32[64,384]{1,0:T(8,128)S(1)} %collective-permute-done.11.b2, f32[80,384]{1,0:T(8,128)S(1)} %collective-permute-done.9.n3.b3, bf16[512,512]{1,0:T(8,128)(2,1)S(1)} %copy-done.14, ...), custom_call_target="tpu_custom_call" | custom-call | flops 2000000000 | bytes 4000000 | tf_op jit(solution)/shard_map/pallas_call | solution.py:426
  40.7 0.9 %collective-permute-done.7.from_chip = f32[14,64,256]{2,1,0:T(8,128)S(1)} collective-permute-done((f32[14,64,256]{2,1,0:T(8,128)S(1)}, f32[14,64,256]{2,1,0:T(8,128)S(1)}, u32[]{:S(2)}, u32[]{:S(2)}) %collective-permute-start.7) | collective-permute-done | bytes 917536 | tf_op jit(solution)/shard_map/ppermute | solution.py:493
  41.6 1.4 %collective-permute-done.8.z_in = f32[2,64,256]{2,1,0:T(8,128)S(1)} collective-permute-done((f32[2,64,256]{2,1,0:T(8,128)S(1)}, f32[2,64,256]{2,1,0:T(8,128)S(1)}, u32[]{:S(2)}, u32[]{:S(2)}) %collective-permute-start.8) | collective-permute-done | bytes 131104 | tf_op jit(solution)/shard_map/ppermute | solution.py:502
  43.1 2.2 %shard_map.228 = (f32[2,64,256]{2,1,0:T(8,128)}, f32[2,64,256]{2,1,0:T(8,128)}, f32[6,64,256]{2,1,0:T(8,128)}, f32[6,64,256]{2,1,0:T(8,128)}, f32[6,64,256]{2,1,...) custom-call(f32[2,64,256]{2,1,0:T(8,128)S(1)} %bitcast.61, ...), custom_call_target="tpu_custom_call" | custom-call | flops 500 | bytes 1 | tf_op jit(solution)/shard_map/pallas_call | solution.py:426
  (34 shorter events, 0.1 us)
Async XLA Ops:
  0.6 7.8 %copy-start = (f32[6,2,1,64,256]{4,3,2,1,0:T(8,128)S(1)}, f32[6,2,1,64,256]{4,3,2,1,0:T(8,128)}, u32[]{:S(2)}) copy-start(f32[6,2,1,64,256]{4,3,2,1,0:T(8,128)} %param.23) | copy-start | bytes 2359300
  0.7 7.8 %copy-start.1 = (f32[6,2,1,64,256]{4,3,2,1,0:T(8,128)S(1)}, f32[6,2,1,64,256]{4,3,2,1,0:T(8,128)}, u32[]{:S(2)}) copy-start(f32[6,2,1,64,256]{4,3,2,1,0:T(8,128)} %param.24) | copy-start | bytes 2359300
  0.7 7.8 %copy-start.2 = (f32[3,2,1,64,256]{4,3,2,1,0:T(8,128)S(1)}, f32[3,2,1,64,256]{4,3,2,1,0:T(8,128)}, u32[]{:S(2)}) copy-start(f32[3,2,1,64,256]{4,3,2,1,0:T(8,128)} %param.21) | copy-start | bytes 1179652
  0.7 7.8 %copy-start.3 = (f32[3,2,1,64,256]{4,3,2,1,0:T(8,128)S(1)}, f32[3,2,1,64,256]{4,3,2,1,0:T(8,128)}, u32[]{:S(2)}) copy-start(f32[3,2,1,64,256]{4,3,2,1,0:T(8,128)} %param.22) | copy-start | bytes 1179652
  2.7 10.9 %collective-permute-start = (f32[80,384]{1,0:T(8,128)S(1)}, f32[80,384]{1,0:T(8,128)S(1)}, u32[]{:S(2)}, u32[]{:S(2)}) collective-permute-start(f32[80,384]{1,0:T(8,128)S(1)} %get-tuple-element.39), channel_id=1, source_target_pairs={{0,4},{4,8},{8,12},{12,0},{1,5},{5,9},{9,13},{13,1},{2,6},{6,10},{... | collective-permute-start | bytes 368648 | tf_op jit(solution)/shard_map/ppermute | solution.py:438
  4.9 8.8 %collective-permute-start.1 = (f32[64,384]{1,0:T(8,128)S(1)}, f32[64,384]{1,0:T(8,128)S(1)}, u32[]{:S(2)}, u32[]{:S(2)}) collective-permute-start(f32[64,384]{1,0:T(8,128)S(1)} %get-tuple-element.40), channel_id=1, source_target_pairs={{0,8},{4,12},{8,0},{12,4},{1,9},{5,13},{9,1},{13,5},{2,10},{6,14},... | collective-permute-start | bytes 294920 | tf_op jit(solution)/shard_map/ppermute | solution.py:438
  7.3 6.3 %collective-permute-start.2 = (f32[64,384]{1,0:T(8,128)S(1)}, f32[64,384]{1,0:T(8,128)S(1)}, u32[]{:S(2)}, u32[]{:S(2)}) collective-permute-start(f32[64,384]{1,0:T(8,128)S(1)} %get-tuple-element.41), channel_id=1, source_target_pairs={{0,12},{4,0},{8,4},{12,8},{1,13},{5,1},{9,5},{13,9},{2,14},{6,2},{... | collective-permute-start | bytes 294920 | tf_op jit(solution)/shard_map/ppermute | solution.py:438
  8.5 5.2 %copy-start.11 = (f32[2,3,64,256]{3,2,1,0:T(8,128)S(1)}, f32[2,3,64,256]{3,2,1,0:T(8,128)}, u32[]{:S(2)}) copy-start(f32[2,3,64,256]{3,2,1,0:T(8,128)} %param.26) | copy-start | bytes 1179652
  8.5 5.2 %copy-start.13 = (bf16[512,512]{1,0:T(8,128)(2,1)S(1)}, bf16[512,512]{1,0:T(8,128)(2,1)}, u32[]{:S(2)}) copy-start(bf16[512,512]{1,0:T(8,128)(2,1)} %constant.10.clone.th_ref) | copy-start | bytes 1572868
  8.5 5.2 %copy-start.15 = (bf16[512,512]{1,0:T(8,128)(2,1)S(1)}, bf16[512,512]{1,0:T(8,128)(2,1)}, u32[]{:S(2)}) copy-start(bf16[512,512]{1,0:T(8,128)(2,1)} %constant.11.clone.tl_ref) | copy-start | bytes 1572868
  8.5 10.9 %collective-permute-start.4 = (f32[144,256]{1,0:T(8,128)S(1)}, f32[144,256]{1,0:T(8,128)S(1)}, u32[]{:S(2)}, u32[]{:S(2)}) collective-permute-start(f32[144,256]{1,0:T(8,128)S(1)} %shard_map.225), channel_id=1, source_target_pairs={{0,16},{16,32},{32,48},{48,64},{64,80},{80,96},{96,112},{112,128},... | collective-permute-start | bytes 442376 | tf_op jit(solution)/shard_map/ppermute | solution.py:470
  13.7 5.8 %copy-start.5 = (f32[3,2,1,64,256]{4,3,2,1,0:T(8,128)S(1)}, f32[3,2,1,64,256]{4,3,2,1,0:T(8,128)}, u32[]{:S(2)}) copy-start(f32[3,2,1,64,256]{4,3,2,1,0:T(8,128)} %param.18) | copy-start | bytes 1179652
  13.7 5.8 %copy-start.6 = (f32[3,2,1,64,256]{4,3,2,1,0:T(8,128)S(1)}, f32[3,2,1,64,256]{4,3,2,1,0:T(8,128)}, u32[]{:S(2)}) copy-start(f32[3,2,1,64,256]{4,3,2,1,0:T(8,128)} %param.19) | copy-start | bytes 1179652
  13.7 5.8 %copy-start.9 = (f32[2,1,64,256]{3,2,1,0:T(8,128)S(1)}, f32[2,1,64,256]{3,2,1,0:T(8,128)}, u32[]{:S(2)}) copy-start(f32[2,1,64,256]{3,2,1,0:T(8,128)} %param.16) | copy-start | bytes 393220
  13.7 5.8 %copy-start.10 = (f32[2,1,64,256]{3,2,1,0:T(8,128)S(1)}, f32[2,1,64,256]{3,2,1,0:T(8,128)}, u32[]{:S(2)}) copy-start(f32[2,1,64,256]{3,2,1,0:T(8,128)} %param.17) | copy-start | bytes 393220
  14.3 8.5 %collective-permute-start.3 = (f32[2,64,256]{2,1,0:T(8,128)S(1)}, f32[2,64,256]{2,1,0:T(8,128)S(1)}, u32[]{:S(2)}, u32[]{:S(2)}) collective-permute-start(f32[2,64,256]{2,1,0:T(8,128)S(1)} %shard_map.224.order), channel_id=1, source_target_pairs={{0,1},{1,0},{2,3},{3,2},{16,19},{17,18},{18,17},{19,16},{32,33},{3... | collective-permute-start | bytes 393224 | tf_op jit(solution)/shard_map/ppermute | solution.py:483
  19.5 11.1 %copy-start.8 = (bf16[256,512]{1,0:T(8,128)(2,1)S(1)}, bf16[256,512]{1,0:T(8,128)(2,1)}, u32[]{:S(2)}) copy-start(bf16[256,512]{1,0:T(8,128)(2,1)} %constant.9.clone.tl_hbm.tl_ref) | copy-start | bytes 786436
  20.6 10.0 %copy-start.7 = (bf16[256,512]{1,0:T(8,128)(2,1)S(1)}, bf16[256,512]{1,0:T(8,128)(2,1)}, u32[]{:S(2)}) copy-start(bf16[256,512]{1,0:T(8,128)(2,1)} %constant.8.clone.th_hbm.th_ref) | copy-start | bytes 786436
  22.8 7.8 %collective-permute-start.5 = (f32[2,64,256]{2,1,0:T(8,128)S(1)}, f32[2,64,256]{2,1,0:T(8,128)S(1)}, u32[]{:S(2)}, u32[]{:S(2)}) collective-permute-start(f32[2,64,256]{2,1,0:T(8,128)S(1)} %add.3.sum_a), channel_id=1, source_target_pairs={{0,3},{1,2},{2,1},{3,0},{16,17},{17,16},{18,19},{19,18},{32,35},{3... | collective-permute-start | bytes 393224 | tf_op jit(solution)/shard_map/ppermute | solution.py:486
  24.0 10.7 %collective-permute-start.6 = (f32[14,64,256]{2,1,0:T(8,128)S(1)}, f32[14,64,256]{2,1,0:T(8,128)S(1)}, u32[]{:S(2)}, u32[]{:S(2)}) collective-permute-start(f32[14,64,256]{2,1,0:T(8,128)S(1)} %get-tuple-element.50), channel_id=1, source_target_pairs={{0,16},{16,0},{32,48},{48,32},{64,80},{80,64},{96,112},{112,96},{1... | collective-permute-start | bytes 2752520 | tf_op jit(solution)/shard_map/ppermute | solution.py:494
  26.7 14.9 %collective-permute-start.7 = (f32[14,64,256]{2,1,0:T(8,128)S(1)}, f32[14,64,256]{2,1,0:T(8,128)S(1)}, u32[]{:S(2)}, u32[]{:S(2)}) collective-permute-start(f32[14,64,256]{2,1,0:T(8,128)S(1)} %get-tuple-element.52), channel_id=1, source_target_pairs={{16,32},{32,16},{17,33},{33,17},{18,34},{34,18},{19,35},{35,19},{4... | collective-permute-start | bytes 2752520 | tf_op jit(solution)/shard_map/ppermute | solution.py:493
  30.6 8.8 %copy-start.4 = (f32[2,1,3,64,256]{4,3,2,1,0:T(8,128)S(1)}, f32[2,1,3,64,256]{4,3,2,1,0:T(8,128)}, u32[]{:S(2)}) copy-start(f32[2,1,3,64,256]{4,3,2,1,0:T(8,128)} %param.20) | copy-start | bytes 1179652
  30.6 8.8 %copy-start.12 = (f32[2,1,3,64,256]{4,3,2,1,0:T(8,128)S(1)}, f32[2,1,3,64,256]{4,3,2,1,0:T(8,128)}, u32[]{:S(2)}) copy-start(f32[2,1,3,64,256]{4,3,2,1,0:T(8,128)} %param.25) | copy-start | bytes 1179652
  30.6 8.8 %copy-start.14 = (bf16[512,512]{1,0:T(8,128)(2,1)S(1)}, bf16[512,512]{1,0:T(8,128)(2,1)}, u32[]{:S(2)}) copy-start(bf16[512,512]{1,0:T(8,128)(2,1)} %constant.10.clone.th_ref) | copy-start | bytes 1572868
  30.7 8.8 %copy-start.16 = (bf16[512,512]{1,0:T(8,128)(2,1)S(1)}, bf16[512,512]{1,0:T(8,128)(2,1)}, u32[]{:S(2)}) copy-start(bf16[512,512]{1,0:T(8,128)(2,1)} %constant.11.clone.tl_ref) | copy-start | bytes 1572868
  31.3 8.1 %collective-permute-start.9 = (f32[80,384]{1,0:T(8,128)S(1)}, f32[80,384]{1,0:T(8,128)S(1)}, u32[]{:S(2)}, u32[]{:S(2)}) collective-permute-start(f32[80,384]{1,0:T(8,128)S(1)} %get-tuple-element.54), channel_id=1, source_target_pairs={{0,12},{4,0},{8,4},{12,8},{1,13},{5,1},{9,5},{13,9},{2,14},{6,2},{... | collective-permute-start | bytes 368648 | tf_op jit(solution)/shard_map/ppermute | solution.py:438
  33.2 6.2 %collective-permute-start.10 = (f32[64,384]{1,0:T(8,128)S(1)}, f32[64,384]{1,0:T(8,128)S(1)}, u32[]{:S(2)}, u32[]{:S(2)}) collective-permute-start(f32[64,384]{1,0:T(8,128)S(1)} %get-tuple-element.60), channel_id=1, source_target_pairs={{0,4},{4,8},{8,12},{12,0},{1,5},{5,9},{9,13},{13,1},{2,6},{6,10},{... | collective-permute-start | bytes 294920 | tf_op jit(solution)/shard_map/ppermute | solution.py:438
  33.2 6.2 %collective-permute-start.11 = (f32[64,384]{1,0:T(8,128)S(1)}, f32[64,384]{1,0:T(8,128)S(1)}, u32[]{:S(2)}, u32[]{:S(2)}) collective-permute-start(f32[64,384]{1,0:T(8,128)S(1)} %get-tuple-element.61), channel_id=1, source_target_pairs={{0,8},{4,12},{8,0},{12,4},{1,9},{5,13},{9,1},{13,5},{2,10},{6,14},... | collective-permute-start | bytes 294920 | tf_op jit(solution)/shard_map/ppermute | solution.py:438
  34.7 8.4 %collective-permute-start.8 = (f32[2,64,256]{2,1,0:T(8,128)S(1)}, f32[2,64,256]{2,1,0:T(8,128)S(1)}, u32[]{:S(2)}, u32[]{:S(2)}) collective-permute-start(f32[2,64,256]{2,1,0:T(8,128)S(1)} %get-tuple-element.53.z), channel_id=1, source_target_pairs={{16,0},{32,16},{48,32},{64,48},{80,64},{96,80},{112,96},{128,112},... | collective-permute-start | bytes 393224 | tf_op jit(solution)/shard_map/ppermute | solution.py:502

commit v5 on v4

--- a/solution.py
+++ b/solution.py
@@ -491,6 +491,7 @@
             pairs.append((t * groups + c, (t + 1) * groups + there))
             pairs.append(((t + 1) * groups + there, t * groups + c))
     from_chip = lax.ppermute(to_chip, ("tm", "coil"), pairs)
+    to_core, rest = lax.optimization_barrier((to_core, rest))
     from_core = lax.ppermute(to_core, "tm", [(t, t ^ 1) for t in range(frames)])
     c_blocks = (shape(BLOCK, 384), shape(BLOCK, 384), shape(BLOCK, 384), shape(BLOCK + 16, 384))
     c0, c1, c2, c3, z = call(

time: 45.7 us -> 45.4 us (level)
    ppermute x1, starting transfers between devices: 3.83 us -> 6.54 us  [body(): from_chip = lax.ppermute(to_chip, ('tm', 'coil'), pairs)]
    ppermute x1, starting transfers between devices: 2.71 us -> 0.09 us  [body(): from_core = lax.ppermute(to_core, 'tm', [(t, t ^ 1) for t in range(frames)])]
    ppermute x6, waiting for transfers between devices: 1.26 us -> 3.03 us  [turn(): lax.ppermute(block, 'row', [(i, (i + distance) % ROWS) for i in range(ROW...]
    ppermute x1, waiting for transfers between devices: 1.4 us -> 0.49 us  [body(): z_in = lax.ppermute(z, 'tm', [(i + 1, i) for i in range(frames - 1)])]
    ppermute x1, waiting for transfers between devices: 0.9 us -> 0.01 us  [body(): from_chip = lax.ppermute(to_chip, ('tm', 'coil'), pairs)]
    ppermute x1, starting transfers between devices: 3.5 us -> 2.76 us  [body(): z_in = lax.ppermute(z, 'tm', [(i + 1, i) for i in range(frames - 1)])]
    ppermute x6, starting transfers between devices: 9.1 us -> 9.76 us  [turn(): lax.ppermute(block, 'row', [(i, (i + distance) % ROWS) for i in range(ROW...]
  transfers between devices with their start and end apart: 12 -> 12, of which waited for: 4 -> 3; matrix products, arithmetic and copies ran while one was open for 0% -> 0% of each run, Pallas kernels for 8% -> 8%
where the time goes in v5:
time: 45.4 us; the launch traced here: 45.2 us
  starting transfers between devices  30.7 us (68%)
  Pallas kernels  7.73 us (17%)
  waiting for transfers between devices  5.67 us (12%)
  between operations  0.99 us (2%)
    ppermute x6, starting transfers between devices, turn(): lax.ppermute(block, 'row', [(i, (i + distance) % ROWS) for i in range(ROW...  9.76 us
    pallas_call x7, Pallas kernels, call(): pl.pallas_call(kernel, out_shape=outs, in_specs=in_specs or [pl.BlockSpec...  7.73 us
    ppermute x1, starting transfers between devices, body(): from_chip = lax.ppermute(to_chip, ('tm', 'coil'), pairs)  6.54 us
    ppermute x1, starting transfers between devices, body(): received = lax.ppermute(partial, ('tm', 'coil'), swaps[0])  5.21 us
    ppermute x1, starting transfers between devices, body(): q_first = lax.ppermute(q_first, 'tm', after)  5.08 us
    ppermute x6, waiting for transfers between devices, turn(): lax.ppermute(block, 'row', [(i, (i + distance) % ROWS) for i in range(ROW...  3.03 us
    ppermute x1, starting transfers between devices, body(): z_in = lax.ppermute(z, 'tm', [(i + 1, i) for i in range(frames - 1)])  2.76 us
    ppermute x1, waiting for transfers between devices, body(): received = lax.ppermute(partial, ('tm', 'coil'), swaps[0])  2.14 us
  transfers between devices with their start and end apart: 12, of which 3 were waited for; matrix products, arithmetic and copies ran while one was open for 0% of the time, Pallas kernels for 8%

profile of v5, /device:TPU:1, one launch (start us, length us, event | category | flops | bytes accessed | tf_op | source)
XLA Modules:
  0.0 45.2 jit_solution(18436970024197753165)
XLA Ops:
  0.7 2.0 %shard_map.223 = (f32[64,384]{1,0:T(8,128)S(1)}, f32[80,384]{1,0:T(8,128)S(1)}, f32[64,384]{1,0:T(8,128)S(1)}, f32[64,384]{1,0:T(8,128)S(1)}, f32[1,256]{1,0:T(1,128)S(1)}) custom-call(f32[6,64,256]{2,1,0:T(8,128)} %bitcast.54, s32[1,256]{1,0:T(1,128)} %lines_hbm.1, bf16[256,512]{1,0:T(8,128)(2,1)} %constant.8.clone.th_hbm.th_ref, ...), custom_call_target="tpu_custom_call" | custom-call | flops 500 | bytes 1 | tf_op jit(solution)/shard_map/pallas_call | solution.py:426
  2.7 2.1 %collective-permute-start = (f32[80,384]{1,0:T(8,128)S(1)}, f32[80,384]{1,0:T(8,128)S(1)}, u32[]{:S(2)}, u32[]{:S(2)}) collective-permute-start(f32[80,384]{1,0:T(8,128)S(1)} %get-tuple-element.41), channel_id=1, source_target_pairs={{0,4},{4,8},{8,12},{12,0},{1,5},{5,9},{9,13},{13,1},{2,6},{6,10},{... | collective-permute-start | bytes 368648 | tf_op jit(solution)/shard_map/ppermute | solution.py:438
  4.9 2.4 %collective-permute-start.1 = (f32[64,384]{1,0:T(8,128)S(1)}, f32[64,384]{1,0:T(8,128)S(1)}, u32[]{:S(2)}, u32[]{:S(2)}) collective-permute-start(f32[64,384]{1,0:T(8,128)S(1)} %get-tuple-element.42), channel_id=1, source_target_pairs={{0,8},{4,12},{8,0},{12,4},{1,9},{5,13},{9,1},{13,5},{2,10},{6,14},... | collective-permute-start | bytes 294920 | tf_op jit(solution)/shard_map/ppermute | solution.py:438
  7.3 1.2 %collective-permute-start.2 = (f32[64,384]{1,0:T(8,128)S(1)}, f32[64,384]{1,0:T(8,128)S(1)}, u32[]{:S(2)}, u32[]{:S(2)}) collective-permute-start(f32[64,384]{1,0:T(8,128)S(1)} %get-tuple-element.43), channel_id=1, source_target_pairs={{0,12},{4,0},{8,4},{12,8},{1,13},{5,1},{9,5},{13,9},{2,14},{6,2},{... | collective-permute-start | bytes 294920 | tf_op jit(solution)/shard_map/ppermute | solution.py:438
  8.5 0.0 copy-start.11
  8.5 0.0 copy-start.13
  8.5 0.0 copy-start.15
  8.5 5.1 %collective-permute-start.4 = (f32[144,256]{1,0:T(8,128)S(1)}, f32[144,256]{1,0:T(8,128)S(1)}, u32[]{:S(2)}, u32[]{:S(2)}) collective-permute-start(f32[144,256]{1,0:T(8,128)S(1)} %shard_map.225), channel_id=1, source_target_pairs={{0,16},{16,32},{32,48},{48,64},{64,80},{80,96},{96,112},{112,128},... | collective-permute-start | bytes 442376 | tf_op jit(solution)/shard_map/ppermute | solution.py:470
  13.7 0.0 copy-start.5
  13.7 0.0 copy-start.6
  13.7 0.0 copy-start.9
  13.7 0.0 copy-start.10
  13.7 0.5 %shard_map.224.order = f32[2,64,256]{2,1,0:T(8,128)S(1)} custom-call(f32[64,384]{1,0:T(8,128)S(1)} %get-tuple-element.40.b0.order, f32[80,384]{1,0:T(8,128)S(1)} %collective-permute-done.b1, f32[64,384]{1,0:T(8,128)S(1)} %collective-permute-done.1.b2, f32[64,384]{1,0:T(8,128)S(1)} %collective-permute-done.2.b3, bf16[512,512]{1,0:T(8,128)(2,1)S(1)} %copy-done.13, ...), custom_call_target="tpu_custom_call" | custom-call | flops 99999997952 | bytes 200000000 | tf_op jit(solution)/shard_map/pallas_call | solution.py:426
  14.3 5.2 %collective-permute-start.3 = (f32[2,64,256]{2,1,0:T(8,128)S(1)}, f32[2,64,256]{2,1,0:T(8,128)S(1)}, u32[]{:S(2)}, u32[]{:S(2)}) collective-permute-start(f32[2,64,256]{2,1,0:T(8,128)S(1)} %shard_map.224.order), channel_id=1, source_target_pairs={{0,1},{1,0},{2,3},{3,2},{16,19},{17,18},{18,17},{19,16},{32,33},{3... | collective-permute-start | bytes 393224 | tf_op jit(solution)/shard_map/ppermute | solution.py:483
  19.5 0.0 copy-start.8
  19.5 1.1 %shard_map.226 = (f32[16,64,256]{2,1,0:T(8,128)S(1)}, f32[2,64,256]{2,1,0:T(8,128)S(1)}, f32[16,256]{1,0:T(8,128)S(1)}, f32[2,64,256]{2,1,0:T(8,128)S(1)}, f32[1...) custom-call(f32[2,64,256]{2,1,0:T(8,128)S(1)} %bitcast.60, f32[2,64,256]{2,1,0:T(8,128)S(1)} %bitcast.62, ...), custom_call_target="tpu_custom_call" | custom-call | flops 49999998976 | bytes 100000000 | tf_op jit(solution)/shard_map/pallas_call | solution.py:426
  20.6 0.0 copy-start.7
  20.6 2.1 %collective-permute-done.3 = f32[2,64,256]{2,1,0:T(8,128)S(1)} collective-permute-done((f32[2,64,256]{2,1,0:T(8,128)S(1)}, f32[2,64,256]{2,1,0:T(8,128)S(1)}, u32[]{:S(2)}, u32[]{:S(2)}) %collective-permute-start.3) | collective-permute-done | bytes 131104 | tf_op jit(solution)/shard_map/ppermute | solution.py:483
  22.8 1.3 %collective-permute-start.5 = (f32[2,64,256]{2,1,0:T(8,128)S(1)}, f32[2,64,256]{2,1,0:T(8,128)S(1)}, u32[]{:S(2)}, u32[]{:S(2)}) collective-permute-start(f32[2,64,256]{2,1,0:T(8,128)S(1)} %add.3.sum_a), channel_id=1, source_target_pairs={{0,3},{1,2},{2,1},{3,0},{16,17},{17,16},{18,19},{19,18},{32,35},{3... | collective-permute-start | bytes 393224 | tf_op jit(solution)/shard_map/ppermute | solution.py:486
  24.0 6.5 %collective-permute-start.7 = (f32[14,64,256]{2,1,0:T(8,128)S(1)}, f32[14,64,256]{2,1,0:T(8,128)S(1)}, u32[]{:S(2)}, u32[]{:S(2)}) collective-permute-start(f32[14,64,256]{2,1,0:T(8,128)S(1)} %get-tuple-element.56), channel_id=1, source_target_pairs={{16,32},{32,16},{17,33},{33,17},{18,34},{34,18},{19,35},{35,19},{4... | collective-permute-start | bytes 2752520 | tf_op jit(solution)/shard_map/ppermute | solution.py:493
  30.6 0.1 collective-permute-start.6
  30.7 0.0 copy-start.12
  30.7 0.0 copy-start.14
  30.7 0.0 copy-start.16
  30.8 0.6 %shard_map.227 = (f32[64,384]{1,0:T(8,128)S(1)}, f32[64,384]{1,0:T(8,128)S(1)}, f32[64,384]{1,0:T(8,128)S(1)}, f32[80,384]{1,0:T(8,128)S(1)}, f32[2,64,256]{2,1,0:T(8,128)S(1)}) custom-call(f32[2,64,256]{2,1,0:T(8,128)S(1)} %add.3.sum_a, f32[2,64,256]{2,1,0:T(8,128)S(1)} %collective-permute-done.5.sum_b, f32[2,64,256]{2,1,0:T(8,128)S(1)} %get-tuple-element.51.base, ...), custom_call_target="tpu_custom_call" | custom-call | flops 99999997952 | bytes 200000000 | tf_op jit(solution)/shard_map/pallas_call | solution.py:426
  31.4 2.3 %collective-permute-start.9 = (f32[80,384]{1,0:T(8,128)S(1)}, f32[80,384]{1,0:T(8,128)S(1)}, u32[]{:S(2)}, u32[]{:S(2)}) collective-permute-start(f32[80,384]{1,0:T(8,128)S(1)} %get-tuple-element.58), channel_id=1, source_target_pairs={{0,12},{4,0},{8,4},{12,8},{1,13},{5,1},{9,5},{13,9},{2,14},{6,2},{... | collective-permute-start | bytes 368648 | tf_op jit(solution)/shard_map/ppermute | solution.py:438
  33.7 1.7 %collective-permute-start.11 = (f32[64,384]{1,0:T(8,128)S(1)}, f32[64,384]{1,0:T(8,128)S(1)}, u32[]{:S(2)}, u32[]{:S(2)}) collective-permute-start(f32[64,384]{1,0:T(8,128)S(1)} %get-tuple-element.65), channel_id=1, source_target_pairs={{0,8},{4,12},{8,0},{12,4},{1,9},{5,13},{9,1},{13,5},{2,10},{6,14},... | collective-permute-start | bytes 294920 | tf_op jit(solution)/shard_map/ppermute | solution.py:438
  35.4 2.8 %collective-permute-start.8 = (f32[2,64,256]{2,1,0:T(8,128)S(1)}, f32[2,64,256]{2,1,0:T(8,128)S(1)}, u32[]{:S(2)}, u32[]{:S(2)}) collective-permute-start(f32[2,64,256]{2,1,0:T(8,128)S(1)} %get-tuple-element.57.z), channel_id=1, source_target_pairs={{16,0},{32,16},{48,32},{64,48},{80,64},{96,80},{112,96},{128,112},... | collective-permute-start | bytes 393224 | tf_op jit(solution)/shard_map/ppermute | solution.py:503
  38.2 3.0 %collective-permute-done.10.b1 = f32[64,384]{1,0:T(8,128)S(1)} collective-permute-done((f32[64,384]{1,0:T(8,128)S(1)}, f32[64,384]{1,0:T(8,128)S(1)}, u32[]{:S(2)}, u32[]{:S(2)}) %collective-permute-start.10) | collective-permute-done | bytes 98336 | tf_op jit(solution)/shard_map/ppermute | solution.py:438
  41.3 1.3 %shard_map.229 = f32[6,64,256]{2,1,0:T(8,128)} custom-call(f32[64,384]{1,0:T(8,128)S(1)} %get-tuple-element.63.b0, f32[64,384]{1,0:T(8,128)S(1)} %collective-permute-done.10.b1, f32[64,384]{1,0:T(8,128)S(1)} %collective-permute-done.11.b2, f32[80,384]{1,0:T(8,128)S(1)} %collective-permute-done.9.n3.b3, bf16[512,512]{1,0:T(8,128)(2,1)S(1)} %copy-done.14, ...), custom_call_target="tpu_custom_call" | custom-call | flops 2000000000 | bytes 4000000 | tf_op jit(solution)/shard_map/pallas_call | solution.py:426
  42.6 0.5 %collective-permute-done.8.z_in = f32[2,64,256]{2,1,0:T(8,128)S(1)} collective-permute-done((f32[2,64,256]{2,1,0:T(8,128)S(1)}, f32[2,64,256]{2,1,0:T(8,128)S(1)}, u32[]{:S(2)}, u32[]{:S(2)}) %collective-permute-start.8) | collective-permute-done | bytes 131104 | tf_op jit(solution)/shard_map/ppermute | solution.py:503
  43.0 2.2 %shard_map.228 = (f32[2,64,256]{2,1,0:T(8,128)}, f32[2,64,256]{2,1,0:T(8,128)}, f32[6,64,256]{2,1,0:T(8,128)}, f32[6,64,256]{2,1,0:T(8,128)}, f32[6,64,256]{2,1,...) custom-call(f32[2,64,256]{2,1,0:T(8,128)S(1)} %bitcast.61, ...), custom_call_target="tpu_custom_call" | custom-call | flops 500 | bytes 1 | tf_op jit(solution)/shard_map/pallas_call | solution.py:426
  (34 shorter events, 0.1 us)
Async XLA Ops:
  0.6 7.8 %copy-start = (f32[6,2,1,64,256]{4,3,2,1,0:T(8,128)S(1)}, f32[6,2,1,64,256]{4,3,2,1,0:T(8,128)}, u32[]{:S(2)}) copy-start(f32[6,2,1,64,256]{4,3,2,1,0:T(8,128)} %param.23) | copy-start | bytes 2359300
  0.7 7.8 %copy-start.1 = (f32[6,2,1,64,256]{4,3,2,1,0:T(8,128)S(1)}, f32[6,2,1,64,256]{4,3,2,1,0:T(8,128)}, u32[]{:S(2)}) copy-start(f32[6,2,1,64,256]{4,3,2,1,0:T(8,128)} %param.24) | copy-start | bytes 2359300
  0.7 7.8 %copy-start.2 = (f32[3,2,1,64,256]{4,3,2,1,0:T(8,128)S(1)}, f32[3,2,1,64,256]{4,3,2,1,0:T(8,128)}, u32[]{:S(2)}) copy-start(f32[3,2,1,64,256]{4,3,2,1,0:T(8,128)} %param.21) | copy-start | bytes 1179652
  0.7 7.8 %copy-start.3 = (f32[3,2,1,64,256]{4,3,2,1,0:T(8,128)S(1)}, f32[3,2,1,64,256]{4,3,2,1,0:T(8,128)}, u32[]{:S(2)}) copy-start(f32[3,2,1,64,256]{4,3,2,1,0:T(8,128)} %param.22) | copy-start | bytes 1179652
  2.7 10.9 %collective-permute-start = (f32[80,384]{1,0:T(8,128)S(1)}, f32[80,384]{1,0:T(8,128)S(1)}, u32[]{:S(2)}, u32[]{:S(2)}) collective-permute-start(f32[80,384]{1,0:T(8,128)S(1)} %get-tuple-element.41), channel_id=1, source_target_pairs={{0,4},{4,8},{8,12},{12,0},{1,5},{5,9},{9,13},{13,1},{2,6},{6,10},{... | collective-permute-start | bytes 368648 | tf_op jit(solution)/shard_map/ppermute | solution.py:438
  4.9 8.8 %collective-permute-start.1 = (f32[64,384]{1,0:T(8,128)S(1)}, f32[64,384]{1,0:T(8,128)S(1)}, u32[]{:S(2)}, u32[]{:S(2)}) collective-permute-start(f32[64,384]{1,0:T(8,128)S(1)} %get-tuple-element.42), channel_id=1, source_target_pairs={{0,8},{4,12},{8,0},{12,4},{1,9},{5,13},{9,1},{13,5},{2,10},{6,14},... | collective-permute-start | bytes 294920 | tf_op jit(solution)/shard_map/ppermute | solution.py:438
  7.3 6.3 %collective-permute-start.2 = (f32[64,384]{1,0:T(8,128)S(1)}, f32[64,384]{1,0:T(8,128)S(1)}, u32[]{:S(2)}, u32[]{:S(2)}) collective-permute-start(f32[64,384]{1,0:T(8,128)S(1)} %get-tuple-element.43), channel_id=1, source_target_pairs={{0,12},{4,0},{8,4},{12,8},{1,13},{5,1},{9,5},{13,9},{2,14},{6,2},{... | collective-permute-start | bytes 294920 | tf_op jit(solution)/shard_map/ppermute | solution.py:438
  8.5 5.2 %copy-start.11 = (f32[2,3,64,256]{3,2,1,0:T(8,128)S(1)}, f32[2,3,64,256]{3,2,1,0:T(8,128)}, u32[]{:S(2)}) copy-start(f32[2,3,64,256]{3,2,1,0:T(8,128)} %param.26) | copy-start | bytes 1179652
  8.5 5.2 %copy-start.13 = (bf16[512,512]{1,0:T(8,128)(2,1)S(1)}, bf16[512,512]{1,0:T(8,128)(2,1)}, u32[]{:S(2)}) copy-start(bf16[512,512]{1,0:T(8,128)(2,1)} %constant.10.clone.th_ref) | copy-start | bytes 1572868
  8.5 5.2 %copy-start.15 = (bf16[512,512]{1,0:T(8,128)(2,1)S(1)}, bf16[512,512]{1,0:T(8,128)(2,1)}, u32[]{:S(2)}) copy-start(bf16[512,512]{1,0:T(8,128)(2,1)} %constant.11.clone.tl_ref) | copy-start | bytes 1572868
  8.5 10.9 %collective-permute-start.4 = (f32[144,256]{1,0:T(8,128)S(1)}, f32[144,256]{1,0:T(8,128)S(1)}, u32[]{:S(2)}, u32[]{:S(2)}) collective-permute-start(f32[144,256]{1,0:T(8,128)S(1)} %shard_map.225), channel_id=1, source_target_pairs={{0,16},{16,32},{32,48},{48,64},{64,80},{80,96},{96,112},{112,128},... | collective-permute-start | bytes 442376 | tf_op jit(solution)/shard_map/ppermute | solution.py:470
  13.7 5.8 %copy-start.5 = (f32[3,2,1,64,256]{4,3,2,1,0:T(8,128)S(1)}, f32[3,2,1,64,256]{4,3,2,1,0:T(8,128)}, u32[]{:S(2)}) copy-start(f32[3,2,1,64,256]{4,3,2,1,0:T(8,128)} %param.18) | copy-start | bytes 1179652
  13.7 5.8 %copy-start.6 = (f32[3,2,1,64,256]{4,3,2,1,0:T(8,128)S(1)}, f32[3,2,1,64,256]{4,3,2,1,0:T(8,128)}, u32[]{:S(2)}) copy-start(f32[3,2,1,64,256]{4,3,2,1,0:T(8,128)} %param.19) | copy-start | bytes 1179652
  13.7 5.8 %copy-start.9 = (f32[2,1,64,256]{3,2,1,0:T(8,128)S(1)}, f32[2,1,64,256]{3,2,1,0:T(8,128)}, u32[]{:S(2)}) copy-start(f32[2,1,64,256]{3,2,1,0:T(8,128)} %param.16) | copy-start | bytes 393220
  13.7 5.8 %copy-start.10 = (f32[2,1,64,256]{3,2,1,0:T(8,128)S(1)}, f32[2,1,64,256]{3,2,1,0:T(8,128)}, u32[]{:S(2)}) copy-start(f32[2,1,64,256]{3,2,1,0:T(8,128)} %param.17) | copy-start | bytes 393220
  14.3 8.5 %collective-permute-start.3 = (f32[2,64,256]{2,1,0:T(8,128)S(1)}, f32[2,64,256]{2,1,0:T(8,128)S(1)}, u32[]{:S(2)}, u32[]{:S(2)}) collective-permute-start(f32[2,64,256]{2,1,0:T(8,128)S(1)} %shard_map.224.order), channel_id=1, source_target_pairs={{0,1},{1,0},{2,3},{3,2},{16,19},{17,18},{18,17},{19,16},{32,33},{3... | collective-permute-start | bytes 393224 | tf_op jit(solution)/shard_map/ppermute | solution.py:483
  19.5 11.2 %copy-start.8 = (bf16[256,512]{1,0:T(8,128)(2,1)S(1)}, bf16[256,512]{1,0:T(8,128)(2,1)}, u32[]{:S(2)}) copy-start(bf16[256,512]{1,0:T(8,128)(2,1)} %constant.9.clone.tl_hbm.tl_ref) | copy-start | bytes 786436
  20.6 10.1 %copy-start.7 = (bf16[256,512]{1,0:T(8,128)(2,1)S(1)}, bf16[256,512]{1,0:T(8,128)(2,1)}, u32[]{:S(2)}) copy-start(bf16[256,512]{1,0:T(8,128)(2,1)} %constant.8.clone.th_hbm.th_ref) | copy-start | bytes 786436
  22.8 7.8 %collective-permute-start.5 = (f32[2,64,256]{2,1,0:T(8,128)S(1)}, f32[2,64,256]{2,1,0:T(8,128)S(1)}, u32[]{:S(2)}, u32[]{:S(2)}) collective-permute-start(f32[2,64,256]{2,1,0:T(8,128)S(1)} %add.3.sum_a), channel_id=1, source_target_pairs={{0,3},{1,2},{2,1},{3,0},{16,17},{17,16},{18,19},{19,18},{32,35},{3... | collective-permute-start | bytes 393224 | tf_op jit(solution)/shard_map/ppermute | solution.py:486
  24.0 18.5 %collective-permute-start.7 = (f32[14,64,256]{2,1,0:T(8,128)S(1)}, f32[14,64,256]{2,1,0:T(8,128)S(1)}, u32[]{:S(2)}, u32[]{:S(2)}) collective-permute-start(f32[14,64,256]{2,1,0:T(8,128)S(1)} %get-tuple-element.56), channel_id=1, source_target_pairs={{16,32},{32,16},{17,33},{33,17},{18,34},{34,18},{19,35},{35,19},{4... | collective-permute-start | bytes 2752520 | tf_op jit(solution)/shard_map/ppermute | solution.py:493
  30.6 4.9 %collective-permute-start.6 = (f32[14,64,256]{2,1,0:T(8,128)S(1)}, f32[14,64,256]{2,1,0:T(8,128)S(1)}, u32[]{:S(2)}, u32[]{:S(2)}) collective-permute-start(f32[14,64,256]{2,1,0:T(8,128)S(1)} %get-tuple-element.54), channel_id=1, source_target_pairs={{0,16},{16,0},{32,48},{48,32},{64,80},{80,64},{96,112},{112,96},{1... | collective-permute-start | bytes 2752520 | tf_op jit(solution)/shard_map/ppermute | solution.py:495
  30.7 10.5 %copy-start.4 = (f32[2,1,3,64,256]{4,3,2,1,0:T(8,128)S(1)}, f32[2,1,3,64,256]{4,3,2,1,0:T(8,128)}, u32[]{:S(2)}) copy-start(f32[2,1,3,64,256]{4,3,2,1,0:T(8,128)} %param.20) | copy-start | bytes 1179652
  30.7 10.5 %copy-start.12 = (f32[2,1,3,64,256]{4,3,2,1,0:T(8,128)S(1)}, f32[2,1,3,64,256]{4,3,2,1,0:T(8,128)}, u32[]{:S(2)}) copy-start(f32[2,1,3,64,256]{4,3,2,1,0:T(8,128)} %param.25) | copy-start | bytes 1179652
  30.7 10.5 %copy-start.14 = (bf16[512,512]{1,0:T(8,128)(2,1)S(1)}, bf16[512,512]{1,0:T(8,128)(2,1)}, u32[]{:S(2)}) copy-start(bf16[512,512]{1,0:T(8,128)(2,1)} %constant.10.clone.th_ref) | copy-start | bytes 1572868
  30.7 10.5 %copy-start.16 = (bf16[512,512]{1,0:T(8,128)(2,1)S(1)}, bf16[512,512]{1,0:T(8,128)(2,1)}, u32[]{:S(2)}) copy-start(bf16[512,512]{1,0:T(8,128)(2,1)} %constant.11.clone.tl_ref) | copy-start | bytes 1572868
  31.4 9.8 %collective-permute-start.9 = (f32[80,384]{1,0:T(8,128)S(1)}, f32[80,384]{1,0:T(8,128)S(1)}, u32[]{:S(2)}, u32[]{:S(2)}) collective-permute-start(f32[80,384]{1,0:T(8,128)S(1)} %get-tuple-element.58), channel_id=1, source_target_pairs={{0,12},{4,0},{8,4},{12,8},{1,13},{5,1},{9,5},{13,9},{2,14},{6,2},{... | collective-permute-start | bytes 368648 | tf_op jit(solution)/shard_map/ppermute | solution.py:438
  33.7 7.5 %collective-permute-start.10 = (f32[64,384]{1,0:T(8,128)S(1)}, f32[64,384]{1,0:T(8,128)S(1)}, u32[]{:S(2)}, u32[]{:S(2)}) collective-permute-start(f32[64,384]{1,0:T(8,128)S(1)} %get-tuple-element.64), channel_id=1, source_target_pairs={{0,4},{4,8},{8,12},{12,0},{1,5},{5,9},{9,13},{13,1},{2,6},{6,10},{... | collective-permute-start | bytes 294920 | tf_op jit(solution)/shard_map/ppermute | solution.py:438
  33.7 7.5 %collective-permute-start.11 = (f32[64,384]{1,0:T(8,128)S(1)}, f32[64,384]{1,0:T(8,128)S(1)}, u32[]{:S(2)}, u32[]{:S(2)}) collective-permute-start(f32[64,384]{1,0:T(8,128)S(1)} %get-tuple-element.65), channel_id=1, source_target_pairs={{0,8},{4,12},{8,0},{12,4},{1,9},{5,13},{9,1},{13,5},{2,10},{6,14},... | collective-permute-start | bytes 294920 | tf_op jit(solution)/shard_map/ppermute | solution.py:438
  35.4 7.6 %collective-permute-start.8 = (f32[2,64,256]{2,1,0:T(8,128)S(1)}, f32[2,64,256]{2,1,0:T(8,128)S(1)}, u32[]{:S(2)}, u32[]{:S(2)}) collective-permute-start(f32[2,64,256]{2,1,0:T(8,128)S(1)} %get-tuple-element.57.z), channel_id=1, source_target_pairs={{16,0},{32,16},{48,32},{64,48},{80,64},{96,80},{112,96},{128,112},... | collective-permute-start | bytes 393224 | tf_op jit(solution)/shard_map/ppermute | solution.py:503

commit v6 on v5

--- a/solution.py
+++ b/solution.py
@@ -131,6 +131,7 @@
     for copy in copies[4:]:
         copy.wait()
     o1[BLOCK:, LENGTH:] = jnp.zeros((16, 128), F32)
+    o2[BLOCK:, :] = jnp.zeros((24, 384), F32)
     for plane in range(16):
         o1[BLOCK + plane : BLOCK + plane + 1, 0:LENGTH] = ends[plane, 7:8, :]
 
@@ -448,7 +449,7 @@
     first_high, first_low, high, low = map(jnp.asarray, dft_tables())
     frames = lax.axis_size("tm")
     groups = lax.axis_size("coil")
-    blocks = (shape(BLOCK, 384), shape(BLOCK + 16, 384), shape(BLOCK, 384), shape(BLOCK, 384))
+    blocks = (shape(BLOCK, 384), shape(BLOCK + 16, 384), shape(BLOCK + 24, 384), shape(BLOCK, 384))
     hbm = pl.BlockSpec(memory_space=pltpu.HBM)
     a0, a1, a2, a3, mask = call(
         start_kernel, (*blocks, shape(1, LENGTH)),

time: 45.4 us -> 46.5 us (1.024)
  starting transfers between devices: 30.7 us -> 31.9 us
    ppermute x1, starting transfers between devices: 6.54 us -> 7.87 us  [body(): from_chip = lax.ppermute(to_chip, ('tm', 'coil'), pairs)]
    ppermute x1, starting transfers between devices: 1.26 us -> 0.68 us  [body(): rest = lax.ppermute(pair, ('tm', 'coil'), swaps[1])]
    ppermute x6, starting transfers between devices: 9.76 us -> 10.3 us  [turn(): lax.ppermute(block, 'row', [(i, (i + distance) % ROWS) for i in range(ROW...]
  transfers between devices with their start and end apart: 12 -> 12, of which waited for: 3 -> 4; matrix products, arithmetic and copies ran while one was open for 0% -> 0% of each run, Pallas kernels for 8% -> 8%
where the time goes in v6:
time: 46.5 us; the launch traced here: 46 us
  starting transfers between devices  31.9 us (69%)
  Pallas kernels  7.72 us (17%)
  waiting for transfers between devices  5.3 us (11%)
  between operations  0.95 us (2%)
    ppermute x6, starting transfers between devices, turn(): lax.ppermute(block, 'row', [(i, (i + distance) % ROWS) for i in range(ROW...  10.3 us
    ppermute x1, starting transfers between devices, body(): from_chip = lax.ppermute(to_chip, ('tm', 'coil'), pairs)  7.87 us
    pallas_call x7, Pallas kernels, call(): pl.pallas_call(kernel, out_shape=outs, in_specs=in_specs or [pl.BlockSpec...  7.72 us
    ppermute x1, starting transfers between devices, body(): received = lax.ppermute(partial, ('tm', 'coil'), swaps[0])  5.37 us
    ppermute x1, starting transfers between devices, body(): q_first = lax.ppermute(q_first, 'tm', after)  5.08 us
    ppermute x6, waiting for transfers between devices, turn(): lax.ppermute(block, 'row', [(i, (i + distance) % ROWS) for i in range(ROW...  2.62 us
    ppermute x1, starting transfers between devices, body(): z_in = lax.ppermute(z, 'tm', [(i + 1, i) for i in range(frames - 1)])  2.48 us
    ppermute x1, waiting for transfers between devices, body(): received = lax.ppermute(partial, ('tm', 'coil'), swaps[0])  1.99 us
  transfers between devices with their start and end apart: 12, of which 4 were waited for; matrix products, arithmetic and copies ran while one was open for 0% of the time, Pallas kernels for 8%

profile of v6, /device:TPU:1, one launch (start us, length us, event | category | flops | bytes accessed | tf_op | source)
XLA Modules:
  0.0 46.0 jit_solution(1450517896069576800)
XLA Ops:
  0.7 2.0 %shard_map.223 = (f32[64,384]{1,0:T(8,128)S(1)}, f32[80,384]{1,0:T(8,128)S(1)}, f32[88,384]{1,0:T(8,128)S(1)}, f32[64,384]{1,0:T(8,128)S(1)}, f32[1,256]{1,0:T(1,128)S(1)}) custom-call(f32[6,64,256]{2,1,0:T(8,128)} %bitcast.54, s32[1,256]{1,0:T(1,128)} %lines_hbm.1, bf16[256,512]{1,0:T(8,128)(2,1)} %constant.8.clone.th_hbm.th_ref, ...), custom_call_target="tpu_custom_call" | custom-call | flops 500 | bytes 1 | tf_op jit(solution)/shard_map/pallas_call | solution.py:427
  2.7 2.1 %collective-permute-start = (f32[80,384]{1,0:T(8,128)S(1)}, f32[80,384]{1,0:T(8,128)S(1)}, u32[]{:S(2)}, u32[]{:S(2)}) collective-permute-start(f32[80,384]{1,0:T(8,128)S(1)} %get-tuple-element.41), channel_id=1, source_target_pairs={{0,4},{4,8},{8,12},{12,0},{1,5},{5,9},{9,13},{13,1},{2,6},{6,10},{... | collective-permute-start | bytes 368648 | tf_op jit(solution)/shard_map/ppermute | solution.py:439
  4.9 2.4 %collective-permute-start.1 = (f32[88,384]{1,0:T(8,128)S(1)}, f32[88,384]{1,0:T(8,128)S(1)}, u32[]{:S(2)}, u32[]{:S(2)}) collective-permute-start(f32[88,384]{1,0:T(8,128)S(1)} %get-tuple-element.42), channel_id=1, source_target_pairs={{0,8},{4,12},{8,0},{12,4},{1,9},{5,13},{9,1},{13,5},{2,10},{6,14},... | collective-permute-start | bytes 405512 | tf_op jit(solution)/shard_map/ppermute | solution.py:439
  7.3 1.2 %collective-permute-start.2 = (f32[64,384]{1,0:T(8,128)S(1)}, f32[64,384]{1,0:T(8,128)S(1)}, u32[]{:S(2)}, u32[]{:S(2)}) collective-permute-start(f32[64,384]{1,0:T(8,128)S(1)} %get-tuple-element.43), channel_id=1, source_target_pairs={{0,12},{4,0},{8,4},{12,8},{1,13},{5,1},{9,5},{13,9},{2,14},{6,2},{... | collective-permute-start | bytes 294920 | tf_op jit(solution)/shard_map/ppermute | solution.py:439
  8.5 0.0 copy-start.11
  8.5 0.0 copy-start.13
  8.5 0.0 copy-start.15
  8.5 5.1 %collective-permute-start.4 = (f32[144,256]{1,0:T(8,128)S(1)}, f32[144,256]{1,0:T(8,128)S(1)}, u32[]{:S(2)}, u32[]{:S(2)}) collective-permute-start(f32[144,256]{1,0:T(8,128)S(1)} %shard_map.225), channel_id=1, source_target_pairs={{0,16},{16,32},{32,48},{48,64},{64,80},{80,96},{96,112},{112,128},... | collective-permute-start | bytes 442376 | tf_op jit(solution)/shard_map/ppermute | solution.py:471
  13.7 0.0 copy-start.5
  13.7 0.0 copy-start.6
  13.7 0.0 copy-start.10
  13.7 0.5 %shard_map.224.order = f32[2,64,256]{2,1,0:T(8,128)S(1)} custom-call(f32[64,384]{1,0:T(8,128)S(1)} %get-tuple-element.40.b0.order, f32[80,384]{1,0:T(8,128)S(1)} %collective-permute-done.b1, f32[88,384]{1,0:T(8,128)S(1)} %collective-permute-done.1.b2, f32[64,384]{1,0:T(8,128)S(1)} %collective-permute-done.2.b3, bf16[512,512]{1,0:T(8,128)(2,1)S(1)} %copy-done.13, ...), custom_call_target="tpu_custom_call" | custom-call | flops 99999997952 | bytes 200000000 | tf_op jit(solution)/shard_map/pallas_call | solution.py:427
  14.3 5.4 %collective-permute-start.3 = (f32[2,64,256]{2,1,0:T(8,128)S(1)}, f32[2,64,256]{2,1,0:T(8,128)S(1)}, u32[]{:S(2)}, u32[]{:S(2)}) collective-permute-start(f32[2,64,256]{2,1,0:T(8,128)S(1)} %shard_map.224.order), channel_id=1, source_target_pairs={{0,1},{1,0},{2,3},{3,2},{16,19},{17,18},{18,17},{19,16},{32,33},{3... | collective-permute-start | bytes 393224 | tf_op jit(solution)/shard_map/ppermute | solution.py:484
  19.7 0.0 copy-start.8
  19.7 1.1 %shard_map.226 = (f32[16,64,256]{2,1,0:T(8,128)S(1)}, f32[2,64,256]{2,1,0:T(8,128)S(1)}, f32[16,256]{1,0:T(8,128)S(1)}, f32[2,64,256]{2,1,0:T(8,128)S(1)}, f32[1...) custom-call(f32[2,64,256]{2,1,0:T(8,128)S(1)} %bitcast.60, f32[2,64,256]{2,1,0:T(8,128)S(1)} %bitcast.62, ...), custom_call_target="tpu_custom_call" | custom-call | flops 49999998976 | bytes 100000000 | tf_op jit(solution)/shard_map/pallas_call | solution.py:427
  20.8 0.0 copy-start.7
  20.8 2.0 %collective-permute-done.3 = f32[2,64,256]{2,1,0:T(8,128)S(1)} collective-permute-done((f32[2,64,256]{2,1,0:T(8,128)S(1)}, f32[2,64,256]{2,1,0:T(8,128)S(1)}, u32[]{:S(2)}, u32[]{:S(2)}) %collective-permute-start.3) | collective-permute-done | bytes 131104 | tf_op jit(solution)/shard_map/ppermute | solution.py:484
  22.8 0.7 %collective-permute-start.5 = (f32[2,64,256]{2,1,0:T(8,128)S(1)}, f32[2,64,256]{2,1,0:T(8,128)S(1)}, u32[]{:S(2)}, u32[]{:S(2)}) collective-permute-start(f32[2,64,256]{2,1,0:T(8,128)S(1)} %add.3.sum_a), channel_id=1, source_target_pairs={{0,3},{1,2},{2,1},{3,0},{16,17},{17,16},{18,19},{19,18},{32,35},{3... | collective-permute-start | bytes 393224 | tf_op jit(solution)/shard_map/ppermute | solution.py:487
  23.5 7.9 %collective-permute-start.7 = (f32[14,64,256]{2,1,0:T(8,128)S(1)}, f32[14,64,256]{2,1,0:T(8,128)S(1)}, u32[]{:S(2)}, u32[]{:S(2)}) collective-permute-start(f32[14,64,256]{2,1,0:T(8,128)S(1)} %get-tuple-element.56), channel_id=1, source_target_pairs={{16,32},{32,16},{17,33},{33,17},{18,34},{34,18},{19,35},{35,19},{4... | collective-permute-start | bytes 2752520 | tf_op jit(solution)/shard_map/ppermute | solution.py:494
  31.4 0.1 collective-permute-start.6
  31.5 0.0 copy-start.14
  31.5 0.0 copy-start.16
  31.5 0.6 %shard_map.227 = (f32[64,384]{1,0:T(8,128)S(1)}, f32[64,384]{1,0:T(8,128)S(1)}, f32[64,384]{1,0:T(8,128)S(1)}, f32[80,384]{1,0:T(8,128)S(1)}, f32[2,64,256]{2,1,0:T(8,128)S(1)}) custom-call(f32[2,64,256]{2,1,0:T(8,128)S(1)} %add.3.sum_a, f32[2,64,256]{2,1,0:T(8,128)S(1)} %collective-permute-done.5.sum_b, f32[2,64,256]{2,1,0:T(8,128)S(1)} %get-tuple-element.51.base, ...), custom_call_target="tpu_custom_call" | custom-call | flops 99999997952 | bytes 200000000 | tf_op jit(solution)/shard_map/pallas_call | solution.py:427
  32.2 2.7 %collective-permute-start.9 = (f32[80,384]{1,0:T(8,128)S(1)}, f32[80,384]{1,0:T(8,128)S(1)}, u32[]{:S(2)}, u32[]{:S(2)}) collective-permute-start(f32[80,384]{1,0:T(8,128)S(1)} %get-tuple-element.58), channel_id=1, source_target_pairs={{0,12},{4,0},{8,4},{12,8},{1,13},{5,1},{9,5},{13,9},{2,14},{6,2},{... | collective-permute-start | bytes 368648 | tf_op jit(solution)/shard_map/ppermute | solution.py:439
  34.8 0.2 collective-permute-start.10
  35.0 1.7 %collective-permute-start.11 = (f32[64,384]{1,0:T(8,128)S(1)}, f32[64,384]{1,0:T(8,128)S(1)}, u32[]{:S(2)}, u32[]{:S(2)}) collective-permute-start(f32[64,384]{1,0:T(8,128)S(1)} %get-tuple-element.65), channel_id=1, source_target_pairs={{0,8},{4,12},{8,0},{12,4},{1,9},{5,13},{9,1},{13,5},{2,10},{6,14},... | collective-permute-start | bytes 294920 | tf_op jit(solution)/shard_map/ppermute | solution.py:439
  36.7 2.5 %collective-permute-start.8 = (f32[2,64,256]{2,1,0:T(8,128)S(1)}, f32[2,64,256]{2,1,0:T(8,128)S(1)}, u32[]{:S(2)}, u32[]{:S(2)}) collective-permute-start(f32[2,64,256]{2,1,0:T(8,128)S(1)} %get-tuple-element.57.z), channel_id=1, source_target_pairs={{16,0},{32,16},{48,32},{64,48},{80,64},{96,80},{112,96},{128,112},... | collective-permute-start | bytes 393224 | tf_op jit(solution)/shard_map/ppermute | solution.py:504
  39.2 1.4 %collective-permute-done.10.b1 = f32[64,384]{1,0:T(8,128)S(1)} collective-permute-done((f32[64,384]{1,0:T(8,128)S(1)}, f32[64,384]{1,0:T(8,128)S(1)}, u32[]{:S(2)}, u32[]{:S(2)}) %collective-permute-start.10) | collective-permute-done | bytes 98336 | tf_op jit(solution)/shard_map/ppermute | solution.py:439
  40.6 1.2 %collective-permute-done.11.b2 = f32[64,384]{1,0:T(8,128)S(1)} collective-permute-done((f32[64,384]{1,0:T(8,128)S(1)}, f32[64,384]{1,0:T(8,128)S(1)}, u32[]{:S(2)}, u32[]{:S(2)}) %collective-permute-start.11) | collective-permute-done | bytes 98336 | tf_op jit(solution)/shard_map/ppermute | solution.py:439
  41.8 1.3 %shard_map.229 = f32[6,64,256]{2,1,0:T(8,128)} custom-call(f32[64,384]{1,0:T(8,128)S(1)} %get-tuple-element.63.b0, f32[64,384]{1,0:T(8,128)S(1)} %collective-permute-done.10.b1, f32[64,384]{1,0:T(8,128)S(1)} %collective-permute-done.11.b2, f32[80,384]{1,0:T(8,128)S(1)} %collective-permute-done.9.n3.b3, bf16[512,512]{1,0:T(8,128)(2,1)S(1)} %copy-done.14, ...), custom_call_target="tpu_custom_call" | custom-call | flops 2000000000 | bytes 4000000 | tf_op jit(solution)/shard_map/pallas_call | solution.py:427
  43.1 0.7 %collective-permute-done.8.z_in = f32[2,64,256]{2,1,0:T(8,128)S(1)} collective-permute-done((f32[2,64,256]{2,1,0:T(8,128)S(1)}, f32[2,64,256]{2,1,0:T(8,128)S(1)}, u32[]{:S(2)}, u32[]{:S(2)}) %collective-permute-start.8) | collective-permute-done | bytes 131104 | tf_op jit(solution)/shard_map/ppermute | solution.py:504
  43.8 2.2 %shard_map.228 = (f32[2,64,256]{2,1,0:T(8,128)}, f32[2,64,256]{2,1,0:T(8,128)}, f32[6,64,256]{2,1,0:T(8,128)}, f32[6,64,256]{2,1,0:T(8,128)}, f32[6,64,256]{2,1,...) custom-call(f32[2,64,256]{2,1,0:T(8,128)S(1)} %bitcast.61, ...), custom_call_target="tpu_custom_call" | custom-call | flops 500 | bytes 1 | tf_op jit(solution)/shard_map/pallas_call | solution.py:427
  (34 shorter events, 0.1 us)
Async XLA Ops:
  0.6 7.8 %copy-start = (f32[6,2,1,64,256]{4,3,2,1,0:T(8,128)S(1)}, f32[6,2,1,64,256]{4,3,2,1,0:T(8,128)}, u32[]{:S(2)}) copy-start(f32[6,2,1,64,256]{4,3,2,1,0:T(8,128)} %param.23) | copy-start | bytes 2359300
  0.7 7.8 %copy-start.1 = (f32[6,2,1,64,256]{4,3,2,1,0:T(8,128)S(1)}, f32[6,2,1,64,256]{4,3,2,1,0:T(8,128)}, u32[]{:S(2)}) copy-start(f32[6,2,1,64,256]{4,3,2,1,0:T(8,128)} %param.24) | copy-start | bytes 2359300
  0.7 7.8 %copy-start.2 = (f32[3,2,1,64,256]{4,3,2,1,0:T(8,128)S(1)}, f32[3,2,1,64,256]{4,3,2,1,0:T(8,128)}, u32[]{:S(2)}) copy-start(f32[3,2,1,64,256]{4,3,2,1,0:T(8,128)} %param.21) | copy-start | bytes 1179652
  0.7 7.8 %copy-start.3 = (f32[3,2,1,64,256]{4,3,2,1,0:T(8,128)S(1)}, f32[3,2,1,64,256]{4,3,2,1,0:T(8,128)}, u32[]{:S(2)}) copy-start(f32[3,2,1,64,256]{4,3,2,1,0:T(8,128)} %param.22) | copy-start | bytes 1179652
  2.7 10.9 %collective-permute-start = (f32[80,384]{1,0:T(8,128)S(1)}, f32[80,384]{1,0:T(8,128)S(1)}, u32[]{:S(2)}, u32[]{:S(2)}) collective-permute-start(f32[80,384]{1,0:T(8,128)S(1)} %get-tuple-element.41), channel_id=1, source_target_pairs={{0,4},{4,8},{8,12},{12,0},{1,5},{5,9},{9,13},{13,1},{2,6},{6,10},{... | collective-permute-start | bytes 368648 | tf_op jit(solution)/shard_map/ppermute | solution.py:439
  4.9 8.8 %collective-permute-start.1 = (f32[88,384]{1,0:T(8,128)S(1)}, f32[88,384]{1,0:T(8,128)S(1)}, u32[]{:S(2)}, u32[]{:S(2)}) collective-permute-start(f32[88,384]{1,0:T(8,128)S(1)} %get-tuple-element.42), channel_id=1, source_target_pairs={{0,8},{4,12},{8,0},{12,4},{1,9},{5,13},{9,1},{13,5},{2,10},{6,14},... | collective-permute-start | bytes 405512 | tf_op jit(solution)/shard_map/ppermute | solution.py:439
  7.3 6.3 %collective-permute-start.2 = (f32[64,384]{1,0:T(8,128)S(1)}, f32[64,384]{1,0:T(8,128)S(1)}, u32[]{:S(2)}, u32[]{:S(2)}) collective-permute-start(f32[64,384]{1,0:T(8,128)S(1)} %get-tuple-element.43), channel_id=1, source_target_pairs={{0,12},{4,0},{8,4},{12,8},{1,13},{5,1},{9,5},{13,9},{2,14},{6,2},{... | collective-permute-start | bytes 294920 | tf_op jit(solution)/shard_map/ppermute | solution.py:439
  8.5 5.2 %copy-start.11 = (f32[2,3,64,256]{3,2,1,0:T(8,128)S(1)}, f32[2,3,64,256]{3,2,1,0:T(8,128)}, u32[]{:S(2)}) copy-start(f32[2,3,64,256]{3,2,1,0:T(8,128)} %param.26) | copy-start | bytes 1179652
  8.5 5.2 %copy-start.13 = (bf16[512,512]{1,0:T(8,128)(2,1)S(1)}, bf16[512,512]{1,0:T(8,128)(2,1)}, u32[]{:S(2)}) copy-start(bf16[512,512]{1,0:T(8,128)(2,1)} %constant.10.clone.th_ref) | copy-start | bytes 1572868
  8.5 5.2 %copy-start.15 = (bf16[512,512]{1,0:T(8,128)(2,1)S(1)}, bf16[512,512]{1,0:T(8,128)(2,1)}, u32[]{:S(2)}) copy-start(bf16[512,512]{1,0:T(8,128)(2,1)} %constant.11.clone.tl_ref) | copy-start | bytes 1572868
  8.5 11.1 %collective-permute-start.4 = (f32[144,256]{1,0:T(8,128)S(1)}, f32[144,256]{1,0:T(8,128)S(1)}, u32[]{:S(2)}, u32[]{:S(2)}) collective-permute-start(f32[144,256]{1,0:T(8,128)S(1)} %shard_map.225), channel_id=1, source_target_pairs={{0,16},{16,32},{32,48},{48,64},{64,80},{80,96},{96,112},{112,128},... | collective-permute-start | bytes 442376 | tf_op jit(solution)/shard_map/ppermute | solution.py:471
  13.7 5.9 %copy-start.5 = (f32[3,2,1,64,256]{4,3,2,1,0:T(8,128)S(1)}, f32[3,2,1,64,256]{4,3,2,1,0:T(8,128)}, u32[]{:S(2)}) copy-start(f32[3,2,1,64,256]{4,3,2,1,0:T(8,128)} %param.18) | copy-start | bytes 1179652
  13.7 5.9 %copy-start.6 = (f32[3,2,1,64,256]{4,3,2,1,0:T(8,128)S(1)}, f32[3,2,1,64,256]{4,3,2,1,0:T(8,128)}, u32[]{:S(2)}) copy-start(f32[3,2,1,64,256]{4,3,2,1,0:T(8,128)} %param.19) | copy-start | bytes 1179652
  13.7 5.9 %copy-start.9 = (f32[2,1,64,256]{3,2,1,0:T(8,128)S(1)}, f32[2,1,64,256]{3,2,1,0:T(8,128)}, u32[]{:S(2)}) copy-start(f32[2,1,64,256]{3,2,1,0:T(8,128)} %param.16) | copy-start | bytes 393220
  13.7 5.9 %copy-start.10 = (f32[2,1,64,256]{3,2,1,0:T(8,128)S(1)}, f32[2,1,64,256]{3,2,1,0:T(8,128)}, u32[]{:S(2)}) copy-start(f32[2,1,64,256]{3,2,1,0:T(8,128)} %param.17) | copy-start | bytes 393220
  14.3 8.5 %collective-permute-start.3 = (f32[2,64,256]{2,1,0:T(8,128)S(1)}, f32[2,64,256]{2,1,0:T(8,128)S(1)}, u32[]{:S(2)}, u32[]{:S(2)}) collective-permute-start(f32[2,64,256]{2,1,0:T(8,128)S(1)} %shard_map.224.order), channel_id=1, source_target_pairs={{0,1},{1,0},{2,3},{3,2},{16,19},{17,18},{18,17},{19,16},{32,33},{3... | collective-permute-start | bytes 393224 | tf_op jit(solution)/shard_map/ppermute | solution.py:484
  19.7 11.8 %copy-start.8 = (bf16[256,512]{1,0:T(8,128)(2,1)S(1)}, bf16[256,512]{1,0:T(8,128)(2,1)}, u32[]{:S(2)}) copy-start(bf16[256,512]{1,0:T(8,128)(2,1)} %constant.9.clone.tl_hbm.tl_ref) | copy-start | bytes 786436
  20.8 10.7 %copy-start.7 = (bf16[256,512]{1,0:T(8,128)(2,1)S(1)}, bf16[256,512]{1,0:T(8,128)(2,1)}, u32[]{:S(2)}) copy-start(bf16[256,512]{1,0:T(8,128)(2,1)} %constant.8.clone.th_hbm.th_ref) | copy-start | bytes 786436
  22.8 8.6 %collective-permute-start.5 = (f32[2,64,256]{2,1,0:T(8,128)S(1)}, f32[2,64,256]{2,1,0:T(8,128)S(1)}, u32[]{:S(2)}, u32[]{:S(2)}) collective-permute-start(f32[2,64,256]{2,1,0:T(8,128)S(1)} %add.3.sum_a), channel_id=1, source_target_pairs={{0,3},{1,2},{2,1},{3,0},{16,17},{17,16},{18,19},{19,18},{32,35},{3... | collective-permute-start | bytes 393224 | tf_op jit(solution)/shard_map/ppermute | solution.py:487
  23.5 19.7 %collective-permute-start.7 = (f32[14,64,256]{2,1,0:T(8,128)S(1)}, f32[14,64,256]{2,1,0:T(8,128)S(1)}, u32[]{:S(2)}, u32[]{:S(2)}) collective-permute-start(f32[14,64,256]{2,1,0:T(8,128)S(1)} %get-tuple-element.56), channel_id=1, source_target_pairs={{16,32},{32,16},{17,33},{33,17},{18,34},{34,18},{19,35},{35,19},{4... | collective-permute-start | bytes 2752520 | tf_op jit(solution)/shard_map/ppermute | solution.py:494
  31.4 5.4 %collective-permute-start.6 = (f32[14,64,256]{2,1,0:T(8,128)S(1)}, f32[14,64,256]{2,1,0:T(8,128)S(1)}, u32[]{:S(2)}, u32[]{:S(2)}) collective-permute-start(f32[14,64,256]{2,1,0:T(8,128)S(1)} %get-tuple-element.54), channel_id=1, source_target_pairs={{0,16},{16,0},{32,48},{48,32},{64,80},{80,64},{96,112},{112,96},{1... | collective-permute-start | bytes 2752520 | tf_op jit(solution)/shard_map/ppermute | solution.py:496
  31.5 10.3 %copy-start.4 = (f32[2,1,3,64,256]{4,3,2,1,0:T(8,128)S(1)}, f32[2,1,3,64,256]{4,3,2,1,0:T(8,128)}, u32[]{:S(2)}) copy-start(f32[2,1,3,64,256]{4,3,2,1,0:T(8,128)} %param.20) | copy-start | bytes 1179652
  31.5 10.3 %copy-start.12 = (f32[2,1,3,64,256]{4,3,2,1,0:T(8,128)S(1)}, f32[2,1,3,64,256]{4,3,2,1,0:T(8,128)}, u32[]{:S(2)}) copy-start(f32[2,1,3,64,256]{4,3,2,1,0:T(8,128)} %param.25) | copy-start | bytes 1179652
  31.5 10.3 %copy-start.14 = (bf16[512,512]{1,0:T(8,128)(2,1)S(1)}, bf16[512,512]{1,0:T(8,128)(2,1)}, u32[]{:S(2)}) copy-start(bf16[512,512]{1,0:T(8,128)(2,1)} %constant.10.clone.th_ref) | copy-start | bytes 1572868
  31.5 10.3 %copy-start.16 = (bf16[512,512]{1,0:T(8,128)(2,1)S(1)}, bf16[512,512]{1,0:T(8,128)(2,1)}, u32[]{:S(2)}) copy-start(bf16[512,512]{1,0:T(8,128)(2,1)} %constant.11.clone.tl_ref) | copy-start | bytes 1572868
  32.2 9.6 %collective-permute-start.9 = (f32[80,384]{1,0:T(8,128)S(1)}, f32[80,384]{1,0:T(8,128)S(1)}, u32[]{:S(2)}, u32[]{:S(2)}) collective-permute-start(f32[80,384]{1,0:T(8,128)S(1)} %get-tuple-element.58), channel_id=1, source_target_pairs={{0,12},{4,0},{8,4},{12,8},{1,13},{5,1},{9,5},{13,9},{2,14},{6,2},{... | collective-permute-start | bytes 368648 | tf_op jit(solution)/shard_map/ppermute | solution.py:439
  34.8 5.7 %collective-permute-start.10 = (f32[64,384]{1,0:T(8,128)S(1)}, f32[64,384]{1,0:T(8,128)S(1)}, u32[]{:S(2)}, u32[]{:S(2)}) collective-permute-start(f32[64,384]{1,0:T(8,128)S(1)} %get-tuple-element.64), channel_id=1, source_target_pairs={{0,4},{4,8},{8,12},{12,0},{1,5},{5,9},{9,13},{13,1},{2,6},{6,10},{... | collective-permute-start | bytes 294920 | tf_op jit(solution)/shard_map/ppermute | solution.py:439
  35.0 6.8 %collective-permute-start.11 = (f32[64,384]{1,0:T(8,128)S(1)}, f32[64,384]{1,0:T(8,128)S(1)}, u32[]{:S(2)}, u32[]{:S(2)}) collective-permute-start(f32[64,384]{1,0:T(8,128)S(1)} %get-tuple-element.65), channel_id=1, source_target_pairs={{0,8},{4,12},{8,0},{12,4},{1,9},{5,13},{9,1},{13,5},{2,10},{6,14},... | collective-permute-start | bytes 294920 | tf_op jit(solution)/shard_map/ppermute | solution.py:439
  36.7 7.1 %collective-permute-start.8 = (f32[2,64,256]{2,1,0:T(8,128)S(1)}, f32[2,64,256]{2,1,0:T(8,128)S(1)}, u32[]{:S(2)}, u32[]{:S(2)}) collective-permute-start(f32[2,64,256]{2,1,0:T(8,128)S(1)} %get-tuple-element.57.z), channel_id=1, source_target_pairs={{16,0},{32,16},{48,32},{64,48},{80,64},{96,80},{112,96},{128,112},... | collective-permute-start | bytes 393224 | tf_op jit(solution)/shard_map/ppermute | solution.py:504
